TPU v7x, 512 devices: a whole 4x4x16 slice. The times are simulated.
512 devices in a mesh: slab: 16 (over z_hi, x, core), trace: 32 (over y, z_lo).
Axes of the slice: x: 4, y: 4, z: 16 (z_hi: 2, z_lo: 8; z = z_hi * 8 + z_lo), core: 2. Of those that a mesh axis runs over, the one named last changes fastest.
Arguments:
- incident: float32 [4, 3072, 128], P(None, 'trace'), may hold values from -6 to 6
- green_interior: bfloat16 [16, 2, 4608, 3072], P('slab', None, 'trace'), may hold values from -0.078125 to 0.078125
- green_next: bfloat16 [16, 2, 3072, 3072], P('slab', None, 'trace'), may hold values from -0.0625 to 0.0625
- sources: float32 [16, 4, 3072, 128], P('slab', None, 'trace'), may hold values from -3 to 3
Outputs:
- interior: float32 [16, 4, 4608, 128], P('slab', None, 'trace')
- traces: float32 [16, 4, 3072, 128], P('slab', None, 'trace')
All inputs are finite; a program needn't handle non-finite values.
Results may differ from a plain program's by a relative error of at most 0.014.
Values may be sent and summed in bfloat16 or wider, within the bound.
No kernel may reach another device: no remote copies, remote signals or barrier semaphores. Data moves between devices by JAX's collectives and lax.ppermute only.
A program may use at most 64 MiB of HBM per device.

v0:
```python
import jax
import jax.numpy as jnp
from jax import lax
from jax.sharding import PartitionSpec as P


def copy_for_each(x, axis):
    copies = jnp.broadcast_to(x, (lax.axis_size(axis), *x.shape))
    return lax.all_to_all(copies, axis, split_axis=0, concat_axis=0, tiled=True)


def in_order(pieces, dim):
    pieces = jnp.moveaxis(pieces, 0, dim)
    lengths = pieces.shape
    return pieces.reshape(*lengths[:dim], lengths[dim] * lengths[dim + 1], *lengths[dim + 2 :])


def gather_directly(x, axis, dim):
    pieces = copy_for_each(x, axis)
    return in_order(pieces, dim)


def shifted(value, axis, steps):
    count = lax.axis_size(axis)
    initial, last = (max(0, -steps), min(count, count - steps))
    return lax.ppermute(value, axis, [(source, source + steps) for source in range(initial, last)])


def complex_apply(halves, vectors, batches):
    row_count = halves.shape[1]
    inner_width = halves.shape[2]
    half_cols = vectors.shape[1] // (2 * batches)
    product = jnp.dot(
        halves.reshape(2 * row_count, inner_width), vectors, preferred_element_type=jnp.float32
    )
    product = product.reshape(2, row_count, batches, 2, half_cols)
    real_part = product[0, :, :, 0] - product[1, :, :, 1]
    imag_part = product[0, :, :, 1] + product[1, :, :, 0]
    return jnp.stack([real_part, imag_part], axis=2)


def to_fronts(product):
    row_count, batches, two_parts, half_cols = product.shape
    return jnp.transpose(product, (1, 0, 2, 3)).reshape(batches, row_count, two_parts * half_cols)


def local(incident, green_interior, green_next, sources):
    slab_count = lax.axis_size("slab")
    position = lax.axis_index("slab")
    fronts = incident.shape[0]
    local_rows = incident.shape[1]
    columns = incident.shape[2]
    total_steps = fronts + slab_count - 1
    next_halves = green_next[0]
    inner_halves = green_interior[0]
    local_sources = sources[0]

    def advance(counter, carried):
        received, leaving_all, inner_all, stored = carried
        front_index = counter - position
        active = (front_index >= 0) & (front_index < fronts)
        chosen = jnp.clip(front_index, 0, fronts - 1)
        start_front = jnp.clip(counter, 0, fronts - 1).astype(jnp.int32)
        boundary = lax.dynamic_index_in_dim(incident, start_front, 0, keepdims=False).astype(
            jnp.bfloat16
        )
        entering = jnp.where(position == 0, boundary, received)
        gathered = gather_directly(entering, "trace", 0)
        own_source = lax.dynamic_index_in_dim(local_sources, chosen, 0, keepdims=False)
        leaving = to_fronts(complex_apply(next_halves, gathered, 1))[0] + own_source
        previous = lax.dynamic_index_in_dim(leaving_all, chosen, 0, keepdims=False)
        leaving_all = lax.dynamic_update_index_in_dim(
            leaving_all, jnp.where(active, leaving, previous), chosen, 0
        )
        received = shifted(leaving.astype(jnp.bfloat16), "slab", 1)
        previous_cols = lax.dynamic_slice_in_dim(stored, chosen * columns, columns, 1)
        stored = lax.dynamic_update_slice_in_dim(
            stored, jnp.where(active, gathered, previous_cols), chosen * columns, 1
        )
        return (received, leaving_all, inner_all, stored)

    received_start = jnp.zeros((local_rows, columns), jnp.bfloat16)
    leaving_start = jnp.zeros((fronts, local_rows, columns), jnp.float32)
    inner_start = jnp.zeros((1, 1), jnp.float32)
    stored_start = jnp.zeros((next_halves.shape[2], fronts * columns), jnp.bfloat16)

    def step_without(counter, carried):
        return advance(counter, carried)

    final_state = lax.fori_loop(
        0, total_steps, step_without, (received_start, leaving_start, inner_start, stored_start)
    )
    interior_rows = to_fronts(complex_apply(inner_halves, final_state[3], fronts))
    return (interior_rows[None], final_state[1][None])


def solution(mesh):
    return jax.shard_map(
        local,
        mesh=mesh,
        in_specs=(
            P(None, "trace", None),
            P("slab", None, "trace", None),
            P("slab", None, "trace", None),
            P("slab", None, "trace", None),
        ),
        out_specs=(P("slab", None, "trace", None), P("slab", None, "trace", None)),
        check_vma=False,
    )
```

profile of v0, /device:TPU:1, one launch (start us, length us, event | category | flops | bytes accessed | tf_op | source)
XLA Modules:
  0.0 1064.3 jit_solution(1441304064718037158)
XLA Ops:
  6.0 1050.0 %while.18 = (s32[]{:T(128)}, bf16[96,128]{0,1:T(8,128)(2,1)S(1)}, f32[4,96,128]{2,1,0:T(8,128)S(1)}, bf16[3072,512]{1,0:T(8,128)(2,1)}, pred[]{:T(512)}, /*index...) while((s32[]{:T(128)}, bf16[96,128]{0,1:T(8,128)(2,1)S(1)}, ...), condition=%wide.region_1.2_spmd, body=%wide.region_0.1_spmd.sunk | while | flops 151474176 | bytes 9363823 | solution.py:90
  7.2 16.1 %all-to-all-start = ((bf16[32,96,128]{2,1,0:T(8,128)(2,1)}), bf16[32,96,128]{2,1,0:T(8,128)(2,1)S(1)}, u32[]{:S(2)}, u32[]{:S(2)}) async-start(bf16[32,96,128]{2,1,0:T(8,128)(2,1)} %broadcast_in_dim.29), calls=%async_computation | async-start | bytes 1572864 | tf_op jit(solution)/shard_map/while/body/eval_jaxpr/all_to_all | solution.py:9
  23.5 39.7 %all-to-all-done = bf16[32,96,128]{2,1,0:T(8,128)(2,1)S(1)} async-done(((bf16[32,96,128]{2,1,0:T(8,128)(2,1)}), bf16[32,96,128]{2,1,0:T(8,128)(2,1)S(1)}, u32[]{:S(2)}, u32[]{:S(2)}) %all-to-all-start) | async-done | bytes 786464 | tf_op jit(solution)/shard_map/while/body/eval_jaxpr/all_to_all | solution.py:9
  65.4 4.8 collective-permute-start
  73.8 5.2 all-to-all-start
  79.1 39.8 %all-to-all-done = bf16[32,96,128]{2,1,0:T(8,128)(2,1)S(1)} async-done(((bf16[32,96,128]{2,1,0:T(8,128)(2,1)}), bf16[32,96,128]{2,1,0:T(8,128)(2,1)S(1)}, u32[]{:S(2)}, u32[]{:S(2)}) %all-to-all-start) | async-done | bytes 786464 | tf_op jit(solution)/shard_map/while/body/eval_jaxpr/all_to_all | solution.py:9
  121.1 4.7 collective-permute-start
  129.3 5.1 all-to-all-start
  134.6 39.3 %all-to-all-done = bf16[32,96,128]{2,1,0:T(8,128)(2,1)S(1)} async-done(((bf16[32,96,128]{2,1,0:T(8,128)(2,1)}), bf16[32,96,128]{2,1,0:T(8,128)(2,1)S(1)}, u32[]{:S(2)}, u32[]{:S(2)}) %all-to-all-start) | async-done | bytes 786464 | tf_op jit(solution)/shard_map/while/body/eval_jaxpr/all_to_all | solution.py:9
  176.1 4.9 collective-permute-start
  184.5 5.1 all-to-all-start
  189.8 39.1 %all-to-all-done = bf16[32,96,128]{2,1,0:T(8,128)(2,1)S(1)} async-done(((bf16[32,96,128]{2,1,0:T(8,128)(2,1)}), bf16[32,96,128]{2,1,0:T(8,128)(2,1)S(1)}, u32[]{:S(2)}, u32[]{:S(2)}) %all-to-all-start) | async-done | bytes 786464 | tf_op jit(solution)/shard_map/while/body/eval_jaxpr/all_to_all | solution.py:9
  231.1 5.2 collective-permute-start
  239.9 5.1 all-to-all-start
  245.2 38.8 %all-to-all-done = bf16[32,96,128]{2,1,0:T(8,128)(2,1)S(1)} async-done(((bf16[32,96,128]{2,1,0:T(8,128)(2,1)}), bf16[32,96,128]{2,1,0:T(8,128)(2,1)S(1)}, u32[]{:S(2)}, u32[]{:S(2)}) %all-to-all-start) | async-done | bytes 786464 | tf_op jit(solution)/shard_map/while/body/eval_jaxpr/all_to_all | solution.py:9
  286.2 5.4 collective-permute-start
  291.7 2.3 select_dynamic-update-slice_fusion.2
  295.3 5.1 all-to-all-start
  300.5 38.8 %all-to-all-done = bf16[32,96,128]{2,1,0:T(8,128)(2,1)S(1)} async-done(((bf16[32,96,128]{2,1,0:T(8,128)(2,1)}), bf16[32,96,128]{2,1,0:T(8,128)(2,1)S(1)}, u32[]{:S(2)}, u32[]{:S(2)}) %all-to-all-start) | async-done | bytes 786464 | tf_op jit(solution)/shard_map/while/body/eval_jaxpr/all_to_all | solution.py:9
  341.5 5.4 collective-permute-start
  347.0 2.3 select_dynamic-update-slice_fusion.2
  350.6 5.1 all-to-all-start
  355.8 38.8 %all-to-all-done = bf16[32,96,128]{2,1,0:T(8,128)(2,1)S(1)} async-done(((bf16[32,96,128]{2,1,0:T(8,128)(2,1)}), bf16[32,96,128]{2,1,0:T(8,128)(2,1)S(1)}, u32[]{:S(2)}, u32[]{:S(2)}) %all-to-all-start) | async-done | bytes 786464 | tf_op jit(solution)/shard_map/while/body/eval_jaxpr/all_to_all | solution.py:9
  396.9 5.5 collective-permute-start
  402.4 2.3 select_dynamic-update-slice_fusion.2
  405.9 5.1 all-to-all-start
  411.2 38.7 %all-to-all-done = bf16[32,96,128]{2,1,0:T(8,128)(2,1)S(1)} async-done(((bf16[32,96,128]{2,1,0:T(8,128)(2,1)}), bf16[32,96,128]{2,1,0:T(8,128)(2,1)S(1)}, u32[]{:S(2)}, u32[]{:S(2)}) %all-to-all-start) | async-done | bytes 786464 | tf_op jit(solution)/shard_map/while/body/eval_jaxpr/all_to_all | solution.py:9
  452.2 5.6 collective-permute-start
  457.7 2.3 select_dynamic-update-slice_fusion.2
  461.3 5.1 all-to-all-start
  466.6 38.6 %all-to-all-done = bf16[32,96,128]{2,1,0:T(8,128)(2,1)S(1)} async-done(((bf16[32,96,128]{2,1,0:T(8,128)(2,1)}), bf16[32,96,128]{2,1,0:T(8,128)(2,1)S(1)}, u32[]{:S(2)}, u32[]{:S(2)}) %all-to-all-start) | async-done | bytes 786464 | tf_op jit(solution)/shard_map/while/body/eval_jaxpr/all_to_all | solution.py:9
  507.5 5.8 collective-permute-start
  513.3 2.3 select_dynamic-update-slice_fusion.2
  516.8 5.1 all-to-all-start
  522.1 38.4 %all-to-all-done = bf16[32,96,128]{2,1,0:T(8,128)(2,1)S(1)} async-done(((bf16[32,96,128]{2,1,0:T(8,128)(2,1)}), bf16[32,96,128]{2,1,0:T(8,128)(2,1)S(1)}, u32[]{:S(2)}, u32[]{:S(2)}) %all-to-all-start) | async-done | bytes 786464 | tf_op jit(solution)/shard_map/while/body/eval_jaxpr/all_to_all | solution.py:9
  562.8 6.0 collective-permute-start
  568.8 2.3 select_dynamic-update-slice_fusion.2
  572.4 5.1 all-to-all-start
  577.7 38.2 %all-to-all-done = bf16[32,96,128]{2,1,0:T(8,128)(2,1)S(1)} async-done(((bf16[32,96,128]{2,1,0:T(8,128)(2,1)}), bf16[32,96,128]{2,1,0:T(8,128)(2,1)S(1)}, u32[]{:S(2)}, u32[]{:S(2)}) %all-to-all-start) | async-done | bytes 786464 | tf_op jit(solution)/shard_map/while/body/eval_jaxpr/all_to_all | solution.py:9
  618.1 5.0 collective-permute-start
  626.7 5.4 all-to-all-start
  632.2 38.9 %all-to-all-done = bf16[32,96,128]{2,1,0:T(8,128)(2,1)S(1)} async-done(((bf16[32,96,128]{2,1,0:T(8,128)(2,1)}), bf16[32,96,128]{2,1,0:T(8,128)(2,1)S(1)}, u32[]{:S(2)}, u32[]{:S(2)}) %all-to-all-start) | async-done | bytes 786464 | tf_op jit(solution)/shard_map/while/body/eval_jaxpr/all_to_all | solution.py:9
  673.4 3.5 collective-permute-start
  680.5 5.4 all-to-all-start
  686.0 40.4 %all-to-all-done = bf16[32,96,128]{2,1,0:T(8,128)(2,1)S(1)} async-done(((bf16[32,96,128]{2,1,0:T(8,128)(2,1)}), bf16[32,96,128]{2,1,0:T(8,128)(2,1)S(1)}, u32[]{:S(2)}, u32[]{:S(2)}) %all-to-all-start) | async-done | bytes 786464 | tf_op jit(solution)/shard_map/while/body/eval_jaxpr/all_to_all | solution.py:9
  734.3 5.4 all-to-all-start
  739.9 39.8 %all-to-all-done = bf16[32,96,128]{2,1,0:T(8,128)(2,1)S(1)} async-done(((bf16[32,96,128]{2,1,0:T(8,128)(2,1)}), bf16[32,96,128]{2,1,0:T(8,128)(2,1)S(1)}, u32[]{:S(2)}, u32[]{:S(2)}) %all-to-all-start) | async-done | bytes 786464 | tf_op jit(solution)/shard_map/while/body/eval_jaxpr/all_to_all | solution.py:9
  782.0 2.6 collective-permute-start
  788.2 5.4 all-to-all-start
  793.7 39.9 %all-to-all-done = bf16[32,96,128]{2,1,0:T(8,128)(2,1)S(1)} async-done(((bf16[32,96,128]{2,1,0:T(8,128)(2,1)}), bf16[32,96,128]{2,1,0:T(8,128)(2,1)S(1)}, u32[]{:S(2)}, u32[]{:S(2)}) %all-to-all-start) | async-done | bytes 786464 | tf_op jit(solution)/shard_map/while/body/eval_jaxpr/all_to_all | solution.py:9
  835.9 2.5 collective-permute-start
  842.0 5.4 all-to-all-start
  847.5 39.8 %all-to-all-done = bf16[32,96,128]{2,1,0:T(8,128)(2,1)S(1)} async-done(((bf16[32,96,128]{2,1,0:T(8,128)(2,1)}), bf16[32,96,128]{2,1,0:T(8,128)(2,1)S(1)}, u32[]{:S(2)}, u32[]{:S(2)}) %all-to-all-start) | async-done | bytes 786464 | tf_op jit(solution)/shard_map/while/body/eval_jaxpr/all_to_all | solution.py:9
  889.6 2.6 collective-permute-start
  895.8 5.4 all-to-all-start
  901.4 39.9 %all-to-all-done = bf16[32,96,128]{2,1,0:T(8,128)(2,1)S(1)} async-done(((bf16[32,96,128]{2,1,0:T(8,128)(2,1)}), bf16[32,96,128]{2,1,0:T(8,128)(2,1)S(1)}, u32[]{:S(2)}, u32[]{:S(2)}) %all-to-all-start) | async-done | bytes 786464 | tf_op jit(solution)/shard_map/while/body/eval_jaxpr/all_to_all | solution.py:9
  943.5 2.6 collective-permute-start
  949.6 5.4 all-to-all-start
  955.2 39.9 %all-to-all-done = bf16[32,96,128]{2,1,0:T(8,128)(2,1)S(1)} async-done(((bf16[32,96,128]{2,1,0:T(8,128)(2,1)}), bf16[32,96,128]{2,1,0:T(8,128)(2,1)S(1)}, u32[]{:S(2)}, u32[]{:S(2)}) %all-to-all-start) | async-done | bytes 786464 | tf_op jit(solution)/shard_map/while/body/eval_jaxpr/all_to_all | solution.py:9
  997.3 2.6 collective-permute-start
  1003.4 5.4 all-to-all-start
  1009.0 39.8 %all-to-all-done = bf16[32,96,128]{2,1,0:T(8,128)(2,1)S(1)} async-done(((bf16[32,96,128]{2,1,0:T(8,128)(2,1)}), bf16[32,96,128]{2,1,0:T(8,128)(2,1)S(1)}, u32[]{:S(2)}, u32[]{:S(2)}) %all-to-all-start) | async-done | bytes 786464 | tf_op jit(solution)/shard_map/while/body/eval_jaxpr/all_to_all | solution.py:9
  1051.0 2.6 collective-permute-start
  1056.0 3.9 convolution_bitcast_fusion.1
  (371 shorter events, 107.9 us)
Async XLA Ops:
  0.6 1.5 copy-start
  7.2 56.0 %all-to-all-start = ((bf16[32,96,128]{2,1,0:T(8,128)(2,1)}), bf16[32,96,128]{2,1,0:T(8,128)(2,1)S(1)}, u32[]{:S(2)}, u32[]{:S(2)}) async-start(bf16[32,96,128]{2,1,0:T(8,128)(2,1)} %broadcast_in_dim.29), calls=%async_computation | async-start | bytes 1572864 | tf_op jit(solution)/shard_map/while/body/eval_jaxpr/all_to_all | solution.py:9
  65.4 7.0 collective-permute-start
  73.8 45.1 %all-to-all-start = ((bf16[32,96,128]{2,1,0:T(8,128)(2,1)}), bf16[32,96,128]{2,1,0:T(8,128)(2,1)S(1)}, u32[]{:S(2)}, u32[]{:S(2)}) async-start(bf16[32,96,128]{2,1,0:T(8,128)(2,1)} %broadcast_in_dim.29), calls=%async_computation | async-start | bytes 1572864 | tf_op jit(solution)/shard_map/while/body/eval_jaxpr/all_to_all | solution.py:9
  121.1 7.0 collective-permute-start
  129.3 44.5 %all-to-all-start = ((bf16[32,96,128]{2,1,0:T(8,128)(2,1)}), bf16[32,96,128]{2,1,0:T(8,128)(2,1)S(1)}, u32[]{:S(2)}, u32[]{:S(2)}) async-start(bf16[32,96,128]{2,1,0:T(8,128)(2,1)} %broadcast_in_dim.29), calls=%async_computation | async-start | bytes 1572864 | tf_op jit(solution)/shard_map/while/body/eval_jaxpr/all_to_all | solution.py:9
  176.1 7.2 collective-permute-start
  184.5 44.4 %all-to-all-start = ((bf16[32,96,128]{2,1,0:T(8,128)(2,1)}), bf16[32,96,128]{2,1,0:T(8,128)(2,1)S(1)}, u32[]{:S(2)}, u32[]{:S(2)}) async-start(bf16[32,96,128]{2,1,0:T(8,128)(2,1)} %broadcast_in_dim.29), calls=%async_computation | async-start | bytes 1572864 | tf_op jit(solution)/shard_map/while/body/eval_jaxpr/all_to_all | solution.py:9
  231.1 7.5 collective-permute-start
  239.9 44.1 %all-to-all-start = ((bf16[32,96,128]{2,1,0:T(8,128)(2,1)}), bf16[32,96,128]{2,1,0:T(8,128)(2,1)S(1)}, u32[]{:S(2)}, u32[]{:S(2)}) async-start(bf16[32,96,128]{2,1,0:T(8,128)(2,1)} %broadcast_in_dim.29), calls=%async_computation | async-start | bytes 1572864 | tf_op jit(solution)/shard_map/while/body/eval_jaxpr/all_to_all | solution.py:9
  286.2 7.8 collective-permute-start
  295.3 44.1 %all-to-all-start = ((bf16[32,96,128]{2,1,0:T(8,128)(2,1)}), bf16[32,96,128]{2,1,0:T(8,128)(2,1)S(1)}, u32[]{:S(2)}, u32[]{:S(2)}) async-start(bf16[32,96,128]{2,1,0:T(8,128)(2,1)} %broadcast_in_dim.29), calls=%async_computation | async-start | bytes 1572864 | tf_op jit(solution)/shard_map/while/body/eval_jaxpr/all_to_all | solution.py:9
  341.5 7.8 collective-permute-start
  350.6 44.1 %all-to-all-start = ((bf16[32,96,128]{2,1,0:T(8,128)(2,1)}), bf16[32,96,128]{2,1,0:T(8,128)(2,1)S(1)}, u32[]{:S(2)}, u32[]{:S(2)}) async-start(bf16[32,96,128]{2,1,0:T(8,128)(2,1)} %broadcast_in_dim.29), calls=%async_computation | async-start | bytes 1572864 | tf_op jit(solution)/shard_map/while/body/eval_jaxpr/all_to_all | solution.py:9
  396.9 7.8 collective-permute-start
  405.9 44.0 %all-to-all-start = ((bf16[32,96,128]{2,1,0:T(8,128)(2,1)}), bf16[32,96,128]{2,1,0:T(8,128)(2,1)S(1)}, u32[]{:S(2)}, u32[]{:S(2)}) async-start(bf16[32,96,128]{2,1,0:T(8,128)(2,1)} %broadcast_in_dim.29), calls=%async_computation | async-start | bytes 1572864 | tf_op jit(solution)/shard_map/while/body/eval_jaxpr/all_to_all | solution.py:9
  452.2 7.9 collective-permute-start
  461.3 43.9 %all-to-all-start = ((bf16[32,96,128]{2,1,0:T(8,128)(2,1)}), bf16[32,96,128]{2,1,0:T(8,128)(2,1)S(1)}, u32[]{:S(2)}, u32[]{:S(2)}) async-start(bf16[32,96,128]{2,1,0:T(8,128)(2,1)} %broadcast_in_dim.29), calls=%async_computation | async-start | bytes 1572864 | tf_op jit(solution)/shard_map/while/body/eval_jaxpr/all_to_all | solution.py:9
  507.5 8.1 collective-permute-start
  516.8 43.7 %all-to-all-start = ((bf16[32,96,128]{2,1,0:T(8,128)(2,1)}), bf16[32,96,128]{2,1,0:T(8,128)(2,1)S(1)}, u32[]{:S(2)}, u32[]{:S(2)}) async-start(bf16[32,96,128]{2,1,0:T(8,128)(2,1)} %broadcast_in_dim.29), calls=%async_computation | async-start | bytes 1572864 | tf_op jit(solution)/shard_map/while/body/eval_jaxpr/all_to_all | solution.py:9
  562.8 8.3 collective-permute-start
  572.4 43.5 %all-to-all-start = ((bf16[32,96,128]{2,1,0:T(8,128)(2,1)}), bf16[32,96,128]{2,1,0:T(8,128)(2,1)S(1)}, u32[]{:S(2)}, u32[]{:S(2)}) async-start(bf16[32,96,128]{2,1,0:T(8,128)(2,1)} %broadcast_in_dim.29), calls=%async_computation | async-start | bytes 1572864 | tf_op jit(solution)/shard_map/while/body/eval_jaxpr/all_to_all | solution.py:9
  618.1 7.3 collective-permute-start
  626.7 44.5 %all-to-all-start = ((bf16[32,96,128]{2,1,0:T(8,128)(2,1)}), bf16[32,96,128]{2,1,0:T(8,128)(2,1)S(1)}, u32[]{:S(2)}, u32[]{:S(2)}) async-start(bf16[32,96,128]{2,1,0:T(8,128)(2,1)} %broadcast_in_dim.29), calls=%async_computation | async-start | bytes 1572864 | tf_op jit(solution)/shard_map/while/body/eval_jaxpr/all_to_all | solution.py:9
  673.4 5.8 collective-permute-start
  680.5 45.9 %all-to-all-start = ((bf16[32,96,128]{2,1,0:T(8,128)(2,1)}), bf16[32,96,128]{2,1,0:T(8,128)(2,1)S(1)}, u32[]{:S(2)}, u32[]{:S(2)}) async-start(bf16[32,96,128]{2,1,0:T(8,128)(2,1)} %broadcast_in_dim.29), calls=%async_computation | async-start | bytes 1572864 | tf_op jit(solution)/shard_map/while/body/eval_jaxpr/all_to_all | solution.py:9
  728.6 4.4 collective-permute-start
  734.3 45.4 %all-to-all-start = ((bf16[32,96,128]{2,1,0:T(8,128)(2,1)}), bf16[32,96,128]{2,1,0:T(8,128)(2,1)S(1)}, u32[]{:S(2)}, u32[]{:S(2)}) async-start(bf16[32,96,128]{2,1,0:T(8,128)(2,1)} %broadcast_in_dim.29), calls=%async_computation | async-start | bytes 1572864 | tf_op jit(solution)/shard_map/while/body/eval_jaxpr/all_to_all | solution.py:9
  782.0 4.9 collective-permute-start
  788.2 45.4 %all-to-all-start = ((bf16[32,96,128]{2,1,0:T(8,128)(2,1)}), bf16[32,96,128]{2,1,0:T(8,128)(2,1)S(1)}, u32[]{:S(2)}, u32[]{:S(2)}) async-start(bf16[32,96,128]{2,1,0:T(8,128)(2,1)} %broadcast_in_dim.29), calls=%async_computation | async-start | bytes 1572864 | tf_op jit(solution)/shard_map/while/body/eval_jaxpr/all_to_all | solution.py:9
  835.9 4.8 collective-permute-start
  842.0 45.4 %all-to-all-start = ((bf16[32,96,128]{2,1,0:T(8,128)(2,1)}), bf16[32,96,128]{2,1,0:T(8,128)(2,1)S(1)}, u32[]{:S(2)}, u32[]{:S(2)}) async-start(bf16[32,96,128]{2,1,0:T(8,128)(2,1)} %broadcast_in_dim.29), calls=%async_computation | async-start | bytes 1572864 | tf_op jit(solution)/shard_map/while/body/eval_jaxpr/all_to_all | solution.py:9
  889.6 5.0 collective-permute-start
  895.8 45.4 %all-to-all-start = ((bf16[32,96,128]{2,1,0:T(8,128)(2,1)}), bf16[32,96,128]{2,1,0:T(8,128)(2,1)S(1)}, u32[]{:S(2)}, u32[]{:S(2)}) async-start(bf16[32,96,128]{2,1,0:T(8,128)(2,1)} %broadcast_in_dim.29), calls=%async_computation | async-start | bytes 1572864 | tf_op jit(solution)/shard_map/while/body/eval_jaxpr/all_to_all | solution.py:9
  943.5 4.9 collective-permute-start
  949.6 45.4 %all-to-all-start = ((bf16[32,96,128]{2,1,0:T(8,128)(2,1)}), bf16[32,96,128]{2,1,0:T(8,128)(2,1)S(1)}, u32[]{:S(2)}, u32[]{:S(2)}) async-start(bf16[32,96,128]{2,1,0:T(8,128)(2,1)} %broadcast_in_dim.29), calls=%async_computation | async-start | bytes 1572864 | tf_op jit(solution)/shard_map/while/body/eval_jaxpr/all_to_all | solution.py:9
  997.3 4.9 collective-permute-start
  1003.4 45.4 %all-to-all-start = ((bf16[32,96,128]{2,1,0:T(8,128)(2,1)}), bf16[32,96,128]{2,1,0:T(8,128)(2,1)S(1)}, u32[]{:S(2)}, u32[]{:S(2)}) async-start(bf16[32,96,128]{2,1,0:T(8,128)(2,1)} %broadcast_in_dim.29), calls=%async_computation | async-start | bytes 1572864 | tf_op jit(solution)/shard_map/while/body/eval_jaxpr/all_to_all | solution.py:9
  1051.0 4.9 collective-permute-start
  1056.0 3.9 copy-start.1
where the time goes:
time: 1070 us; the launch traced here: 1060 us
  waiting for transfers between devices  747 us (70%)
  starting transfers between devices  190 us (18%)
  other arithmetic  48.1 us (4%)
  local copies, waits for them, and re-layouts  38.7 us (4%)
  matrix products  36.6 us (3%)
    all_to_all x19, waiting for transfers between devices, copy_for_each(): return lax.all_to_all(copies, axis, split_axis=0, concat_axis=0, tiled=True)  747 us
    all_to_all x19, starting transfers between devices, copy_for_each(): return lax.all_to_all(copies, axis, split_axis=0, concat_axis=0, tiled=True)  111 us
    ppermute x19, starting transfers between devices, shifted(): lax.ppermute(value, axis, [(source, source + steps) for source in range(i...  79.5 us
    dynamic_update_slice x19, other arithmetic, advance(): lax.dynamic_update_slice_in_dim(stored, jnp.where(active, gathered, previ...  43.4 us
    dot_general x20, matrix products, complex_apply(): jnp.dot(halves.reshape(2 * row_count, inner_width), vectors, preferred_el...  36.6 us
  transfers between devices with their start and end apart: 38, of which 19 were waited for; matrix products, arithmetic and copies ran while one was open for 4% of the time, Pallas kernels for 0%

commit v1 on v0

v1 whole, which is shorter than its diff:
```python
import jax
import jax.numpy as jnp
from jax import lax
from jax.experimental import pallas as pl
from jax.experimental.pallas import tpu as pltpu
from jax.sharding import Mesh, PartitionSpec as P

NB = 4
NY = 4
NZ = 8
NS = 16
BF = jnp.bfloat16
F32 = jnp.float32


def block_of(shape):
    lane = lax.broadcasted_iota(jnp.int32, shape, len(shape) - 1)
    return (lane // 16) % 4


def roll_blocks(x, k):
    k = (16 * k) % 128
    return pltpu.roll(x, k, x.ndim - 1) if k else x


def turn(x):
    lane = lax.broadcasted_iota(jnp.int32, x.shape, x.ndim - 1)
    swapped = pltpu.roll(x, 64, x.ndim - 1)
    return jnp.where(lane < 64, -swapped, swapped)


def pack_kernel(src_ref, out_ref):
    blk = block_of(src_ref.shape[1:])
    for b in range(NB):
        total = jnp.zeros(src_ref.shape[1:], F32)
        for y in range(NY):
            total = jnp.where(blk == y, roll_blocks(src_ref[y].astype(F32), y - b), total)
        out_ref[b] = total.astype(out_ref.dtype)


def swap_blocks(x, dtype):
    n, rows, lanes = x.shape
    step = 96
    return pl.pallas_call(
        pack_kernel,
        grid=(rows // step,),
        in_specs=[pl.BlockSpec((n, step, lanes), lambda i: (0, i, 0))],
        out_specs=pl.BlockSpec((n, step, lanes), lambda i: (0, i, 0)),
        out_shape=jax.ShapeDtypeStruct(x.shape, dtype),
        name="swap_blocks",
    )(x)


def step_kernel(idx_ref, g_ref, op_ref, src_ref, out_ref, send_ref, acc0, acc1):
    q = pl.program_id(0)
    g = g_ref[...]
    rows = NY * op_ref.shape[2]
    width = op_ref.shape[3]
    blk = block_of((rows, 128))
    for part, acc in ((0, acc0), (1, acc1)):
        d = jnp.dot(op_ref[:, part].reshape(rows, width), g, preferred_element_type=F32)
        acc[...] = jnp.where(blk == q, d, acc[...])

    @pl.when(q == NY - 1)
    def _():
        d = acc0[...] + turn(acc1[...])
        d = d + roll_blocks(d, 1)
        d = d + roll_blocks(d, 2)
        n = rows // NY
        small = block_of((n, 128))
        total = jnp.zeros((n, 128), F32)
        for y in range(NY):
            total = jnp.where(small == y, roll_blocks(d[y * n : (y + 1) * n], y - 3), total)
        total = total + src_ref[0]
        out_ref[...] = total
        send_ref[...] = total.astype(BF)


def apply_next(index, g, op, src):
    n = op.shape[2]
    depth = g.shape[0]
    return pl.pallas_call(
        step_kernel,
        grid_spec=pltpu.PrefetchScalarGridSpec(
            num_scalar_prefetch=1,
            grid=(NY,),
            in_specs=[
                pl.BlockSpec((depth, 128), lambda q, i: (0, 0)),
                pl.BlockSpec((NY, 2, n, depth), lambda q, i: (0, 0, 0, q)),
                pl.BlockSpec((1, n, 128), lambda q, i: (i[0], 0, 0)),
            ],
            out_specs=[
                pl.BlockSpec((n, 128), lambda q, i: (0, 0)),
                pl.BlockSpec((n, 128), lambda q, i: (0, 0)),
            ],
            scratch_shapes=[pltpu.VMEM((NY * n, 128), F32), pltpu.VMEM((NY * n, 128), F32)],
        ),
        out_shape=[jax.ShapeDtypeStruct((n, 128), F32), jax.ShapeDtypeStruct((n, 128), BF)],
        compiler_params=pltpu.CompilerParams(vmem_limit_bytes=24 * 2**20),
        cost_estimate=pl.CostEstimate(flops=2 * 8 * n * depth * 4 * 128, bytes_accessed=op.size * 2, transcendentals=0),
        name="apply_next",
    )(index, g, op, src)


def interior_kernel(op_ref, v_ref, out_ref):
    v = v_ref[0]
    d0 = jnp.dot(op_ref[0], v, preferred_element_type=F32)
    d1 = jnp.dot(op_ref[1], v, preferred_element_type=F32)
    out_ref[0] = d0 + turn(d1)


def apply_interior(op, v):
    _, n, depth = op.shape
    return pl.pallas_call(
        interior_kernel,
        grid=(NY,),
        in_specs=[
            pl.BlockSpec((2, n, depth), lambda f: (0, 0, 0)),
            pl.BlockSpec((1, depth, 128), lambda f: (f, 0, 0)),
        ],
        out_specs=pl.BlockSpec((1, n, 128), lambda f: (f, 0, 0)),
        out_shape=jax.ShapeDtypeStruct((NY, n, 128), F32),
        compiler_params=pltpu.CompilerParams(vmem_limit_bytes=24 * 2**20),
        name="apply_interior",
    )(op, v)


def spread(x, axis):
    copies = jnp.broadcast_to(x, (lax.axis_size(axis), *x.shape))
    return lax.all_to_all(copies, axis, split_axis=0, concat_axis=0, tiled=True)


def local(incident, green_interior, green_next, sources):
    s = lax.axis_index("slab")
    rows = incident.shape[1]
    op = spread(green_next[0], "y")
    inc = lax.all_to_all(incident.astype(BF), "y", 0, 0, tiled=True)
    src = lax.all_to_all(sources[0], "y", 0, 0, tiled=True)
    inc = swap_blocks(inc, BF)
    src = swap_blocks(src, F32)
    stored = jnp.zeros((NB + 2, NZ * rows, 128), BF)
    kept = jnp.zeros((NB + 2, rows, 128), F32)
    received = jnp.zeros((rows, 128), BF)
    for c in range(NS + NB - 1):
        entering = jnp.where(s == 0, inc[min(c, NB - 1)], received)
        g = spread(entering, "zl").reshape(NZ * rows, 128)
        batch = c - s
        chosen = jnp.clip(batch, 0, NB - 1).astype(jnp.int32).reshape(1)
        leaving, send = apply_next(chosen, g, op, src)
        if c < NS + NB - 2:
            pairs = [(a, a + 1) for a in range(NS - 1) if 0 <= c - a < NB]
            received = lax.ppermute(send, "slab", pairs)
        slot = jnp.clip(batch + 1, 0, NB + 1)
        stored = lax.dynamic_update_index_in_dim(stored, g, slot, 0)
        kept = lax.dynamic_update_index_in_dim(kept, leaving, slot, 0)
    traces = swap_blocks(kept[1 : NB + 1], F32)
    traces = lax.all_to_all(traces, "y", 0, 0, tiled=True)
    v = swap_blocks(stored[1 : NB + 1], BF).reshape(NY * NZ * rows, 128)
    fronts = spread(v, "y")
    interior = apply_interior(green_interior[0], fronts)
    return interior[None], traces[None]


def solution(mesh):
    fine = Mesh(mesh.devices.reshape(NS, NY, NZ), ("slab", "y", "zl"))
    trace = ("y", "zl")
    return jax.shard_map(
        local,
        mesh=fine,
        in_specs=(
            P(None, trace, None),
            P("slab", None, trace, None),
            P("slab", None, trace, None),
            P("slab", None, trace, None),
        ),
        out_specs=(P("slab", None, trace, None), P("slab", None, trace, None)),
        check_vma=False,
    )
```

time: 1070 us -> 684 us (0.64)
  the two profiles are of different devices: /device:TPU:1 before, /device:TPU:484 now
where the time goes in v1:
time: 684 us; the launch traced here: 680 us
  waiting for transfers between devices  308 us (45%)
  starting transfers between devices  216 us (32%)
  other arithmetic  97.8 us (14%)
  local copies, waits for them, and re-layouts  26.6 us (4%)
  blocking collectives  16.2 us (2%)
  Pallas kernels  14 us (2%)
    all_to_all x20, waiting for transfers between devices, spread(): return lax.all_to_all(copies, axis, split_axis=0, concat_axis=0, tiled=True)  213 us
    all_to_all x20, starting transfers between devices, spread(): return lax.all_to_all(copies, axis, split_axis=0, concat_axis=0, tiled=True)  188 us
    pallas_call x19, other arithmetic, apply_next(): pl.pallas_call(step_kernel, grid_spec=pltpu.PrefetchScalarGridSpec(num_sc...  95.2 us
    ppermute x18, waiting for transfers between devices, local(): received = lax.ppermute(send, 'slab', pairs)  84.8 us
    broadcast_in_dim x21, local copies, waits for them, and re-layouts, spread(): copies = jnp.broadcast_to(x, (lax.axis_size(axis), *x.shape))  18.7 us
    ppermute x18, starting transfers between devices, local(): received = lax.ppermute(send, 'slab', pairs)  16.9 us
    all_to_all x1, blocking collectives, spread(): return lax.all_to_all(copies, axis, split_axis=0, concat_axis=0, tiled=True)  16.2 us
  transfers between devices with their start and end apart: 41, of which 27 were waited for; matrix products, arithmetic and copies ran while one was open for 0% of the time, Pallas kernels for 1%

profile of v1, /device:TPU:484, one launch (start us, length us, event | category | flops | bytes accessed | tf_op | source)
XLA Modules:
  0.0 679.9 jit_solution(5033916312712719933)
XLA Ops:
  6.8 5.8 all-to-all-done.src_ref
  22.3 16.2 %all_to_all.120 = bf16[8,96,128]{2,1,0:T(8,128)(2,1)S(1)} all-to-all(bf16[8,96,128]{2,1,0:T(8,128)(2,1)S(1)} %broadcast_in_dim.196), channel_id=1, replica_groups=mesh['slab'=16,'y'=4,'zl'=8] {'zl'}, dimensions={0} | all-to-all | bytes 393216 | tf_op jit(solution)/shard_map/all_to_all | solution.py:130
  48.1 50.6 %all-to-all-done.2 = bf16[4,2,96,3072]{3,2,1,0:T(8,128)(2,1)} async-done(((bf16[4,2,96,3072]{3,2,1,0:T(8,128)(2,1)}), bf16[4,2,96,3072]{3,2,1,0:T(8,128)(2,1)}, u32[]{:S(2)}, u32[]{:S(2)}) %all-to-all-start.2) | async-done | bytes 4718624 | tf_op jit(solution)/shard_map/all_to_all | solution.py:130
  99.4 5.0 apply_next.37
  105.8 9.9 %all-to-all-start.4 = ((bf16[8,96,128]{2,1,0:T(8,128)(2,1)}), bf16[8,96,128]{2,1,0:T(8,128)(2,1)S(1)}, u32[]{:S(2)}, u32[]{:S(2)}) async-start(bf16[8,96,128]{2,1,0:T(8,128)(2,1)} %broadcast_in_dim.199), calls=%async_computation.4 | async-start | bytes 393216 | tf_op jit(solution)/shard_map/all_to_all | solution.py:130
  115.7 6.5 all-to-all-done.4
  122.2 5.0 apply_next.36
  128.6 9.9 %all-to-all-start.5 = ((bf16[8,96,128]{2,1,0:T(8,128)(2,1)}), bf16[8,96,128]{2,1,0:T(8,128)(2,1)S(1)}, u32[]{:S(2)}, u32[]{:S(2)}) async-start(bf16[8,96,128]{2,1,0:T(8,128)(2,1)} %broadcast_in_dim.201), calls=%async_computation.5 | async-start | bytes 393216 | tf_op jit(solution)/shard_map/all_to_all | solution.py:130
  138.5 6.7 all-to-all-done.5
  145.2 5.0 apply_next.35
  151.6 9.9 %all-to-all-start.6 = ((bf16[8,96,128]{2,1,0:T(8,128)(2,1)}), bf16[8,96,128]{2,1,0:T(8,128)(2,1)S(1)}, u32[]{:S(2)}, u32[]{:S(2)}) async-start(bf16[8,96,128]{2,1,0:T(8,128)(2,1)} %broadcast_in_dim.203), calls=%async_computation.6 | async-start | bytes 393216 | tf_op jit(solution)/shard_map/all_to_all | solution.py:130
  161.5 6.6 all-to-all-done.6
  168.1 5.0 apply_next.34
  174.5 9.9 %all-to-all-start.7 = ((bf16[8,96,128]{2,1,0:T(8,128)(2,1)}), bf16[8,96,128]{2,1,0:T(8,128)(2,1)S(1)}, u32[]{:S(2)}, u32[]{:S(2)}) async-start(bf16[8,96,128]{2,1,0:T(8,128)(2,1)} %broadcast_in_dim.205), calls=%async_computation.7 | async-start | bytes 393216 | tf_op jit(solution)/shard_map/all_to_all | solution.py:130
  184.4 6.6 all-to-all-done.7
  191.0 5.0 apply_next.33
  197.4 9.9 %all-to-all-start.8 = ((bf16[8,96,128]{2,1,0:T(8,128)(2,1)}), bf16[8,96,128]{2,1,0:T(8,128)(2,1)S(1)}, u32[]{:S(2)}, u32[]{:S(2)}) async-start(bf16[8,96,128]{2,1,0:T(8,128)(2,1)} %broadcast_in_dim.207), calls=%async_computation.8 | async-start | bytes 393216 | tf_op jit(solution)/shard_map/all_to_all | solution.py:130
  207.3 6.6 all-to-all-done.8
  214.0 5.0 apply_next.32
  220.3 9.9 %all-to-all-start.9 = ((bf16[8,96,128]{2,1,0:T(8,128)(2,1)}), bf16[8,96,128]{2,1,0:T(8,128)(2,1)S(1)}, u32[]{:S(2)}, u32[]{:S(2)}) async-start(bf16[8,96,128]{2,1,0:T(8,128)(2,1)} %broadcast_in_dim.209), calls=%async_computation.9 | async-start | bytes 393216 | tf_op jit(solution)/shard_map/all_to_all | solution.py:130
  230.2 6.6 all-to-all-done.9
  236.9 5.0 apply_next.31
  243.3 9.9 %all-to-all-start.10 = ((bf16[8,96,128]{2,1,0:T(8,128)(2,1)}), bf16[8,96,128]{2,1,0:T(8,128)(2,1)S(1)}, u32[]{:S(2)}, u32[]{:S(2)}) async-start(bf16[8,96,128]{2,1,0:T(8,128)(2,1)} %broadcast_in_dim.211), calls=%async_computation.10 | async-start | bytes 393216 | tf_op jit(solution)/shard_map/all_to_all | solution.py:130
  253.2 6.6 all-to-all-done.10
  259.8 5.0 apply_next.30
  266.2 9.9 %all-to-all-start.11 = ((bf16[8,96,128]{2,1,0:T(8,128)(2,1)}), bf16[8,96,128]{2,1,0:T(8,128)(2,1)S(1)}, u32[]{:S(2)}, u32[]{:S(2)}) async-start(bf16[8,96,128]{2,1,0:T(8,128)(2,1)} %broadcast_in_dim.213), calls=%async_computation.11 | async-start | bytes 393216 | tf_op jit(solution)/shard_map/all_to_all | solution.py:130
  276.1 6.6 all-to-all-done.11
  282.7 5.0 apply_next.29
  289.1 9.9 %all-to-all-start.12 = ((bf16[8,96,128]{2,1,0:T(8,128)(2,1)}), bf16[8,96,128]{2,1,0:T(8,128)(2,1)S(1)}, u32[]{:S(2)}, u32[]{:S(2)}) async-start(bf16[8,96,128]{2,1,0:T(8,128)(2,1)} %broadcast_in_dim.215), calls=%async_computation.12 | async-start | bytes 393216 | tf_op jit(solution)/shard_map/all_to_all | solution.py:130
  299.0 6.6 all-to-all-done.12
  305.7 5.0 apply_next.28
  312.0 9.9 %all-to-all-start.13 = ((bf16[8,96,128]{2,1,0:T(8,128)(2,1)}), bf16[8,96,128]{2,1,0:T(8,128)(2,1)S(1)}, u32[]{:S(2)}, u32[]{:S(2)}) async-start(bf16[8,96,128]{2,1,0:T(8,128)(2,1)} %broadcast_in_dim.217), calls=%async_computation.13 | async-start | bytes 393216 | tf_op jit(solution)/shard_map/all_to_all | solution.py:130
  321.9 6.6 all-to-all-done.13
  328.6 5.1 apply_next.27
  335.0 9.9 %all-to-all-start.14 = ((bf16[8,96,128]{2,1,0:T(8,128)(2,1)}), bf16[8,96,128]{2,1,0:T(8,128)(2,1)S(1)}, u32[]{:S(2)}, u32[]{:S(2)}) async-start(bf16[8,96,128]{2,1,0:T(8,128)(2,1)} %broadcast_in_dim.219), calls=%async_computation.14 | async-start | bytes 393216 | tf_op jit(solution)/shard_map/all_to_all | solution.py:130
  344.9 6.7 all-to-all-done.14
  351.6 5.1 apply_next.26
  357.9 35.6 %collective-permute-done.11 = bf16[96,128]{1,0:T(8,128)(2,1)S(1)} collective-permute-done((bf16[96,128]{1,0:T(8,128)(2,1)S(1)}, bf16[96,128]{1,0:T(8,128)(2,1)S(1)}, u32[]{:S(2)}, u32[]{:S(2)}) %collective-permute-start.11) | collective-permute-done | bytes 24608 | tf_op jit(solution)/shard_map/ppermute | solution.py:152
  394.2 9.9 %all-to-all-start.15 = ((bf16[8,96,128]{2,1,0:T(8,128)(2,1)}), bf16[8,96,128]{2,1,0:T(8,128)(2,1)S(1)}, u32[]{:S(2)}, u32[]{:S(2)}) async-start(bf16[8,96,128]{2,1,0:T(8,128)(2,1)} %broadcast_in_dim.221), calls=%async_computation.15 | async-start | bytes 393216 | tf_op jit(solution)/shard_map/all_to_all | solution.py:130
  404.1 6.2 all-to-all-done.15
  410.4 5.1 apply_next.25
  417.3 14.0 %collective-permute-done.12 = bf16[96,128]{1,0:T(8,128)(2,1)S(1)} collective-permute-done((bf16[96,128]{1,0:T(8,128)(2,1)S(1)}, bf16[96,128]{1,0:T(8,128)(2,1)S(1)}, u32[]{:S(2)}, u32[]{:S(2)}) %collective-permute-start.12) | collective-permute-done | bytes 24608 | tf_op jit(solution)/shard_map/ppermute | solution.py:152
  432.1 9.9 %all-to-all-start.16 = ((bf16[8,96,128]{2,1,0:T(8,128)(2,1)}), bf16[8,96,128]{2,1,0:T(8,128)(2,1)S(1)}, u32[]{:S(2)}, u32[]{:S(2)}) async-start(bf16[8,96,128]{2,1,0:T(8,128)(2,1)} %broadcast_in_dim.223), calls=%async_computation.16 | async-start | bytes 393216 | tf_op jit(solution)/shard_map/all_to_all | solution.py:130
  442.0 6.2 all-to-all-done.16
  448.2 5.1 apply_next.24
  455.2 14.2 %collective-permute-done.13 = bf16[96,128]{1,0:T(8,128)(2,1)S(1)} collective-permute-done((bf16[96,128]{1,0:T(8,128)(2,1)S(1)}, bf16[96,128]{1,0:T(8,128)(2,1)S(1)}, u32[]{:S(2)}, u32[]{:S(2)}) %collective-permute-start.13) | collective-permute-done | bytes 24608 | tf_op jit(solution)/shard_map/ppermute | solution.py:152
  470.2 9.9 %all-to-all-start.17 = ((bf16[8,96,128]{2,1,0:T(8,128)(2,1)}), bf16[8,96,128]{2,1,0:T(8,128)(2,1)S(1)}, u32[]{:S(2)}, u32[]{:S(2)}) async-start(bf16[8,96,128]{2,1,0:T(8,128)(2,1)} %broadcast_in_dim.225), calls=%async_computation.17 | async-start | bytes 393216 | tf_op jit(solution)/shard_map/all_to_all | solution.py:130
  480.1 6.2 all-to-all-done.17
  486.3 5.1 apply_next.23
  493.3 20.1 %collective-permute-done.14 = bf16[96,128]{1,0:T(8,128)(2,1)S(1)} collective-permute-done((bf16[96,128]{1,0:T(8,128)(2,1)S(1)}, bf16[96,128]{1,0:T(8,128)(2,1)S(1)}, u32[]{:S(2)}, u32[]{:S(2)}) %collective-permute-start.14) | collective-permute-done | bytes 24608 | tf_op jit(solution)/shard_map/ppermute | solution.py:152
  514.0 9.9 %all-to-all-start.18 = ((bf16[8,96,128]{2,1,0:T(8,128)(2,1)}), bf16[8,96,128]{2,1,0:T(8,128)(2,1)S(1)}, u32[]{:S(2)}, u32[]{:S(2)}) async-start(bf16[8,96,128]{2,1,0:T(8,128)(2,1)} %broadcast_in_dim.227), calls=%async_computation.18 | async-start | bytes 393216 | tf_op jit(solution)/shard_map/all_to_all | solution.py:130
  523.9 6.2 all-to-all-done.18
  530.2 5.1 apply_next.22
  538.1 9.9 %all-to-all-start.19 = ((bf16[8,96,128]{2,1,0:T(8,128)(2,1)}), bf16[8,96,128]{2,1,0:T(8,128)(2,1)}, u32[]{:S(2)}, u32[]{:S(2)}) async-start(bf16[8,96,128]{2,1,0:T(8,128)(2,1)} %broadcast_in_dim.229), calls=%async_computation.19 | async-start | bytes 393216 | tf_op jit(solution)/shard_map/all_to_all | solution.py:130
  548.2 9.6 %all-to-all-done.19 = bf16[8,96,128]{2,1,0:T(8,128)(2,1)} async-done(((bf16[8,96,128]{2,1,0:T(8,128)(2,1)}), bf16[8,96,128]{2,1,0:T(8,128)(2,1)}, u32[]{:S(2)}, u32[]{:S(2)}) %all-to-all-start.19) | async-done | bytes 196640 | tf_op jit(solution)/shard_map/all_to_all | solution.py:130
  557.8 5.1 apply_next.21
  564.3 9.9 %all-to-all-start.20 = ((bf16[8,96,128]{2,1,0:T(8,128)(2,1)}), bf16[8,96,128]{2,1,0:T(8,128)(2,1)S(1)}, u32[]{:S(2)}, u32[]{:S(2)}) async-start(bf16[8,96,128]{2,1,0:T(8,128)(2,1)} %broadcast_in_dim.231), calls=%async_computation.20 | async-start | bytes 393216 | tf_op jit(solution)/shard_map/all_to_all | solution.py:130
  574.4 9.9 %all-to-all-done.20 = bf16[8,96,128]{2,1,0:T(8,128)(2,1)S(1)} async-done(((bf16[8,96,128]{2,1,0:T(8,128)(2,1)}), bf16[8,96,128]{2,1,0:T(8,128)(2,1)S(1)}, u32[]{:S(2)}, u32[]{:S(2)}) %all-to-all-start.20) | async-done | bytes 196640 | tf_op jit(solution)/shard_map/all_to_all | solution.py:130
  585.1 5.0 apply_next.20
  591.7 9.9 %all-to-all-start.21 = ((bf16[8,96,128]{2,1,0:T(8,128)(2,1)}), bf16[8,96,128]{2,1,0:T(8,128)(2,1)S(1)}, u32[]{:S(2)}, u32[]{:S(2)}) async-start(bf16[8,96,128]{2,1,0:T(8,128)(2,1)} %broadcast_in_dim.233), calls=%async_computation.21 | async-start | bytes 393216 | tf_op jit(solution)/shard_map/all_to_all | solution.py:130
  602.8 8.1 %all-to-all-done.21 = bf16[8,96,128]{2,1,0:T(8,128)(2,1)S(1)} async-done(((bf16[8,96,128]{2,1,0:T(8,128)(2,1)}), bf16[8,96,128]{2,1,0:T(8,128)(2,1)S(1)}, u32[]{:S(2)}, u32[]{:S(2)}) %all-to-all-start.21) | async-done | bytes 196640 | tf_op jit(solution)/shard_map/all_to_all | solution.py:130
  610.9 5.0 apply_next.19
  623.8 5.6 swap_blocks.6
  637.3 37.3 %all-to-all-done.22.v_ref = bf16[4,3072,128]{2,1,0:T(8,128)(2,1)S(1)} async-done(((bf16[4,3072,128]{2,1,0:T(8,128)(2,1)}), bf16[4,3072,128]{2,1,0:T(8,128)(2,1)S(1)}, u32[]{:S(2)}, u32[]{:S(2)}) %all-to-all-start.22) | async-done | bytes 3145760 | tf_op jit(solution)/shard_map/all_to_all | solution.py:130
  (148 shorter events, 80.2 us)
Async XLA Ops:
  0.6 37.8 %copy-start.17 = (bf16[1,2,96,3072]{3,2,1,0:T(8,128)(2,1)S(1)}, bf16[1,2,96,3072]{3,2,1,0:T(8,128)(2,1)}, u32[]{:S(2)}) copy-start(bf16[1,2,96,3072]{3,2,1,0:T(8,128)(2,1)} %param.6) | copy-start | bytes 3538948
  2.3 10.3 %all-to-all-start = ((bf16[4,96,128]{2,1,0:T(8,128)(2,1)}), bf16[4,96,128]{2,1,0:T(8,128)(2,1)S(1)}, u32[]{:S(2)}, u32[]{:S(2)}) async-start(bf16[4,96,128]{2,1,0:T(8,128)(2,1)} %convert_element_type.3), calls=%async_computation | async-start | bytes 196608 | tf_op jit(solution)/shard_map/all_to_all | solution.py:137
  12.6 3.4 copy-start.19
  12.6 9.7 %all-to-all-start.3 = ((f32[4,96,128]{2,1,0:T(8,128)}), f32[4,96,128]{2,1,0:T(8,128)S(1)}, u32[]{:S(2)}, u32[]{:S(2)}) async-start(f32[4,96,128]{2,1,0:T(8,128)} %bitcast.225), calls=%async_computation.3 | async-start | bytes 393216 | tf_op jit(solution)/shard_map/all_to_all | solution.py:138
  22.3 19.0 %copy-start.18 = (f32[4,96,128]{2,1,0:T(8,128)}, f32[4,96,128]{2,1,0:T(8,128)S(1)}, u32[]{:S(2)}) copy-start(f32[4,96,128]{2,1,0:T(8,128)S(1)} %all-to-all-done.3.src_ref) | copy-start | bytes 589828
  41.3 57.4 %all-to-all-start.2 = ((bf16[4,2,96,3072]{3,2,1,0:T(8,128)(2,1)}), bf16[4,2,96,3072]{3,2,1,0:T(8,128)(2,1)}, u32[]{:S(2)}, u32[]{:S(2)}) async-start(bf16[4,2,96,3072]{3,2,1,0:T(8,128)(2,1)} %broadcast_in_dim.198), calls=%async_computation.2 | async-start | bytes 9437184 | tf_op jit(solution)/shard_map/all_to_all | solution.py:130
  99.4 5.7 copy-start.2
  99.4 22.8 %copy-start.1 = (f32[4,96,128]{2,1,0:T(8,128)S(1)}, f32[4,96,128]{2,1,0:T(8,128)}, u32[]{:S(2)}) copy-start(f32[4,96,128]{2,1,0:T(8,128)} %swap_blocks.5) | copy-start | bytes 589828
  104.4 0.7 collective-permute-start
  105.8 16.4 %all-to-all-start.4 = ((bf16[8,96,128]{2,1,0:T(8,128)(2,1)}), bf16[8,96,128]{2,1,0:T(8,128)(2,1)S(1)}, u32[]{:S(2)}, u32[]{:S(2)}) async-start(bf16[8,96,128]{2,1,0:T(8,128)(2,1)} %broadcast_in_dim.199), calls=%async_computation.4 | async-start | bytes 393216 | tf_op jit(solution)/shard_map/all_to_all | solution.py:130
  127.2 0.7 collective-permute-start.1
  128.6 16.6 %all-to-all-start.5 = ((bf16[8,96,128]{2,1,0:T(8,128)(2,1)}), bf16[8,96,128]{2,1,0:T(8,128)(2,1)S(1)}, u32[]{:S(2)}, u32[]{:S(2)}) async-start(bf16[8,96,128]{2,1,0:T(8,128)(2,1)} %broadcast_in_dim.201), calls=%async_computation.5 | async-start | bytes 393216 | tf_op jit(solution)/shard_map/all_to_all | solution.py:130
  150.2 0.7 collective-permute-start.2
  151.6 16.6 %all-to-all-start.6 = ((bf16[8,96,128]{2,1,0:T(8,128)(2,1)}), bf16[8,96,128]{2,1,0:T(8,128)(2,1)S(1)}, u32[]{:S(2)}, u32[]{:S(2)}) async-start(bf16[8,96,128]{2,1,0:T(8,128)(2,1)} %broadcast_in_dim.203), calls=%async_computation.6 | async-start | bytes 393216 | tf_op jit(solution)/shard_map/all_to_all | solution.py:130
  173.1 0.7 collective-permute-start.3
  174.5 16.6 %all-to-all-start.7 = ((bf16[8,96,128]{2,1,0:T(8,128)(2,1)}), bf16[8,96,128]{2,1,0:T(8,128)(2,1)S(1)}, u32[]{:S(2)}, u32[]{:S(2)}) async-start(bf16[8,96,128]{2,1,0:T(8,128)(2,1)} %broadcast_in_dim.205), calls=%async_computation.7 | async-start | bytes 393216 | tf_op jit(solution)/shard_map/all_to_all | solution.py:130
  196.0 0.7 collective-permute-start.4
  197.4 16.6 %all-to-all-start.8 = ((bf16[8,96,128]{2,1,0:T(8,128)(2,1)}), bf16[8,96,128]{2,1,0:T(8,128)(2,1)S(1)}, u32[]{:S(2)}, u32[]{:S(2)}) async-start(bf16[8,96,128]{2,1,0:T(8,128)(2,1)} %broadcast_in_dim.207), calls=%async_computation.8 | async-start | bytes 393216 | tf_op jit(solution)/shard_map/all_to_all | solution.py:130
  218.9 0.7 collective-permute-start.5
  220.3 16.6 %all-to-all-start.9 = ((bf16[8,96,128]{2,1,0:T(8,128)(2,1)}), bf16[8,96,128]{2,1,0:T(8,128)(2,1)S(1)}, u32[]{:S(2)}, u32[]{:S(2)}) async-start(bf16[8,96,128]{2,1,0:T(8,128)(2,1)} %broadcast_in_dim.209), calls=%async_computation.9 | async-start | bytes 393216 | tf_op jit(solution)/shard_map/all_to_all | solution.py:130
  241.9 0.7 collective-permute-start.6
  243.3 16.6 %all-to-all-start.10 = ((bf16[8,96,128]{2,1,0:T(8,128)(2,1)}), bf16[8,96,128]{2,1,0:T(8,128)(2,1)S(1)}, u32[]{:S(2)}, u32[]{:S(2)}) async-start(bf16[8,96,128]{2,1,0:T(8,128)(2,1)} %broadcast_in_dim.211), calls=%async_computation.10 | async-start | bytes 393216 | tf_op jit(solution)/shard_map/all_to_all | solution.py:130
  264.8 0.7 collective-permute-start.7
  266.2 16.6 %all-to-all-start.11 = ((bf16[8,96,128]{2,1,0:T(8,128)(2,1)}), bf16[8,96,128]{2,1,0:T(8,128)(2,1)S(1)}, u32[]{:S(2)}, u32[]{:S(2)}) async-start(bf16[8,96,128]{2,1,0:T(8,128)(2,1)} %broadcast_in_dim.213), calls=%async_computation.11 | async-start | bytes 393216 | tf_op jit(solution)/shard_map/all_to_all | solution.py:130
  287.7 0.7 collective-permute-start.8
  289.1 16.6 %all-to-all-start.12 = ((bf16[8,96,128]{2,1,0:T(8,128)(2,1)}), bf16[8,96,128]{2,1,0:T(8,128)(2,1)S(1)}, u32[]{:S(2)}, u32[]{:S(2)}) async-start(bf16[8,96,128]{2,1,0:T(8,128)(2,1)} %broadcast_in_dim.215), calls=%async_computation.12 | async-start | bytes 393216 | tf_op jit(solution)/shard_map/all_to_all | solution.py:130
  310.6 0.7 collective-permute-start.9
  312.0 16.6 %all-to-all-start.13 = ((bf16[8,96,128]{2,1,0:T(8,128)(2,1)}), bf16[8,96,128]{2,1,0:T(8,128)(2,1)S(1)}, u32[]{:S(2)}, u32[]{:S(2)}) async-start(bf16[8,96,128]{2,1,0:T(8,128)(2,1)} %broadcast_in_dim.217), calls=%async_computation.13 | async-start | bytes 393216 | tf_op jit(solution)/shard_map/all_to_all | solution.py:130
  328.6 5.1 copy-start.3
  333.6 0.7 collective-permute-start.10
  335.0 16.6 %all-to-all-start.14 = ((bf16[8,96,128]{2,1,0:T(8,128)(2,1)}), bf16[8,96,128]{2,1,0:T(8,128)(2,1)S(1)}, u32[]{:S(2)}, u32[]{:S(2)}) async-start(bf16[8,96,128]{2,1,0:T(8,128)(2,1)} %broadcast_in_dim.219), calls=%async_computation.14 | async-start | bytes 393216 | tf_op jit(solution)/shard_map/all_to_all | solution.py:130
  351.6 5.1 copy-start.5
  356.6 36.9 %collective-permute-start.11 = (bf16[96,128]{1,0:T(8,128)(2,1)S(1)}, bf16[96,128]{1,0:T(8,128)(2,1)S(1)}, u32[]{:S(2)}, u32[]{:S(2)}) collective-permute-start(bf16[96,128]{1,0:T(8,128)(2,1)S(1)} %get-tuple-element.114), channel_id=1, source_target_pairs={{256,288},{288,320},{320,352},{352,384},{257,289},{289,321},{321,3... | collective-permute-start | bytes 73736 | tf_op jit(solution)/shard_map/ppermute | solution.py:152
  394.2 16.1 %all-to-all-start.15 = ((bf16[8,96,128]{2,1,0:T(8,128)(2,1)}), bf16[8,96,128]{2,1,0:T(8,128)(2,1)S(1)}, u32[]{:S(2)}, u32[]{:S(2)}) async-start(bf16[8,96,128]{2,1,0:T(8,128)(2,1)} %broadcast_in_dim.221), calls=%async_computation.15 | async-start | bytes 393216 | tf_op jit(solution)/shard_map/all_to_all | solution.py:130
  410.4 5.1 copy-start.7
  415.4 16.0 %collective-permute-start.12 = (bf16[96,128]{1,0:T(8,128)(2,1)S(1)}, bf16[96,128]{1,0:T(8,128)(2,1)S(1)}, u32[]{:S(2)}, u32[]{:S(2)}) collective-permute-start(bf16[96,128]{1,0:T(8,128)(2,1)S(1)} %get-tuple-element.146), channel_id=1, source_target_pairs={{288,320},{320,352},{352,384},{384,416},{289,321},{321,353},{353,3... | collective-permute-start | bytes 73736 | tf_op jit(solution)/shard_map/ppermute | solution.py:152
  432.1 16.1 %all-to-all-start.16 = ((bf16[8,96,128]{2,1,0:T(8,128)(2,1)}), bf16[8,96,128]{2,1,0:T(8,128)(2,1)S(1)}, u32[]{:S(2)}, u32[]{:S(2)}) async-start(bf16[8,96,128]{2,1,0:T(8,128)(2,1)} %broadcast_in_dim.223), calls=%async_computation.16 | async-start | bytes 393216 | tf_op jit(solution)/shard_map/all_to_all | solution.py:130
  448.2 5.1 copy-start.9
  453.3 16.2 %collective-permute-start.13 = (bf16[96,128]{1,0:T(8,128)(2,1)S(1)}, bf16[96,128]{1,0:T(8,128)(2,1)S(1)}, u32[]{:S(2)}, u32[]{:S(2)}) collective-permute-start(bf16[96,128]{1,0:T(8,128)(2,1)S(1)} %get-tuple-element.118), channel_id=1, source_target_pairs={{320,352},{352,384},{384,416},{416,448},{321,353},{353,385},{385,4... | collective-permute-start | bytes 73736 | tf_op jit(solution)/shard_map/ppermute | solution.py:152
  470.2 16.1 %all-to-all-start.17 = ((bf16[8,96,128]{2,1,0:T(8,128)(2,1)}), bf16[8,96,128]{2,1,0:T(8,128)(2,1)S(1)}, u32[]{:S(2)}, u32[]{:S(2)}) async-start(bf16[8,96,128]{2,1,0:T(8,128)(2,1)} %broadcast_in_dim.225), calls=%async_computation.17 | async-start | bytes 393216 | tf_op jit(solution)/shard_map/all_to_all | solution.py:130
  486.3 5.1 copy-start.11
  491.3 22.0 %collective-permute-start.14 = (bf16[96,128]{1,0:T(8,128)(2,1)S(1)}, bf16[96,128]{1,0:T(8,128)(2,1)S(1)}, u32[]{:S(2)}, u32[]{:S(2)}) collective-permute-start(bf16[96,128]{1,0:T(8,128)(2,1)S(1)} %get-tuple-element.78), channel_id=1, source_target_pairs={{352,384},{384,416},{416,448},{448,480},{353,385},{385,417},{417,4... | collective-permute-start | bytes 73736 | tf_op jit(solution)/shard_map/ppermute | solution.py:152
  514.0 16.1 %all-to-all-start.18 = ((bf16[8,96,128]{2,1,0:T(8,128)(2,1)}), bf16[8,96,128]{2,1,0:T(8,128)(2,1)S(1)}, u32[]{:S(2)}, u32[]{:S(2)}) async-start(bf16[8,96,128]{2,1,0:T(8,128)(2,1)} %broadcast_in_dim.227), calls=%async_computation.18 | async-start | bytes 393216 | tf_op jit(solution)/shard_map/all_to_all | solution.py:130
  530.2 5.1 copy-start.13
  535.2 2.1 collective-permute-start.15
  538.1 19.8 %all-to-all-start.19 = ((bf16[8,96,128]{2,1,0:T(8,128)(2,1)}), bf16[8,96,128]{2,1,0:T(8,128)(2,1)}, u32[]{:S(2)}, u32[]{:S(2)}) async-start(bf16[8,96,128]{2,1,0:T(8,128)(2,1)} %broadcast_in_dim.229), calls=%async_computation.19 | async-start | bytes 393216 | tf_op jit(solution)/shard_map/all_to_all | solution.py:130
  562.9 0.7 collective-permute-start.16
  564.3 20.1 %all-to-all-start.20 = ((bf16[8,96,128]{2,1,0:T(8,128)(2,1)}), bf16[8,96,128]{2,1,0:T(8,128)(2,1)S(1)}, u32[]{:S(2)}, u32[]{:S(2)}) async-start(bf16[8,96,128]{2,1,0:T(8,128)(2,1)} %broadcast_in_dim.231), calls=%async_computation.20 | async-start | bytes 393216 | tf_op jit(solution)/shard_map/all_to_all | solution.py:130
  584.4 0.7 copy-start.15
  585.1 5.8 copy-start.4
  590.1 11.5 %copy-start.6 = (bf16[8,96,128]{2,1,0:T(8,128)(2,1)S(1)}, bf16[8,96,128]{2,1,0:T(8,128)(2,1)}, u32[]{:S(2)}) copy-start(bf16[8,96,128]{2,1,0:T(8,128)(2,1)} %copy-done.5) | copy-start | bytes 589828
  590.1 11.5 %copy-start.8 = (bf16[8,96,128]{2,1,0:T(8,128)(2,1)S(1)}, bf16[8,96,128]{2,1,0:T(8,128)(2,1)}, u32[]{:S(2)}) copy-start(bf16[8,96,128]{2,1,0:T(8,128)(2,1)} %copy-done.7) | copy-start | bytes 589828
  590.1 11.6 %copy-start.10 = (bf16[8,96,128]{2,1,0:T(8,128)(2,1)S(1)}, bf16[8,96,128]{2,1,0:T(8,128)(2,1)}, u32[]{:S(2)}) copy-start(bf16[8,96,128]{2,1,0:T(8,128)(2,1)} %copy-done.9) | copy-start | bytes 589828
  590.1 11.6 %copy-start.12 = (bf16[8,96,128]{2,1,0:T(8,128)(2,1)S(1)}, bf16[8,96,128]{2,1,0:T(8,128)(2,1)}, u32[]{:S(2)}) copy-start(bf16[8,96,128]{2,1,0:T(8,128)(2,1)} %copy-done.11) | copy-start | bytes 589828
  590.1 0.9 collective-permute-start.17
  591.0 10.8 %copy-start.14 = (bf16[8,96,128]{2,1,0:T(8,128)(2,1)S(1)}, bf16[8,96,128]{2,1,0:T(8,128)(2,1)}, u32[]{:S(2)}) copy-start(bf16[8,96,128]{2,1,0:T(8,128)(2,1)} %copy-done.13) | copy-start | bytes 589828
  591.7 19.2 %all-to-all-start.21 = ((bf16[8,96,128]{2,1,0:T(8,128)(2,1)}), bf16[8,96,128]{2,1,0:T(8,128)(2,1)S(1)}, u32[]{:S(2)}, u32[]{:S(2)}) async-start(bf16[8,96,128]{2,1,0:T(8,128)(2,1)} %broadcast_in_dim.233), calls=%async_computation.21 | async-start | bytes 393216 | tf_op jit(solution)/shard_map/all_to_all | solution.py:130
  615.9 6.9 %copy-start.16 = (bf16[8,96,128]{2,1,0:T(8,128)(2,1)S(1)}, bf16[8,96,128]{2,1,0:T(8,128)(2,1)}, u32[]{:S(2)}) copy-start(bf16[8,96,128]{2,1,0:T(8,128)(2,1)} %copy-done.15) | copy-start | bytes 589828
  619.4 10.0 %all-to-all-start.23 = ((f32[4,96,128]{2,1,0:T(8,128)}), f32[4,96,128]{2,1,0:T(8,128)S(1)}, u32[]{:S(2)}, u32[]{:S(2)}) async-start(f32[4,96,128]{2,1,0:T(8,128)} %swap_blocks.7), calls=%async_computation.23 | async-start | bytes 393216 | tf_op jit(solution)/shard_map/all_to_all | solution.py:157
  632.5 42.1 %all-to-all-start.22 = ((bf16[4,3072,128]{2,1,0:T(8,128)(2,1)}), bf16[4,3072,128]{2,1,0:T(8,128)(2,1)S(1)}, u32[]{:S(2)}, u32[]{:S(2)}) async-start(bf16[4,3072,128]{2,1,0:T(8,128)(2,1)} %broadcast_in_dim.235), calls=%async_computation.22 | async-start | bytes 6291456 | tf_op jit(solution)/shard_map/all_to_all | solution.py:130
  674.6 1.5 copy-start

commit v2 on v1

v2 whole, which is shorter than its diff:
```python
import jax
import jax.numpy as jnp
from jax import lax
from jax.experimental import pallas as pl
from jax.experimental.pallas import tpu as pltpu
from jax.sharding import Mesh, PartitionSpec as P

NB = 2
NY = 4
NH = 2
NZ = 4
NS = 16
BF = jnp.bfloat16
F32 = jnp.float32


def block_of(shape):
    lane = lax.broadcasted_iota(jnp.int32, shape, len(shape) - 1)
    return (lane // 16) % 4


def roll_blocks(x, k):
    k = (16 * k) % 128
    return pltpu.roll(x, k, x.ndim - 1) if k else x


def turn(x):
    lane = lax.broadcasted_iota(jnp.int32, x.shape, x.ndim - 1)
    swapped = pltpu.roll(x, 64, x.ndim - 1)
    return jnp.where(lane < 64, -swapped, swapped)


def pack_kernel(src_ref, out_ref):
    blk = block_of(src_ref.shape[1:])
    for b in range(NY):
        total = jnp.zeros(src_ref.shape[1:], F32)
        for y in range(NY):
            total = jnp.where(blk == y, roll_blocks(src_ref[y].astype(F32), y - b), total)
        out_ref[b] = total.astype(out_ref.dtype)


def swap_blocks(x, dtype, source=lambda i: i):
    n, rows, lanes = x.shape
    step = 96
    return pl.pallas_call(
        pack_kernel,
        grid=(rows // step,),
        in_specs=[pl.BlockSpec((n, step, lanes), lambda i: (0, source(i), 0))],
        out_specs=pl.BlockSpec((n, step, lanes), lambda i: (0, i, 0)),
        out_shape=jax.ShapeDtypeStruct(x.shape, dtype),
        name="swap_blocks",
    )(x)


def step_kernel(idx_ref, g_ref, near_ref, far_ref, src_ref, out_ref, send_ref):
    batch, half = idx_ref[0], idx_ref[1]
    n, depth = near_ref.shape[2], near_ref.shape[3] // NY
    rows = NY * n
    g = jnp.concatenate([g_ref[z, h] for h in range(NH) for z in range(NZ)], axis=0)
    blk = block_of((rows, 128))
    small = block_of((n, 128))
    for op_ref, h in ((near_ref, half), (far_ref, 1 - half)):
        parts = []
        for part in range(2):
            acc = jnp.zeros((rows, 128), F32)
            for q in range(NY):
                op = op_ref[:, part, :, depth * q : depth * (q + 1)].reshape(rows, depth)
                acc = jnp.where(blk == q, jnp.dot(op, g, preferred_element_type=F32), acc)
            parts.append(acc)
        d = parts[0] + turn(parts[1])
        d = d + roll_blocks(d, 1)
        d = d + roll_blocks(d, 2)
        total = jnp.zeros((n, 128), F32)
        for y in range(NY):
            total = jnp.where(small == y, roll_blocks(d[y * n : (y + 1) * n], y - 3), total)
        total = total + src_ref[h, batch]
        out_ref[h] = total
        send_ref[h] = total.astype(BF)


def apply_next(index, g, near, far, src):
    n, depth = near.shape[2], near.shape[3]
    whole = pl.BlockSpec(memory_space=pltpu.VMEM)
    return pl.pallas_call(
        step_kernel,
        in_specs=[pl.BlockSpec(memory_space=pltpu.SMEM), whole, whole, whole, whole],
        out_specs=[whole, whole],
        out_shape=[jax.ShapeDtypeStruct((NH, n, 128), F32), jax.ShapeDtypeStruct((NH, n, 128), BF)],
        compiler_params=pltpu.CompilerParams(vmem_limit_bytes=24 * 2**20),
        cost_estimate=pl.CostEstimate(flops=4 * 2 * NH * NY * n * depth * 128, bytes_accessed=near.size * 4, transcendentals=0),
        name="apply_next",
    )(index, g, near, far, src)


def interior_kernel(op_ref, v_ref, out_ref):
    v = v_ref[0]
    d0 = jnp.dot(op_ref[0], v, preferred_element_type=F32)
    d1 = jnp.dot(op_ref[1], v, preferred_element_type=F32)
    out_ref[0] = d0 + turn(d1)


def apply_interior(op, v):
    _, n, depth = op.shape
    return pl.pallas_call(
        interior_kernel,
        grid=(NY,),
        in_specs=[
            pl.BlockSpec((2, n, depth), lambda f: (0, 0, 0)),
            pl.BlockSpec((1, depth, 128), lambda f: (f, 0, 0)),
        ],
        out_specs=pl.BlockSpec((1, n, 128), lambda f: (f, 0, 0)),
        out_shape=jax.ShapeDtypeStruct((NY, n, 128), F32),
        compiler_params=pltpu.CompilerParams(vmem_limit_bytes=24 * 2**20),
        name="apply_interior",
    )(op, v)


def spread(x, axis):
    copies = jnp.broadcast_to(x, (lax.axis_size(axis), *x.shape))
    return lax.all_to_all(copies, axis, split_axis=0, concat_axis=0, tiled=True)


def local(incident, green_interior, green_next, sources):
    s = lax.axis_index("slab")
    half = lax.axis_index("zh")
    rows = incident.shape[1]
    op = green_next[0]
    far = lax.ppermute(op, "zh", [(0, 1), (1, 0)])
    inc = lax.all_to_all(incident.astype(BF), "y", 0, 0, tiled=True)
    src = lax.all_to_all(sources[0], "y", 0, 0, tiled=True)
    near = spread(op, "y")
    inc = swap_blocks(inc, BF).reshape(NH, NB, rows, 128)
    src = swap_blocks(src, F32).reshape(NH, NB, rows, 128)
    inc = lax.all_to_all(inc, "zh", 0, 0, tiled=True)
    src = lax.all_to_all(src, "zh", 0, 0, tiled=True)
    far = spread(far, "y")
    stored = jnp.zeros((NB + 2, NZ, NH, rows, 128), BF)
    kept = jnp.zeros((NB + 2, NH, rows, 128), F32)
    received = jnp.zeros((NH, rows, 128), BF)
    for c in range(NS + NB - 1):
        entering = jnp.where(s == 0, inc[:, min(c, NB - 1)], received)
        g = spread(entering, "zr")
        batch = c - s
        chosen = jnp.clip(batch, 0, NB - 1)
        index = jnp.stack([chosen, half]).astype(jnp.int32)
        leaving, send = apply_next(index, g, near, far, src)
        if c < NS + NB - 2:
            pairs = [(a, a + 1) for a in range(NS - 1) if 0 <= c - a < NB]
            received = lax.ppermute(send, "slab", pairs)
        slot = jnp.clip(batch + 1, 0, NB + 1)
        stored = lax.dynamic_update_index_in_dim(stored, g, slot, 0)
        kept = lax.dynamic_update_index_in_dim(kept, leaving, slot, 0)
    v = spread(stored[1 : NB + 1], "zh").reshape(NH * NB, NZ * NH * rows, 128)
    traces = lax.all_to_all(jnp.swapaxes(kept[1 : NB + 1], 0, 1), "zh", 0, 0, tiled=True)
    traces = swap_blocks(traces.reshape(NH * NB, rows, 128), F32)
    traces = lax.all_to_all(traces, "y", 0, 0, tiled=True)
    v = swap_blocks(v, BF, lambda i: (i % NZ) * NH + i // NZ).reshape(NY * NZ * NH * rows, 128)
    fronts = spread(v, "y")
    interior = apply_interior(green_interior[0], fronts)
    return interior[None], traces[None]


def solution(mesh):
    fine = Mesh(mesh.devices.reshape(NS, NY, NH, NZ), ("slab", "y", "zh", "zr"))
    trace = ("y", "zh", "zr")
    return jax.shard_map(
        local,
        mesh=fine,
        in_specs=(
            P(None, trace, None),
            P("slab", None, trace, None),
            P("slab", None, trace, None),
            P("slab", None, trace, None),
        ),
        out_specs=(P("slab", None, trace, None), P("slab", None, trace, None)),
        check_vma=False,
    )
```

time: 684 us -> 708 us (1.035)
  the two profiles are of different devices: /device:TPU:484 before, /device:TPU:262 now
where the time goes in v2:
time: 708 us; the launch traced here: 697 us
  waiting for transfers between devices  390 us (55%)
  Pallas kernels  128 us (18%)
  starting transfers between devices  106 us (15%)
  local copies, waits for them, and re-layouts  50.4 us (7%)
  blocking collectives  19.3 us (3%)
    all_to_all x20, waiting for transfers between devices, spread(): return lax.all_to_all(copies, axis, split_axis=0, concat_axis=0, tiled=True)  207 us
    pallas_call x17, Pallas kernels, apply_next(): pl.pallas_call(step_kernel, in_specs=[pl.BlockSpec(memory_space=pltpu.SME...  114 us
    ppermute x1, waiting for transfers between devices, local(): far = lax.ppermute(op, 'zh', [(0, 1), (1, 0)])  100 us
    all_to_all x20, starting transfers between devices, spread(): return lax.all_to_all(copies, axis, split_axis=0, concat_axis=0, tiled=True)  72.5 us
    ppermute x16, waiting for transfers between devices, local(): received = lax.ppermute(send, 'slab', pairs)  47.9 us
    broadcast_in_dim x21, local copies, waits for them, and re-layouts, spread(): copies = jnp.broadcast_to(x, (lax.axis_size(axis), *x.shape))  21.1 us
  transfers between devices with their start and end apart: 42, of which 28 were waited for; matrix products, arithmetic and copies ran while one was open for 4% of the time, Pallas kernels for 2%

profile of v2, /device:TPU:262, one launch (start us, length us, event | category | flops | bytes accessed | tf_op | source)
XLA Modules:
  0.0 696.8 jit_solution(9349478733054757994)
XLA Ops:
  1.7 10.2 %all_to_all.135.src_ref = bf16[4,96,128]{2,1,0:T(8,128)(2,1)} all-to-all(bf16[4,96,128]{2,1,0:T(8,128)(2,1)S(1)} %convert_element_type.3), channel_id=1, replica_groups=mesh['slab'=16,'y'=4,'zh'=2,'zr'=4] {'y'}, dimensions={0} | all-to-all | bytes 196608 | tf_op jit(solution)/shard_map/all_to_all | solution.py:129
  11.9 3.4 all-to-all-start.5
  16.9 4.6 all-to-all-done.5.src_ref
  21.5 3.6 all-to-all-start.1
  27.0 6.4 all-to-all-done.1
  33.4 3.4 all-to-all-start.6
  36.9 11.9 %all-to-all-done.6.src_ref = f32[2,2,96,128]{3,2,1,0:T(8,128)S(1)} async-done(((f32[2,2,96,128]{3,2,1,0:T(8,128)}), f32[2,2,96,128]{3,2,1,0:T(8,128)S(1)}, u32[]{:S(2)}, u32[]{:S(2)}) %all-to-all-start.6) | async-done | bytes 196640 | tf_op jit(solution)/shard_map/all_to_all | solution.py:135
  48.7 9.2 %all_to_all.136.g_ref = bf16[4,2,96,128]{3,2,1,0:T(8,128)(2,1)S(1)} all-to-all(bf16[4,2,96,128]{3,2,1,0:T(8,128)(2,1)S(1)} %broadcast_in_dim.184), channel_id=1, replica_groups=mesh['slab'=16,'y'=4,'zh'=2,'zr'=4] {'zr'}, dimensions={0} | all-to-all | bytes 393216 | tf_op jit(solution)/shard_map/all_to_all | solution.py:120
  60.7 4.9 all-to-all-start.3
  68.4 100.3 %collective-permute-done = bf16[2,96,3072]{2,1,0:T(8,128)(2,1)S(1)} collective-permute-done((bf16[2,96,3072]{2,1,0:T(8,128)(2,1)S(1)}, bf16[2,96,3072]{2,1,0:T(8,128)(2,1)S(1)}, u32[]{:S(2)}, u32[]{:S(2)}) %collective-permute-start) | collective-permute-done | bytes 1179680 | tf_op jit(solution)/shard_map/ppermute | solution.py:128
  171.5 5.0 all-to-all-start.4
  176.6 54.7 %all-to-all-done.4.far_ref = bf16[4,2,96,3072]{3,2,1,0:T(8,128)(2,1)} async-done(((bf16[4,2,96,3072]{3,2,1,0:T(8,128)(2,1)}), bf16[4,2,96,3072]{3,2,1,0:T(8,128)(2,1)}, u32[]{:S(2)}, u32[]{:S(2)}) %all-to-all-start.4) | async-done | bytes 4718624 | tf_op jit(solution)/shard_map/all_to_all | solution.py:120
  231.2 6.6 apply_next.17
  239.3 3.4 all-to-all-start.7
  242.7 6.6 all-to-all-done.7.g_ref
  249.4 6.6 apply_next.18
  257.4 3.4 all-to-all-start.8
  260.9 6.1 all-to-all-done.8.g_ref
  267.0 6.6 apply_next.19
  275.0 3.4 all-to-all-start.9
  278.5 6.1 all-to-all-done.9.g_ref
  284.6 6.6 apply_next.20
  292.7 3.8 all-to-all-start.10
  296.6 6.1 all-to-all-done.10.g_ref
  302.7 6.6 apply_next.21
  310.8 3.4 all-to-all-start.11
  314.2 6.1 all-to-all-done.11.g_ref
  320.4 6.6 apply_next.22
  328.4 3.4 all-to-all-start.12
  331.9 6.1 all-to-all-done.12.g_ref
  338.0 6.6 apply_next.23
  346.0 3.4 all-to-all-start.13
  349.6 6.0 all-to-all-done.13.g_ref
  355.6 6.7 apply_next.24
  367.6 5.8 all-to-all-done.14.g_ref
  373.3 6.7 apply_next.25
  381.5 3.5 all-to-all-start.15
  391.3 6.6 apply_next.26
  405.3 4.2 all-to-all-done.16.g_ref
  409.5 6.6 apply_next.27
  423.6 4.2 all-to-all-done.17.g_ref
  427.8 6.6 apply_next.28
  436.5 3.4 all-to-all-start.18
  441.9 4.2 all-to-all-done.18.g_ref
  446.1 6.6 apply_next.29
  460.1 4.2 all-to-all-done.19.g_ref
  464.4 6.6 apply_next.30
  473.2 32.7 %collective-permute-done.14 = bf16[2,96,128]{2,1,0:T(8,128)(2,1)S(1)} collective-permute-done((bf16[2,96,128]{2,1,0:T(8,128)(2,1)S(1)}, bf16[2,96,128]{2,1,0:T(8,128)(2,1)S(1)}, u32[]{:S(2)}, u32[]{:S(2)}) %collective-permute-start.14) | collective-permute-done | bytes 49184 | tf_op jit(solution)/shard_map/ppermute | solution.py:149
  512.0 4.2 all-to-all-done.20.g_ref
  516.2 6.7 apply_next.31
  525.5 14.9 %collective-permute-done.15 = bf16[2,96,128]{2,1,0:T(8,128)(2,1)S(1)} collective-permute-done((bf16[2,96,128]{2,1,0:T(8,128)(2,1)S(1)}, bf16[2,96,128]{2,1,0:T(8,128)(2,1)S(1)}, u32[]{:S(2)}, u32[]{:S(2)}) %collective-permute-start.15) | collective-permute-done | bytes 49184 | tf_op jit(solution)/shard_map/ppermute | solution.py:149
  541.1 3.9 all-to-all-start.21
  547.1 4.2 all-to-all-done.21.g_ref
  551.3 6.6 apply_next.32
  566.2 6.2 all-to-all-done.22.g_ref
  572.4 7.3 %apply_next.33 = (f32[2,96,128]{2,1,0:T(8,128)S(1)}, bf16[2,96,128]{2,1,0:T(8,128)(2,1)}) custom-call(s32[2]{0:T(128)S(1)} %pad_add_fusion.16.idx_ref, bf16[4,2,96,128]{3,2,1,0:T(8,128)(2,1)S(1)} %all-to-all-done.22.g_ref, bf16[4,2,96,3072]{3,2,1,0:T(8,128)(2,1)} %all-to-all-done.3.near_ref, bf16[4,2,96,3072]{3,2,1,0:T(8,128)(2,1)} %all-to-all-done.4.far_ref, ...), custom_call_target="tpu_custom_call" | custom-call | flops 2415919104 | bytes 9437184 | tf_op jit(solution)/shard_map/apply_next/pallas_call | solution.py:84
  582.0 3.4 all-to-all-start.25
  587.8 11.1 %all-to-all-done.25 = f32[2,2,96,128]{3,2,1,0:T(8,128)S(1)} async-done(((f32[2,2,96,128]{3,2,1,0:T(8,128)}), f32[2,2,96,128]{3,2,1,0:T(8,128)S(1)}, u32[]{:S(2)}, u32[]{:S(2)}) %all-to-all-start.25) | async-done | bytes 196640 | tf_op jit(solution)/shard_map/all_to_all | solution.py:154
  600.0 3.5 all-to-all-start.23
  605.4 31.5 %all-to-all-done.23 = bf16[2,2,4,2,96,128]{5,4,3,2,1,0:T(8,128)(2,1)S(1)} async-done(((bf16[2,2,4,2,96,128]{5,4,3,2,1,0:T(8,128)(2,1)}), bf16[2,2,4,2,96,128]{5,4,3,2,1,0:T(8,128)(2,1)S(1)}, u32[]{:S(2)}, u32[]{:S(2)}) %all-to-all-start.23) | async-done | bytes 786464 | tf_op jit(solution)/shard_map/all_to_all | solution.py:120
  636.9 3.4 all-to-all-start.26
  640.3 5.6 swap_blocks.6
  649.8 4.0 all-to-all-start.24
  653.8 37.5 %all-to-all-done.24.v_ref = bf16[4,3072,128]{2,1,0:T(8,128)(2,1)S(1)} async-done(((bf16[4,3072,128]{2,1,0:T(8,128)(2,1)}), bf16[4,3072,128]{2,1,0:T(8,128)(2,1)S(1)}, u32[]{:S(2)}, u32[]{:S(2)}) %all-to-all-start.24) | async-done | bytes 3145760 | tf_op jit(solution)/shard_map/all_to_all | solution.py:120
  (149 shorter events, 101.0 us)
Async XLA Ops:
  0.6 57.3 %copy-start.2 = (bf16[1,2,96,3072]{3,2,1,0:T(8,128)(2,1)S(1)}, bf16[1,2,96,3072]{3,2,1,0:T(8,128)(2,1)}, u32[]{:S(2)}) copy-start(bf16[1,2,96,3072]{3,2,1,0:T(8,128)(2,1)} %param.6) | copy-start | bytes 3538948
  11.9 9.7 %all-to-all-start.5 = ((f32[4,96,128]{2,1,0:T(8,128)}), f32[4,96,128]{2,1,0:T(8,128)S(1)}, u32[]{:S(2)}, u32[]{:S(2)}) async-start(f32[4,96,128]{2,1,0:T(8,128)} %bitcast.180), calls=%async_computation.5 | async-start | bytes 393216 | tf_op jit(solution)/shard_map/all_to_all | solution.py:130
  21.5 3.7 copy-start.4
  21.5 11.9 %all-to-all-start.1 = ((bf16[2,2,96,128]{3,2,1,0:T(8,128)(2,1)}), bf16[2,2,96,128]{3,2,1,0:T(8,128)(2,1)S(1)}, u32[]{:S(2)}, u32[]{:S(2)}) async-start(bf16[2,2,96,128]{3,2,1,0:T(8,128)(2,1)} %bitcast.178), calls=%async_computation.1 | async-start | bytes 196608 | tf_op jit(solution)/shard_map/all_to_all | solution.py:134
  33.4 15.3 %all-to-all-start.6 = ((f32[2,2,96,128]{3,2,1,0:T(8,128)}), f32[2,2,96,128]{3,2,1,0:T(8,128)S(1)}, u32[]{:S(2)}, u32[]{:S(2)}) async-start(f32[2,2,96,128]{3,2,1,0:T(8,128)} %bitcast.177), calls=%async_computation.6 | async-start | bytes 393216 | tf_op jit(solution)/shard_map/all_to_all | solution.py:135
  60.7 108.0 %all-to-all-start.3 = ((bf16[4,2,96,3072]{3,2,1,0:T(8,128)(2,1)}), bf16[4,2,96,3072]{3,2,1,0:T(8,128)(2,1)}, u32[]{:S(2)}, u32[]{:S(2)}) async-start(bf16[4,2,96,3072]{3,2,1,0:T(8,128)(2,1)} %broadcast_in_dim.186), calls=%async_computation.3 | async-start | bytes 9437184 | tf_op jit(solution)/shard_map/all_to_all | solution.py:120
  65.7 103.0 %collective-permute-start = (bf16[2,96,3072]{2,1,0:T(8,128)(2,1)S(1)}, bf16[2,96,3072]{2,1,0:T(8,128)(2,1)S(1)}, u32[]{:S(2)}, u32[]{:S(2)}) collective-permute-start(bf16[2,96,3072]{2,1,0:T(8,128)(2,1)S(1)} %bitcast.174), channel_id=1, source_target_pairs={{0,4},{4,0},{1,5},{5,1},{2,6},{6,2},{3,7},{7,3},{8,12},{12,8},{9,1... | collective-permute-start | bytes 3538952 | tf_op jit(solution)/shard_map/ppermute | solution.py:128
  171.5 59.7 %all-to-all-start.4 = ((bf16[4,2,96,3072]{3,2,1,0:T(8,128)(2,1)}), bf16[4,2,96,3072]{3,2,1,0:T(8,128)(2,1)}, u32[]{:S(2)}, u32[]{:S(2)}) async-start(bf16[4,2,96,3072]{3,2,1,0:T(8,128)(2,1)} %broadcast_in_dim.187), calls=%async_computation.4 | async-start | bytes 9437184 | tf_op jit(solution)/shard_map/all_to_all | solution.py:120
  237.9 0.7 collective-permute-start.1
  239.3 10.1 %all-to-all-start.7 = ((bf16[4,2,96,128]{3,2,1,0:T(8,128)(2,1)}), bf16[4,2,96,128]{3,2,1,0:T(8,128)(2,1)S(1)}, u32[]{:S(2)}, u32[]{:S(2)}) async-start(bf16[4,2,96,128]{3,2,1,0:T(8,128)(2,1)} %broadcast_in_dim.188), calls=%async_computation.7 | async-start | bytes 393216 | tf_op jit(solution)/shard_map/all_to_all | solution.py:120
  256.0 0.7 collective-permute-start.2
  257.4 9.6 %all-to-all-start.8 = ((bf16[4,2,96,128]{3,2,1,0:T(8,128)(2,1)}), bf16[4,2,96,128]{3,2,1,0:T(8,128)(2,1)S(1)}, u32[]{:S(2)}, u32[]{:S(2)}) async-start(bf16[4,2,96,128]{3,2,1,0:T(8,128)(2,1)} %broadcast_in_dim.190), calls=%async_computation.8 | async-start | bytes 393216 | tf_op jit(solution)/shard_map/all_to_all | solution.py:120
  273.6 0.7 collective-permute-start.3
  275.0 9.6 %all-to-all-start.9 = ((bf16[4,2,96,128]{3,2,1,0:T(8,128)(2,1)}), bf16[4,2,96,128]{3,2,1,0:T(8,128)(2,1)S(1)}, u32[]{:S(2)}, u32[]{:S(2)}) async-start(bf16[4,2,96,128]{3,2,1,0:T(8,128)(2,1)} %broadcast_in_dim.192), calls=%async_computation.9 | async-start | bytes 393216 | tf_op jit(solution)/shard_map/all_to_all | solution.py:120
  291.3 0.7 collective-permute-start.4
  292.7 10.0 %all-to-all-start.10 = ((bf16[4,2,96,128]{3,2,1,0:T(8,128)(2,1)}), bf16[4,2,96,128]{3,2,1,0:T(8,128)(2,1)S(1)}, u32[]{:S(2)}, u32[]{:S(2)}) async-start(bf16[4,2,96,128]{3,2,1,0:T(8,128)(2,1)} %broadcast_in_dim.194), calls=%async_computation.10 | async-start | bytes 393216 | tf_op jit(solution)/shard_map/all_to_all | solution.py:120
  309.4 0.7 collective-permute-start.5
  310.8 9.6 %all-to-all-start.11 = ((bf16[4,2,96,128]{3,2,1,0:T(8,128)(2,1)}), bf16[4,2,96,128]{3,2,1,0:T(8,128)(2,1)S(1)}, u32[]{:S(2)}, u32[]{:S(2)}) async-start(bf16[4,2,96,128]{3,2,1,0:T(8,128)(2,1)} %broadcast_in_dim.196), calls=%async_computation.11 | async-start | bytes 393216 | tf_op jit(solution)/shard_map/all_to_all | solution.py:120
  327.0 0.7 collective-permute-start.6
  328.4 9.6 %all-to-all-start.12 = ((bf16[4,2,96,128]{3,2,1,0:T(8,128)(2,1)}), bf16[4,2,96,128]{3,2,1,0:T(8,128)(2,1)S(1)}, u32[]{:S(2)}, u32[]{:S(2)}) async-start(bf16[4,2,96,128]{3,2,1,0:T(8,128)(2,1)} %broadcast_in_dim.198), calls=%async_computation.12 | async-start | bytes 393216 | tf_op jit(solution)/shard_map/all_to_all | solution.py:120
  344.6 0.7 collective-permute-start.7
  346.0 9.6 %all-to-all-start.13 = ((bf16[4,2,96,128]{3,2,1,0:T(8,128)(2,1)}), bf16[4,2,96,128]{3,2,1,0:T(8,128)(2,1)S(1)}, u32[]{:S(2)}, u32[]{:S(2)}) async-start(bf16[4,2,96,128]{3,2,1,0:T(8,128)(2,1)} %broadcast_in_dim.200), calls=%async_computation.13 | async-start | bytes 393216 | tf_op jit(solution)/shard_map/all_to_all | solution.py:120
  362.3 0.8 collective-permute-start.8
  363.8 9.6 %all-to-all-start.14 = ((bf16[4,2,96,128]{3,2,1,0:T(8,128)(2,1)}), bf16[4,2,96,128]{3,2,1,0:T(8,128)(2,1)S(1)}, u32[]{:S(2)}, u32[]{:S(2)}) async-start(bf16[4,2,96,128]{3,2,1,0:T(8,128)(2,1)} %broadcast_in_dim.202), calls=%async_computation.14 | async-start | bytes 393216 | tf_op jit(solution)/shard_map/all_to_all | solution.py:120
  380.0 0.8 collective-permute-start.9
  381.5 9.8 %all-to-all-start.15 = ((bf16[4,2,96,128]{3,2,1,0:T(8,128)(2,1)}), bf16[4,2,96,128]{3,2,1,0:T(8,128)(2,1)S(1)}, u32[]{:S(2)}, u32[]{:S(2)}) async-start(bf16[4,2,96,128]{3,2,1,0:T(8,128)(2,1)} %broadcast_in_dim.204), calls=%async_computation.15 | async-start | bytes 393216 | tf_op jit(solution)/shard_map/all_to_all | solution.py:120
  397.9 1.3 collective-permute-start.10
  399.9 9.6 %all-to-all-start.16 = ((bf16[4,2,96,128]{3,2,1,0:T(8,128)(2,1)}), bf16[4,2,96,128]{3,2,1,0:T(8,128)(2,1)S(1)}, u32[]{:S(2)}, u32[]{:S(2)}) async-start(bf16[4,2,96,128]{3,2,1,0:T(8,128)(2,1)} %broadcast_in_dim.206), calls=%async_computation.16 | async-start | bytes 393216 | tf_op jit(solution)/shard_map/all_to_all | solution.py:120
  416.2 1.3 collective-permute-start.11
  418.2 9.6 %all-to-all-start.17 = ((bf16[4,2,96,128]{3,2,1,0:T(8,128)(2,1)}), bf16[4,2,96,128]{3,2,1,0:T(8,128)(2,1)S(1)}, u32[]{:S(2)}, u32[]{:S(2)}) async-start(bf16[4,2,96,128]{3,2,1,0:T(8,128)(2,1)} %broadcast_in_dim.208), calls=%async_computation.17 | async-start | bytes 393216 | tf_op jit(solution)/shard_map/all_to_all | solution.py:120
  434.4 1.3 collective-permute-start.12
  436.5 9.6 %all-to-all-start.18 = ((bf16[4,2,96,128]{3,2,1,0:T(8,128)(2,1)}), bf16[4,2,96,128]{3,2,1,0:T(8,128)(2,1)S(1)}, u32[]{:S(2)}, u32[]{:S(2)}) async-start(bf16[4,2,96,128]{3,2,1,0:T(8,128)(2,1)} %broadcast_in_dim.210), calls=%async_computation.18 | async-start | bytes 393216 | tf_op jit(solution)/shard_map/all_to_all | solution.py:120
  452.7 1.3 collective-permute-start.13
  454.7 9.6 %all-to-all-start.19 = ((bf16[4,2,96,128]{3,2,1,0:T(8,128)(2,1)}), bf16[4,2,96,128]{3,2,1,0:T(8,128)(2,1)S(1)}, u32[]{:S(2)}, u32[]{:S(2)}) async-start(bf16[4,2,96,128]{3,2,1,0:T(8,128)(2,1)} %broadcast_in_dim.212), calls=%async_computation.19 | async-start | bytes 393216 | tf_op jit(solution)/shard_map/all_to_all | solution.py:120
  471.0 34.9 %collective-permute-start.14 = (bf16[2,96,128]{2,1,0:T(8,128)(2,1)S(1)}, bf16[2,96,128]{2,1,0:T(8,128)(2,1)S(1)}, u32[]{:S(2)}, u32[]{:S(2)}) collective-permute-start(bf16[2,96,128]{2,1,0:T(8,128)(2,1)S(1)} %get-tuple-element.48), channel_id=1, source_target_pairs={{384,416},{416,448},{385,417},{417,449},{386,418},{418,450},{387,4... | collective-permute-start | bytes 147464 | tf_op jit(solution)/shard_map/ppermute | solution.py:149
  506.6 9.6 %all-to-all-start.20 = ((bf16[4,2,96,128]{3,2,1,0:T(8,128)(2,1)}), bf16[4,2,96,128]{3,2,1,0:T(8,128)(2,1)S(1)}, u32[]{:S(2)}, u32[]{:S(2)}) async-start(bf16[4,2,96,128]{3,2,1,0:T(8,128)(2,1)} %broadcast_in_dim.214), calls=%async_computation.20 | async-start | bytes 393216 | tf_op jit(solution)/shard_map/all_to_all | solution.py:120
  522.9 17.5 %collective-permute-start.15 = (bf16[2,96,128]{2,1,0:T(8,128)(2,1)S(1)}, bf16[2,96,128]{2,1,0:T(8,128)(2,1)S(1)}, u32[]{:S(2)}, u32[]{:S(2)}) collective-permute-start(bf16[2,96,128]{2,1,0:T(8,128)(2,1)S(1)} %get-tuple-element.49), channel_id=1, source_target_pairs={{416,448},{448,480},{417,449},{449,481},{418,450},{450,482},{419,4... | collective-permute-start | bytes 147464 | tf_op jit(solution)/shard_map/ppermute | solution.py:149
  541.1 10.2 %all-to-all-start.21 = ((bf16[4,2,96,128]{3,2,1,0:T(8,128)(2,1)}), bf16[4,2,96,128]{3,2,1,0:T(8,128)(2,1)S(1)}, u32[]{:S(2)}, u32[]{:S(2)}) async-start(bf16[4,2,96,128]{3,2,1,0:T(8,128)(2,1)} %broadcast_in_dim.216), calls=%async_computation.21 | async-start | bytes 393216 | tf_op jit(solution)/shard_map/all_to_all | solution.py:120
  558.0 2.2 collective-permute-start.16
  560.8 11.6 %all-to-all-start.22 = ((bf16[4,2,96,128]{3,2,1,0:T(8,128)(2,1)}), bf16[4,2,96,128]{3,2,1,0:T(8,128)(2,1)S(1)}, u32[]{:S(2)}, u32[]{:S(2)}) async-start(bf16[4,2,96,128]{3,2,1,0:T(8,128)(2,1)} %broadcast_in_dim.218), calls=%async_computation.22 | async-start | bytes 393216 | tf_op jit(solution)/shard_map/all_to_all | solution.py:120
  582.0 17.0 %all-to-all-start.25 = ((f32[2,2,96,128]{3,2,1,0:T(8,128)}), f32[2,2,96,128]{3,2,1,0:T(8,128)S(1)}, u32[]{:S(2)}, u32[]{:S(2)}) async-start(f32[2,2,96,128]{3,2,1,0:T(8,128)} %slice_bitcast_fusion), calls=%async_computation.25 | async-start | bytes 393216 | tf_op jit(solution)/shard_map/all_to_all | solution.py:154
  598.9 4.6 copy-start.3
  600.0 36.9 %all-to-all-start.23 = ((bf16[2,2,4,2,96,128]{5,4,3,2,1,0:T(8,128)(2,1)}), bf16[2,2,4,2,96,128]{5,4,3,2,1,0:T(8,128)(2,1)S(1)}, u32[]{:S(2)}, u32[]{:S(2)}) async-start(bf16[2,2,4,2,96,128]{5,4,3,2,1,0:T(8,128)(2,1)} %broadcast_in_dim.220), calls=%async_computation.23 | async-start | bytes 1572864 | tf_op jit(solution)/shard_map/all_to_all | solution.py:120
  636.9 3.4 copy-start.1
  636.9 9.8 %all-to-all-start.26 = ((f32[4,96,128]{2,1,0:T(8,128)}), f32[4,96,128]{2,1,0:T(8,128)S(1)}, u32[]{:S(2)}, u32[]{:S(2)}) async-start(f32[4,96,128]{2,1,0:T(8,128)} %swap_blocks.7), calls=%async_computation.26 | async-start | bytes 393216 | tf_op jit(solution)/shard_map/all_to_all | solution.py:156
  649.8 41.4 %all-to-all-start.24 = ((bf16[4,3072,128]{2,1,0:T(8,128)(2,1)}), bf16[4,3072,128]{2,1,0:T(8,128)(2,1)S(1)}, u32[]{:S(2)}, u32[]{:S(2)}) async-start(bf16[4,3072,128]{2,1,0:T(8,128)(2,1)} %broadcast_in_dim.221), calls=%async_computation.24 | async-start | bytes 6291456 | tf_op jit(solution)/shard_map/all_to_all | solution.py:120
  691.3 1.5 copy-start

commit v3 on v2

--- a/solution.py
+++ b/solution.py
@@ -39,32 +39,45 @@
         out_ref[b] = total.astype(out_ref.dtype)
 
 
-def swap_blocks(x, dtype, source=lambda i: i):
+def swap_blocks(x, dtype):
     n, rows, lanes = x.shape
     step = 96
     return pl.pallas_call(
         pack_kernel,
         grid=(rows // step,),
-        in_specs=[pl.BlockSpec((n, step, lanes), lambda i: (0, source(i), 0))],
+        in_specs=[pl.BlockSpec((n, step, lanes), lambda i: (0, i, 0))],
         out_specs=pl.BlockSpec((n, step, lanes), lambda i: (0, i, 0)),
         out_shape=jax.ShapeDtypeStruct(x.shape, dtype),
         name="swap_blocks",
     )(x)
 
 
-def step_kernel(idx_ref, g_ref, near_ref, far_ref, src_ref, out_ref, send_ref):
+def step_kernel(idx_ref, g_ref, near_hbm, real_hbm, imag_a_hbm, imag_b_hbm, src_ref, out_ref, send_ref, op_ref, sems):
     batch, half = idx_ref[0], idx_ref[1]
-    n, depth = near_ref.shape[2], near_ref.shape[3] // NY
+    n, depth = op_ref.shape[2], op_ref.shape[3] // NY
+    places = (
+        (near_hbm.at[:, 0], op_ref.at[0]),
+        (near_hbm.at[:, 1], op_ref.at[1]),
+        (real_hbm, op_ref.at[2]),
+        (imag_a_hbm, op_ref.at[3, :, : n // 2]),
+        (imag_b_hbm, op_ref.at[3, :, n // 2 :]),
+    )
+    copies = [pltpu.make_async_copy(there, here, sems.at[k]) for k, (there, here) in enumerate(places)]
+    for copy in copies:
+        copy.start()
     rows = NY * n
     g = jnp.concatenate([g_ref[z, h] for h in range(NH) for z in range(NZ)], axis=0)
     blk = block_of((rows, 128))
     small = block_of((n, 128))
-    for op_ref, h in ((near_ref, half), (far_ref, 1 - half)):
+    for far, h in ((0, half), (1, 1 - half)):
         parts = []
         for part in range(2):
             acc = jnp.zeros((rows, 128), F32)
+            copies[2 * far + part].wait()
+            if far and part:
+                copies[4].wait()
             for q in range(NY):
-                op = op_ref[:, part, :, depth * q : depth * (q + 1)].reshape(rows, depth)
+                op = op_ref[2 * far + part, :, :, depth * q : depth * (q + 1)].reshape(rows, depth)
                 acc = jnp.where(blk == q, jnp.dot(op, g, preferred_element_type=F32), acc)
             parts.append(acc)
         d = parts[0] + turn(parts[1])
@@ -78,41 +91,57 @@
         send_ref[h] = total.astype(BF)
 
 
-def apply_next(index, g, near, far, src):
-    n, depth = near.shape[2], near.shape[3]
+def apply_next(index, g, near, real, imag_a, imag_b, src):
+    n, depth = real.shape[1], real.shape[2]
+    there = pl.BlockSpec(memory_space=pl.ANY)
     whole = pl.BlockSpec(memory_space=pltpu.VMEM)
     return pl.pallas_call(
         step_kernel,
-        in_specs=[pl.BlockSpec(memory_space=pltpu.SMEM), whole, whole, whole, whole],
+        in_specs=[pl.BlockSpec(memory_space=pltpu.SMEM), whole, there, there, there, there, whole],
         out_specs=[whole, whole],
+        scratch_shapes=[pltpu.VMEM((4, NY, n, depth), BF), pltpu.SemaphoreType.DMA((5,))],
         out_shape=[jax.ShapeDtypeStruct((NH, n, 128), F32), jax.ShapeDtypeStruct((NH, n, 128), BF)],
         compiler_params=pltpu.CompilerParams(vmem_limit_bytes=24 * 2**20),
         cost_estimate=pl.CostEstimate(flops=4 * 2 * NH * NY * n * depth * 128, bytes_accessed=near.size * 4, transcendentals=0),
         name="apply_next",
-    )(index, g, near, far, src)
-
-
-def interior_kernel(op_ref, v_ref, out_ref):
-    v = v_ref[0]
+    )(index, g, near, real, imag_a, imag_b, src)
+
+
+def interior_kernel(half_ref, op_ref, sets_ref, last_ref, out_ref, v_ref):
+    sets = [sets_ref.at[0, k] for k in range(2 * NB - 1)] + [last_ref.at[0]]
+    first = half_ref[0] == 0
+    n = last_ref.shape[3]
+    blk = block_of((n, 128))
+    for h in range(NH):
+        for z in range(NZ):
+            pieces = [r[z, h].astype(F32) for r in sets]
+            low = [jnp.where(first, pieces[b], pieces[NB + b]) for b in range(NB)]
+            high = [jnp.where(first, pieces[NB + b], pieces[b]) for b in range(NB)]
+            for y in range(NY):
+                total = jnp.zeros((n, 128), F32)
+                for b, piece in enumerate(low + high):
+                    total = jnp.where(blk == b, roll_blocks(piece, b - y), total)
+                v_ref[((y * NH + h) * NZ + z) * n : ((y * NH + h) * NZ + z + 1) * n] = total.astype(BF)
+    v = v_ref[...]
     d0 = jnp.dot(op_ref[0], v, preferred_element_type=F32)
     d1 = jnp.dot(op_ref[1], v, preferred_element_type=F32)
     out_ref[0] = d0 + turn(d1)
 
 
-def apply_interior(op, v):
+def apply_interior(half, op, sets, last):
     _, n, depth = op.shape
+    spec_of = lambda x: pl.BlockSpec((1, *x.shape[1:]), lambda f: (f,) + (0,) * (x.ndim - 1))
     return pl.pallas_call(
         interior_kernel,
         grid=(NY,),
-        in_specs=[
-            pl.BlockSpec((2, n, depth), lambda f: (0, 0, 0)),
-            pl.BlockSpec((1, depth, 128), lambda f: (f, 0, 0)),
-        ],
+        in_specs=[pl.BlockSpec(memory_space=pltpu.SMEM), pl.BlockSpec((2, n, depth), lambda f: (0, 0, 0))]
+        + [spec_of(sets), spec_of(last)],
         out_specs=pl.BlockSpec((1, n, 128), lambda f: (f, 0, 0)),
         out_shape=jax.ShapeDtypeStruct((NY, n, 128), F32),
+        scratch_shapes=[pltpu.VMEM((depth, 128), BF)],
         compiler_params=pltpu.CompilerParams(vmem_limit_bytes=24 * 2**20),
         name="apply_interior",
-    )(op, v)
+    )(half, op, sets, last)
 
 
 def spread(x, axis):
@@ -124,39 +153,56 @@
     s = lax.axis_index("slab")
     half = lax.axis_index("zh")
     rows = incident.shape[1]
-    op = green_next[0]
-    far = lax.ppermute(op, "zh", [(0, 1), (1, 0)])
+    real, imag = green_next[0, 0], green_next[0, 1]
+    imag_a, imag_b = imag[: rows // 2], imag[rows // 2 :]
+    across = [(0, 1), (1, 0)]
+    together = lax.optimization_barrier
+    far_real = lax.ppermute(real, "zh", across)
+    near = spread(green_next[0], "y")
+    far_real, near, imag_a, imag_b, incident, sources = together((far_real, near, imag_a, imag_b, incident, sources))
+    imag_a = lax.ppermute(imag_a, "zh", across)
+    far_real = spread(far_real, "y")
+    far_real, imag_a, imag_b, incident, sources = together((far_real, imag_a, imag_b, incident, sources))
+    imag_b = lax.ppermute(imag_b, "zh", across)
+    imag_a = spread(imag_a, "y")
     inc = lax.all_to_all(incident.astype(BF), "y", 0, 0, tiled=True)
+    inc = swap_blocks(inc, BF).reshape(NH, NB, rows, 128)
+    imag_a, imag_b, inc, sources = together((imag_a, imag_b, inc, sources))
+    imag_b = spread(imag_b, "y")
+    inc = lax.all_to_all(inc, "zh", 0, 0, tiled=True)
     src = lax.all_to_all(sources[0], "y", 0, 0, tiled=True)
-    near = spread(op, "y")
-    inc = swap_blocks(inc, BF).reshape(NH, NB, rows, 128)
     src = swap_blocks(src, F32).reshape(NH, NB, rows, 128)
-    inc = lax.all_to_all(inc, "zh", 0, 0, tiled=True)
     src = lax.all_to_all(src, "zh", 0, 0, tiled=True)
-    far = spread(far, "y")
     stored = jnp.zeros((NB + 2, NZ, NH, rows, 128), BF)
     kept = jnp.zeros((NB + 2, NH, rows, 128), F32)
     received = jnp.zeros((NH, rows, 128), BF)
     for c in range(NS + NB - 1):
         entering = jnp.where(s == 0, inc[:, min(c, NB - 1)], received)
         g = spread(entering, "zr")
+        if c == NS:
+            g, far_first = together((g, far_first))
         batch = c - s
         chosen = jnp.clip(batch, 0, NB - 1)
         index = jnp.stack([chosen, half]).astype(jnp.int32)
-        leaving, send = apply_next(index, g, near, far, src)
+        leaving, send = apply_next(index, g, near, far_real, imag_a, imag_b, src)
         if c < NS + NB - 2:
             pairs = [(a, a + 1) for a in range(NS - 1) if 0 <= c - a < NB]
             received = lax.ppermute(send, "slab", pairs)
         slot = jnp.clip(batch + 1, 0, NB + 1)
         stored = lax.dynamic_update_index_in_dim(stored, g, slot, 0)
         kept = lax.dynamic_update_index_in_dim(kept, leaving, slot, 0)
-    v = spread(stored[1 : NB + 1], "zh").reshape(NH * NB, NZ * NH * rows, 128)
+        if c == NS - 1:
+            first = stored[1]
+            far_first = lax.ppermute(first, "zh", across)
+    second = stored[2]
+    far_second = lax.ppermute(second, "zh", across)
+    sets = spread(jnp.stack([first, second, far_first]), "y")
     traces = lax.all_to_all(jnp.swapaxes(kept[1 : NB + 1], 0, 1), "zh", 0, 0, tiled=True)
+    far_second, sets, traces = together((far_second, sets, traces))
+    far_second = spread(far_second, "y")
     traces = swap_blocks(traces.reshape(NH * NB, rows, 128), F32)
     traces = lax.all_to_all(traces, "y", 0, 0, tiled=True)
-    v = swap_blocks(v, BF, lambda i: (i % NZ) * NH + i // NZ).reshape(NY * NZ * NH * rows, 128)
-    fronts = spread(v, "y")
-    interior = apply_interior(green_interior[0], fronts)
+    interior = apply_interior(half.astype(jnp.int32).reshape(1), green_interior[0], sets, far_second)
     return interior[None], traces[None]
 
 

time: 708 us -> 701 us (level)
  waiting for transfers between devices: 390 us -> 293 us
  local copies, waits for them, and re-layouts: 50.4 us -> 86.4 us
  starting transfers between devices: 106 us -> 128 us
  blocking collectives: 19.3 us -> 40 us
  other arithmetic: 2.49 us -> 19.6 us
  Pallas kernels: 128 us -> 120 us
    all_to_all x20 -> x22, waiting for transfers between devices: 207 us -> 91.8 us  [spread(): return lax.all_to_all(copies, axis, split_axis=0, concat_axis=0, tiled=True)]
    ppermute x1 -> x5, waiting for transfers between devices: 100 us -> 140 us  [the longest x1 53.7 us: local(): far_real = lax.ppermute(real, 'zh', across)]
    all_to_all x0 -> x2, blocking collectives: none -> 20.6 us  [the longest x1 10.9 us: local(): src = lax.all_to_all(sources[0], 'y', 0, 0, tiled=True)]
    all_to_all x20 -> x22, starting transfers between devices: 72.5 us -> 90.8 us  [spread(): return lax.all_to_all(copies, axis, split_axis=0, concat_axis=0, tiled=True)]
    dynamic_update_slice x17, local copies, waits for them, and re-layouts: 11.7 us -> 27.6 us  [local(): stored = lax.dynamic_update_index_in_dim(stored, g, slot, 0)]
    select_n x17, other arithmetic: 0.16 us -> 14.5 us  [local(): entering = jnp.where(s == 0, inc[:, min(c, NB - 1)], received)]
    unnamed x11 -> x75, local copies, waits for them, and re-layouts: 2.17 us -> 12.3 us
    ppermute x1 -> x5, starting transfers between devices: 2.74 us -> 12 us  [the longest x1 4.29 us: local(): far_real = lax.ppermute(real, 'zh', across)]
  transfers between devices with their start and end apart: 42 -> 46, of which waited for: 28 -> 30; matrix products, arithmetic and copies ran while one was open for 4% -> 8% of each run, Pallas kernels for 2% -> 1%
where the time goes in v3:
time: 701 us; the launch traced here: 689 us
  waiting for transfers between devices  293 us (42%)
  starting transfers between devices  128 us (18%)
  Pallas kernels  120 us (17%)
  local copies, waits for them, and re-layouts  86.4 us (12%)
  blocking collectives  40 us (6%)
  other arithmetic  19.6 us (3%)
    pallas_call x17, Pallas kernels, apply_next(): pl.pallas_call(step_kernel, in_specs=[pl.BlockSpec(memory_space=pltpu.SME...  109 us
    all_to_all x22, waiting for transfers between devices, spread(): return lax.all_to_all(copies, axis, split_axis=0, concat_axis=0, tiled=True)  91.8 us
    all_to_all x22, starting transfers between devices, spread(): return lax.all_to_all(copies, axis, split_axis=0, concat_axis=0, tiled=True)  90.8 us
    ppermute x1, waiting for transfers between devices, local(): far_real = lax.ppermute(real, 'zh', across)  53.7 us
    ppermute x16, waiting for transfers between devices, local(): received = lax.ppermute(send, 'slab', pairs)  39.9 us
    dynamic_update_slice x17, local copies, waits for them, and re-layouts, local(): stored = lax.dynamic_update_index_in_dim(stored, g, slot, 0)  27.6 us
    ppermute x1, waiting for transfers between devices, local(): imag_a = lax.ppermute(imag_a, 'zh', across)  26.3 us
    broadcast_in_dim x23, local copies, waits for them, and re-layouts, spread(): copies = jnp.broadcast_to(x, (lax.axis_size(axis), *x.shape))  24.3 us
  transfers between devices with their start and end apart: 46, of which 30 were waited for; matrix products, arithmetic and copies ran while one was open for 8% of the time, Pallas kernels for 1%

profile of v3, /device:TPU:262, one launch (start us, length us, event | category | flops | bytes accessed | tf_op | source)
XLA Modules:
  0.0 689.1 jit_solution(8448764292169206268)
XLA Ops:
  0.6 4.1 broadcast_in_dim.189
  4.7 5.1 all-to-all-start
  9.9 4.3 collective-permute-start
  14.9 53.7 %collective-permute-done = bf16[96,3072]{1,0:T(8,128)(2,1)S(1)} collective-permute-done((bf16[96,3072]{1,0:T(8,128)(2,1)S(1)}, bf16[96,3072]{1,0:T(8,128)(2,1)S(1)}, u32[]{:S(2)}, u32[]{:S(2)}) %collective-permute-start) | collective-permute-done | bytes 589856 | tf_op jit(solution)/shard_map/ppermute | solution.py:160
  70.4 4.6 all-to-all-start.1
  77.0 26.3 %collective-permute-done.1 = bf16[48,3072]{1,0:T(8,128)(2,1)S(1)} collective-permute-done((bf16[48,3072]{1,0:T(8,128)(2,1)S(1)}, bf16[48,3072]{1,0:T(8,128)(2,1)S(1)}, u32[]{:S(2)}, u32[]{:S(2)}) %collective-permute-start.1) | collective-permute-done | bytes 294944 | tf_op jit(solution)/shard_map/ppermute | solution.py:163
  103.9 9.5 %all_to_all.145.src_ref = bf16[4,96,128]{2,1,0:T(8,128)(2,1)} all-to-all(bf16[4,96,128]{2,1,0:T(8,128)(2,1)S(1)} %convert_element_type.3), channel_id=1, replica_groups=mesh['slab'=16,'y'=4,'zh'=2,'zr'=4] {'y'}, dimensions={0} | all-to-all | bytes 196608 | tf_op jit(solution)/shard_map/all_to_all | solution.py:168
  121.7 22.2 %collective-permute-done.2 = bf16[48,3072]{1,0:T(8,128)(2,1)} collective-permute-done((bf16[48,3072]{1,0:T(8,128)(2,1)}, bf16[48,3072]{1,0:T(8,128)(2,1)}, u32[]{:S(2)}, u32[]{:S(2)}) %collective-permute-start.2) | collective-permute-done | bytes 294944 | tf_op jit(solution)/shard_map/ppermute | solution.py:166
  143.9 10.9 %all_to_all.146.src_ref = f32[4,96,128]{2,1,0:T(8,128)} all-to-all(f32[4,96,128]{2,1,0:T(8,128)} %bitcast.186), channel_id=1, replica_groups=mesh['slab'=16,'y'=4,'zh'=2,'zr'=4] {'y'}, dimensions={0} | all-to-all | bytes 393216 | tf_op jit(solution)/shard_map/all_to_all | solution.py:173
  160.6 6.5 all-to-all-done.4
  167.0 4.1 all-to-all-start.8
  172.6 7.4 %all-to-all-done.8.src_ref = f32[2,2,96,128]{3,2,1,0:T(8,128)} async-done(((f32[2,2,96,128]{3,2,1,0:T(8,128)}), f32[2,2,96,128]{3,2,1,0:T(8,128)}, u32[]{:S(2)}, u32[]{:S(2)}) %all-to-all-start.8) | async-done | bytes 196640 | tf_op jit(solution)/shard_map/all_to_all | solution.py:175
  180.8 9.9 %all_to_all.147.g_ref = bf16[4,2,96,128]{3,2,1,0:T(8,128)(2,1)} all-to-all(bf16[4,2,96,128]{3,2,1,0:T(8,128)(2,1)S(1)} %broadcast_in_dim.193), channel_id=1, replica_groups=mesh['slab'=16,'y'=4,'zh'=2,'zr'=4] {'zr'}, dimensions={0} | all-to-all | bytes 393216 | tf_op jit(solution)/shard_map/all_to_all | solution.py:149
  192.8 4.3 all-to-all-start.6
  197.2 13.1 %all-to-all-done.6.imag_b_hbm = bf16[4,48,3072]{2,1,0:T(8,128)(2,1)} async-done(((bf16[4,48,3072]{2,1,0:T(8,128)(2,1)}), bf16[4,48,3072]{2,1,0:T(8,128)(2,1)}, u32[]{:S(2)}, u32[]{:S(2)}) %all-to-all-start.6) | async-done | bytes 1179680 | tf_op jit(solution)/shard_map/all_to_all | solution.py:149
  211.3 6.3 apply_next.17
  220.4 4.0 all-to-all-start.9
  224.4 6.2 all-to-all-done.9.g_ref
  230.7 6.4 apply_next.18
  239.9 4.0 all-to-all-start.10
  243.9 6.2 all-to-all-done.10.g_ref
  250.2 6.4 apply_next.19
  259.4 4.2 all-to-all-start.11
  263.6 6.2 all-to-all-done.11.g_ref
  269.8 6.4 apply_next.20
  279.0 4.0 all-to-all-start.12
  283.1 6.2 all-to-all-done.12.g_ref
  289.3 6.4 apply_next.21
  298.5 4.0 all-to-all-start.13
  302.6 6.2 all-to-all-done.13.g_ref
  308.8 6.4 apply_next.22
  318.0 4.0 all-to-all-start.14
  322.1 6.2 all-to-all-done.14.g_ref
  328.3 6.4 apply_next.23
  337.5 4.2 all-to-all-start.15
  348.0 7.0 %apply_next.24 = (f32[2,96,128]{2,1,0:T(8,128)S(1)}, bf16[2,96,128]{2,1,0:T(8,128)(2,1)}) custom-call(s32[2]{0:T(128)S(1)} %pad_add_fusion.7.idx_ref, bf16[4,2,96,128]{3,2,1,0:T(8,128)(2,1)} %all-to-all-done.15.g_ref, bf16[4,2,96,3072]{3,2,1,0:T(8,128)(2,1)} %all-to-all-done.near_hbm, bf16[4,96,3072]{2,1,0:T(8,128)(2,1)S(1)} %all-to-all-done.1.real_hbm, ...), custom_call_target="tpu_custom_call" | custom-call | flops 2415919104 | bytes 9437184 | tf_op jit(solution)/shard_map/apply_next/pallas_call | solution.py:98
  359.1 4.0 all-to-all-start.16
  370.1 6.4 apply_next.25
  379.5 4.0 all-to-all-start.17
  390.5 6.4 apply_next.26
  399.8 4.0 all-to-all-start.18
  410.7 6.4 apply_next.27
  420.0 4.4 all-to-all-start.19
  431.4 6.4 apply_next.28
  440.6 4.0 all-to-all-start.20
  451.7 6.4 apply_next.29
  461.0 4.9 all-to-all-start.21
  470.7 4.0 all-to-all-done.21.g_ref
  474.7 6.4 apply_next.30
  483.1 26.6 %collective-permute-done.16 = bf16[2,96,128]{2,1,0:T(8,128)(2,1)S(1)} collective-permute-done((bf16[2,96,128]{2,1,0:T(8,128)(2,1)S(1)}, bf16[2,96,128]{2,1,0:T(8,128)(2,1)S(1)}, u32[]{:S(2)}, u32[]{:S(2)}) %collective-permute-start.16) | collective-permute-done | bytes 49184 | tf_op jit(solution)/shard_map/ppermute | solution.py:190
  511.2 4.4 all-to-all-start.22
  521.9 6.4 apply_next.31
  530.9 13.1 %collective-permute-done.17 = bf16[2,96,128]{2,1,0:T(8,128)(2,1)S(1)} collective-permute-done((bf16[2,96,128]{2,1,0:T(8,128)(2,1)S(1)}, bf16[2,96,128]{2,1,0:T(8,128)(2,1)S(1)}, u32[]{:S(2)}, u32[]{:S(2)}) %collective-permute-start.17) | collective-permute-done | bytes 49184 | tf_op jit(solution)/shard_map/ppermute | solution.py:190
  545.5 4.2 all-to-all-start.23
  556.0 6.4 apply_next.32
  566.1 4.0 all-to-all-start.24
  576.8 22.2 %collective-permute-done.19 = bf16[4,2,96,128]{3,2,1,0:T(8,128)(2,1)} collective-permute-done((bf16[4,2,96,128]{3,2,1,0:T(8,128)(2,1)S(1)}, bf16[4,2,96,128]{3,2,1,0:T(8,128)(2,1)}, u32[]{:S(2)}, u32[]{:S(2)}) %collective-permute-start.19) | collective-permute-done | bytes 196640 | tf_op jit(solution)/shard_map/ppermute | solution.py:196
  599.1 7.0 %apply_next.33 = (f32[2,96,128]{2,1,0:T(8,128)S(1)}, bf16[2,96,128]{2,1,0:T(8,128)(2,1)}) custom-call(s32[2]{0:T(128)S(1)} %pad_add_fusion.16.idx_ref, bf16[4,2,96,128]{3,2,1,0:T(8,128)(2,1)} %all-to-all-done.24.g_ref, bf16[4,2,96,3072]{3,2,1,0:T(8,128)(2,1)} %all-to-all-done.near_hbm, bf16[4,96,3072]{2,1,0:T(8,128)(2,1)S(1)} %all-to-all-done.1.real_hbm, ...), custom_call_target="tpu_custom_call" | custom-call | flops 2415919104 | bytes 9437184 | tf_op jit(solution)/shard_map/apply_next/pallas_call | solution.py:98
  613.9 7.0 %all-to-all-done.26 = f32[2,2,96,128]{3,2,1,0:T(8,128)S(1)} async-done(((f32[2,2,96,128]{3,2,1,0:T(8,128)}), f32[2,2,96,128]{3,2,1,0:T(8,128)S(1)}, u32[]{:S(2)}, u32[]{:S(2)}) %all-to-all-start.26) | async-done | bytes 196640 | tf_op jit(solution)/shard_map/all_to_all | solution.py:200
  628.5 16.1 %collective-permute-done.20 = bf16[4,2,96,128]{3,2,1,0:T(8,128)(2,1)S(1)} collective-permute-done((bf16[4,2,96,128]{3,2,1,0:T(8,128)(2,1)S(1)}, bf16[4,2,96,128]{3,2,1,0:T(8,128)(2,1)S(1)}, u32[]{:S(2)}, u32[]{:S(2)}) %collective-permute-start.20) | collective-permute-done | bytes 196640 | tf_op jit(solution)/shard_map/ppermute | solution.py:198
  644.5 10.8 %all-to-all-done.25.sets_ref = bf16[4,3,4,2,96,128]{5,4,3,2,1,0:T(8,128)(2,1)S(1)} async-done(((bf16[4,3,4,2,96,128]{5,4,3,2,1,0:T(8,128)(2,1)}), bf16[4,3,4,2,96,128]{5,4,3,2,1,0:T(8,128)(2,1)S(1)}, u32[]{:S(2)}, u32[]{:S(2)}) %all-to-all-start.25) | async-done | bytes 2359328 | tf_op jit(solution)/shard_map/all_to_all | solution.py:149
  657.1 9.7 %all_to_all.148 = f32[4,96,128]{2,1,0:T(8,128)S(1)} all-to-all(f32[4,96,128]{2,1,0:T(8,128)} %swap_blocks.5), channel_id=1, replica_groups=mesh['slab'=16,'y'=4,'zh'=2,'zr'=4] {'y'}, dimensions={0} | all-to-all | bytes 393216 | tf_op jit(solution)/shard_map/all_to_all | solution.py:204
  671.3 9.8 %all-to-all-done.27.last_ref = bf16[4,4,2,96,128]{4,3,2,1,0:T(8,128)(2,1)S(1)} async-done(((bf16[4,4,2,96,128]{4,3,2,1,0:T(8,128)(2,1)}), bf16[4,4,2,96,128]{4,3,2,1,0:T(8,128)(2,1)S(1)}, u32[]{:S(2)}, u32[]{:S(2)}) %all-to-all-start.27) | async-done | bytes 786464 | tf_op jit(solution)/shard_map/all_to_all | solution.py:149
  682.6 5.6 apply_interior.1
  (228 shorter events, 163.6 us)
Async XLA Ops:
  4.7 5.1 copy-start.31
  4.7 63.9 %all-to-all-start = ((bf16[4,2,96,3072]{3,2,1,0:T(8,128)(2,1)}), bf16[4,2,96,3072]{3,2,1,0:T(8,128)(2,1)}, u32[]{:S(2)}, u32[]{:S(2)}) async-start(bf16[4,2,96,3072]{3,2,1,0:T(8,128)(2,1)} %broadcast_in_dim.189), calls=%async_computation | async-start | bytes 9437184 | tf_op jit(solution)/shard_map/all_to_all | solution.py:149
  9.9 58.8 %collective-permute-start = (bf16[96,3072]{1,0:T(8,128)(2,1)S(1)}, bf16[96,3072]{1,0:T(8,128)(2,1)S(1)}, u32[]{:S(2)}, u32[]{:S(2)}) collective-permute-start(bf16[96,3072]{1,0:T(8,128)(2,1)S(1)} %slice_bitcast_fusion), channel_id=1, source_target_pairs={{0,4},{4,0},{1,5},{5,1},{2,6},{6,2},{3,7},{7,3},{8,12},{12,8},{9,1... | collective-permute-start | bytes 1769480 | tf_op jit(solution)/shard_map/ppermute | solution.py:160
  70.4 33.4 %copy-start.36 = (f32[4,96,128]{2,1,0:T(8,128)S(1)}, f32[4,96,128]{2,1,0:T(8,128)}, u32[]{:S(2)}) copy-start(f32[4,96,128]{2,1,0:T(8,128)} %param.4) | copy-start | bytes 589828
  70.4 33.4 %all-to-all-start.1 = ((bf16[4,96,3072]{2,1,0:T(8,128)(2,1)}), bf16[4,96,3072]{2,1,0:T(8,128)(2,1)S(1)}, u32[]{:S(2)}, u32[]{:S(2)}) async-start(bf16[4,96,3072]{2,1,0:T(8,128)(2,1)} %broadcast_in_dim.190), calls=%async_computation.1 | async-start | bytes 4718592 | tf_op jit(solution)/shard_map/all_to_all | solution.py:149
  75.0 28.2 %collective-permute-start.1 = (bf16[48,3072]{1,0:T(8,128)(2,1)S(1)}, bf16[48,3072]{1,0:T(8,128)(2,1)S(1)}, u32[]{:S(2)}, u32[]{:S(2)}) collective-permute-start(bf16[48,3072]{1,0:T(8,128)(2,1)S(1)} %get-tuple-element.56), channel_id=1, source_target_pairs={{0,4},{4,0},{1,5},{5,1},{2,6},{6,2},{3,7},{7,3},{8,12},{12,8},{9,1... | collective-permute-start | bytes 884744 | tf_op jit(solution)/shard_map/ppermute | solution.py:163
  114.6 29.3 %all-to-all-start.2 = ((bf16[4,48,3072]{2,1,0:T(8,128)(2,1)}), bf16[4,48,3072]{2,1,0:T(8,128)(2,1)S(1)}, u32[]{:S(2)}, u32[]{:S(2)}) async-start(bf16[4,48,3072]{2,1,0:T(8,128)(2,1)} %broadcast_in_dim.191), calls=%async_computation.2 | async-start | bytes 2359296 | tf_op jit(solution)/shard_map/all_to_all | solution.py:149
  118.1 25.8 %collective-permute-start.2 = (bf16[48,3072]{1,0:T(8,128)(2,1)}, bf16[48,3072]{1,0:T(8,128)(2,1)}, u32[]{:S(2)}, u32[]{:S(2)}) collective-permute-start(bf16[48,3072]{1,0:T(8,128)(2,1)} %get-tuple-element.61), channel_id=1, source_target_pairs={{0,4},{4,0},{1,5},{5,1},{2,6},{6,2},{3,7},{7,3},{8,12},{12,8},{9,1... | collective-permute-start | bytes 884744 | tf_op jit(solution)/shard_map/ppermute | solution.py:166
  154.8 12.3 %all-to-all-start.4 = ((bf16[2,2,96,128]{3,2,1,0:T(8,128)(2,1)}), bf16[2,2,96,128]{3,2,1,0:T(8,128)(2,1)}, u32[]{:S(2)}, u32[]{:S(2)}) async-start(bf16[2,2,96,128]{3,2,1,0:T(8,128)(2,1)} %bitcast.184), calls=%async_computation.4 | async-start | bytes 196608 | tf_op jit(solution)/shard_map/all_to_all | solution.py:172
  167.0 12.9 %all-to-all-start.8 = ((f32[2,2,96,128]{3,2,1,0:T(8,128)}), f32[2,2,96,128]{3,2,1,0:T(8,128)}, u32[]{:S(2)}, u32[]{:S(2)}) async-start(f32[2,2,96,128]{3,2,1,0:T(8,128)} %bitcast.182), calls=%async_computation.8 | async-start | bytes 393216 | tf_op jit(solution)/shard_map/all_to_all | solution.py:175
  192.8 17.5 %all-to-all-start.6 = ((bf16[4,48,3072]{2,1,0:T(8,128)(2,1)}), bf16[4,48,3072]{2,1,0:T(8,128)(2,1)}, u32[]{:S(2)}, u32[]{:S(2)}) async-start(bf16[4,48,3072]{2,1,0:T(8,128)(2,1)} %broadcast_in_dim.195), calls=%async_computation.6 | async-start | bytes 2359296 | tf_op jit(solution)/shard_map/all_to_all | solution.py:149
  218.2 0.7 collective-permute-start.3
  220.4 10.3 %all-to-all-start.9 = ((bf16[4,2,96,128]{3,2,1,0:T(8,128)(2,1)}), bf16[4,2,96,128]{3,2,1,0:T(8,128)(2,1)}, u32[]{:S(2)}, u32[]{:S(2)}) async-start(bf16[4,2,96,128]{3,2,1,0:T(8,128)(2,1)} %broadcast_in_dim.196), calls=%async_computation.9 | async-start | bytes 393216 | tf_op jit(solution)/shard_map/all_to_all | solution.py:149
  237.7 0.7 collective-permute-start.4
  239.9 10.3 %all-to-all-start.10 = ((bf16[4,2,96,128]{3,2,1,0:T(8,128)(2,1)}), bf16[4,2,96,128]{3,2,1,0:T(8,128)(2,1)}, u32[]{:S(2)}, u32[]{:S(2)}) async-start(bf16[4,2,96,128]{3,2,1,0:T(8,128)(2,1)} %broadcast_in_dim.198), calls=%async_computation.10 | async-start | bytes 393216 | tf_op jit(solution)/shard_map/all_to_all | solution.py:149
  257.2 0.7 collective-permute-start.5
  259.4 10.5 %all-to-all-start.11 = ((bf16[4,2,96,128]{3,2,1,0:T(8,128)(2,1)}), bf16[4,2,96,128]{3,2,1,0:T(8,128)(2,1)}, u32[]{:S(2)}, u32[]{:S(2)}) async-start(bf16[4,2,96,128]{3,2,1,0:T(8,128)(2,1)} %broadcast_in_dim.200), calls=%async_computation.11 | async-start | bytes 393216 | tf_op jit(solution)/shard_map/all_to_all | solution.py:149
  276.8 0.7 collective-permute-start.6
  279.0 10.3 %all-to-all-start.12 = ((bf16[4,2,96,128]{3,2,1,0:T(8,128)(2,1)}), bf16[4,2,96,128]{3,2,1,0:T(8,128)(2,1)}, u32[]{:S(2)}, u32[]{:S(2)}) async-start(bf16[4,2,96,128]{3,2,1,0:T(8,128)(2,1)} %broadcast_in_dim.202), calls=%async_computation.12 | async-start | bytes 393216 | tf_op jit(solution)/shard_map/all_to_all | solution.py:149
  296.3 0.7 collective-permute-start.7
  298.5 10.3 %all-to-all-start.13 = ((bf16[4,2,96,128]{3,2,1,0:T(8,128)(2,1)}), bf16[4,2,96,128]{3,2,1,0:T(8,128)(2,1)}, u32[]{:S(2)}, u32[]{:S(2)}) async-start(bf16[4,2,96,128]{3,2,1,0:T(8,128)(2,1)} %broadcast_in_dim.204), calls=%async_computation.13 | async-start | bytes 393216 | tf_op jit(solution)/shard_map/all_to_all | solution.py:149
  315.8 0.7 collective-permute-start.8
  318.0 10.3 %all-to-all-start.14 = ((bf16[4,2,96,128]{3,2,1,0:T(8,128)(2,1)}), bf16[4,2,96,128]{3,2,1,0:T(8,128)(2,1)}, u32[]{:S(2)}, u32[]{:S(2)}) async-start(bf16[4,2,96,128]{3,2,1,0:T(8,128)(2,1)} %broadcast_in_dim.206), calls=%async_computation.14 | async-start | bytes 393216 | tf_op jit(solution)/shard_map/all_to_all | solution.py:149
  335.3 0.7 collective-permute-start.9
  337.5 10.5 %all-to-all-start.15 = ((bf16[4,2,96,128]{3,2,1,0:T(8,128)(2,1)}), bf16[4,2,96,128]{3,2,1,0:T(8,128)(2,1)}, u32[]{:S(2)}, u32[]{:S(2)}) async-start(bf16[4,2,96,128]{3,2,1,0:T(8,128)(2,1)} %broadcast_in_dim.208), calls=%async_computation.15 | async-start | bytes 393216 | tf_op jit(solution)/shard_map/all_to_all | solution.py:149
  355.6 1.9 collective-permute-start.10
  359.1 10.3 %all-to-all-start.16 = ((bf16[4,2,96,128]{3,2,1,0:T(8,128)(2,1)}), bf16[4,2,96,128]{3,2,1,0:T(8,128)(2,1)}, u32[]{:S(2)}, u32[]{:S(2)}) async-start(bf16[4,2,96,128]{3,2,1,0:T(8,128)(2,1)} %broadcast_in_dim.210), calls=%async_computation.16 | async-start | bytes 393216 | tf_op jit(solution)/shard_map/all_to_all | solution.py:149
  370.0 7.1 %copy-start.3 = (f32[2,96,128]{2,1,0:T(8,128)S(1)}, f32[2,96,128]{2,1,0:T(8,128)}, u32[]{:S(2)}) copy-start(f32[2,96,128]{2,1,0:T(8,128)} %copy-done.2) | copy-start | bytes 294916
  376.5 0.8 collective-permute-start.11
  379.5 10.3 %all-to-all-start.17 = ((bf16[4,2,96,128]{3,2,1,0:T(8,128)(2,1)}), bf16[4,2,96,128]{3,2,1,0:T(8,128)(2,1)}, u32[]{:S(2)}, u32[]{:S(2)}) async-start(bf16[4,2,96,128]{3,2,1,0:T(8,128)(2,1)} %broadcast_in_dim.212), calls=%async_computation.17 | async-start | bytes 393216 | tf_op jit(solution)/shard_map/all_to_all | solution.py:149
  390.5 7.1 %copy-start.6 = (f32[2,96,128]{2,1,0:T(8,128)S(1)}, f32[2,96,128]{2,1,0:T(8,128)}, u32[]{:S(2)}) copy-start(f32[2,96,128]{2,1,0:T(8,128)} %copy-done.5) | copy-start | bytes 294916
  396.9 1.3 copy-start.16
  396.9 1.3 collective-permute-start.12
  399.8 10.3 %all-to-all-start.18 = ((bf16[4,2,96,128]{3,2,1,0:T(8,128)(2,1)}), bf16[4,2,96,128]{3,2,1,0:T(8,128)(2,1)}, u32[]{:S(2)}, u32[]{:S(2)}) async-start(bf16[4,2,96,128]{3,2,1,0:T(8,128)(2,1)} %broadcast_in_dim.214), calls=%async_computation.18 | async-start | bytes 393216 | tf_op jit(solution)/shard_map/all_to_all | solution.py:149
  410.7 7.1 %copy-start.9 = (f32[2,96,128]{2,1,0:T(8,128)S(1)}, f32[2,96,128]{2,1,0:T(8,128)}, u32[]{:S(2)}) copy-start(f32[2,96,128]{2,1,0:T(8,128)} %copy-done.8) | copy-start | bytes 294916
  417.1 1.3 collective-permute-start.13
  420.0 10.7 %all-to-all-start.19 = ((bf16[4,2,96,128]{3,2,1,0:T(8,128)(2,1)}), bf16[4,2,96,128]{3,2,1,0:T(8,128)(2,1)}, u32[]{:S(2)}, u32[]{:S(2)}) async-start(bf16[4,2,96,128]{3,2,1,0:T(8,128)(2,1)} %broadcast_in_dim.216), calls=%async_computation.19 | async-start | bytes 393216 | tf_op jit(solution)/shard_map/all_to_all | solution.py:149
  431.4 7.1 %copy-start.12 = (f32[2,96,128]{2,1,0:T(8,128)S(1)}, f32[2,96,128]{2,1,0:T(8,128)}, u32[]{:S(2)}) copy-start(f32[2,96,128]{2,1,0:T(8,128)} %copy-done.11) | copy-start | bytes 294916
  437.8 1.3 collective-permute-start.14
  440.6 10.4 %all-to-all-start.20 = ((bf16[4,2,96,128]{3,2,1,0:T(8,128)(2,1)}), bf16[4,2,96,128]{3,2,1,0:T(8,128)(2,1)}, u32[]{:S(2)}, u32[]{:S(2)}) async-start(bf16[4,2,96,128]{3,2,1,0:T(8,128)(2,1)} %broadcast_in_dim.218), calls=%async_computation.20 | async-start | bytes 393216 | tf_op jit(solution)/shard_map/all_to_all | solution.py:149
  451.7 7.1 %copy-start.15 = (f32[2,96,128]{2,1,0:T(8,128)S(1)}, f32[2,96,128]{2,1,0:T(8,128)}, u32[]{:S(2)}) copy-start(f32[2,96,128]{2,1,0:T(8,128)} %copy-done.14) | copy-start | bytes 294916
  458.1 1.3 collective-permute-start.15
  461.0 13.7 %all-to-all-start.21 = ((bf16[4,2,96,128]{3,2,1,0:T(8,128)(2,1)}), bf16[4,2,96,128]{3,2,1,0:T(8,128)(2,1)}, u32[]{:S(2)}, u32[]{:S(2)}) async-start(bf16[4,2,96,128]{3,2,1,0:T(8,128)(2,1)} %broadcast_in_dim.220), calls=%async_computation.21 | async-start | bytes 393216 | tf_op jit(solution)/shard_map/all_to_all | solution.py:149
  474.7 7.7 %copy-start.18 = (f32[2,96,128]{2,1,0:T(8,128)S(1)}, f32[2,96,128]{2,1,0:T(8,128)}, u32[]{:S(2)}) copy-start(f32[2,96,128]{2,1,0:T(8,128)} %copy-done.17) | copy-start | bytes 294916
  481.1 2.0 copy-start.22
  481.1 28.6 %collective-permute-start.16 = (bf16[2,96,128]{2,1,0:T(8,128)(2,1)S(1)}, bf16[2,96,128]{2,1,0:T(8,128)(2,1)S(1)}, u32[]{:S(2)}, u32[]{:S(2)}) collective-permute-start(bf16[2,96,128]{2,1,0:T(8,128)(2,1)S(1)} %get-tuple-element.83), channel_id=1, source_target_pairs={{384,416},{416,448},{385,417},{417,449},{386,418},{418,450},{387,4... | collective-permute-start | bytes 147464 | tf_op jit(solution)/shard_map/ppermute | solution.py:190
  511.2 10.7 %all-to-all-start.22 = ((bf16[4,2,96,128]{3,2,1,0:T(8,128)(2,1)}), bf16[4,2,96,128]{3,2,1,0:T(8,128)(2,1)}, u32[]{:S(2)}, u32[]{:S(2)}) async-start(bf16[4,2,96,128]{3,2,1,0:T(8,128)(2,1)} %broadcast_in_dim.222), calls=%async_computation.22 | async-start | bytes 393216 | tf_op jit(solution)/shard_map/all_to_all | solution.py:149
  521.9 8.3 %copy-start.21 = (f32[2,96,128]{2,1,0:T(8,128)S(1)}, f32[2,96,128]{2,1,0:T(8,128)}, u32[]{:S(2)}) copy-start(f32[2,96,128]{2,1,0:T(8,128)} %copy-done.20) | copy-start | bytes 294916
  528.3 2.6 copy-start.23
  528.3 15.7 %collective-permute-start.17 = (bf16[2,96,128]{2,1,0:T(8,128)(2,1)S(1)}, bf16[2,96,128]{2,1,0:T(8,128)(2,1)S(1)}, u32[]{:S(2)}, u32[]{:S(2)}) collective-permute-start(bf16[2,96,128]{2,1,0:T(8,128)(2,1)S(1)} %get-tuple-element.84), channel_id=1, source_target_pairs={{416,448},{448,480},{417,449},{449,481},{418,450},{450,482},{419,4... | collective-permute-start | bytes 147464 | tf_op jit(solution)/shard_map/ppermute | solution.py:190
  545.5 10.5 %all-to-all-start.23 = ((bf16[4,2,96,128]{3,2,1,0:T(8,128)(2,1)}), bf16[4,2,96,128]{3,2,1,0:T(8,128)(2,1)}, u32[]{:S(2)}, u32[]{:S(2)}) async-start(bf16[4,2,96,128]{3,2,1,0:T(8,128)(2,1)} %broadcast_in_dim.224), calls=%async_computation.23 | async-start | bytes 393216 | tf_op jit(solution)/shard_map/all_to_all | solution.py:149
  556.0 7.7 %copy-start.24 = (f32[2,96,128]{2,1,0:T(8,128)S(1)}, f32[2,96,128]{2,1,0:T(8,128)}, u32[]{:S(2)}) copy-start(f32[2,96,128]{2,1,0:T(8,128)} %copy-done.23) | copy-start | bytes 294916
  562.4 2.0 copy-start.25
  562.4 2.2 collective-permute-start.18
  566.1 33.0 %all-to-all-start.24 = ((bf16[4,2,96,128]{3,2,1,0:T(8,128)(2,1)}), bf16[4,2,96,128]{3,2,1,0:T(8,128)(2,1)}, u32[]{:S(2)}, u32[]{:S(2)}) async-start(bf16[4,2,96,128]{3,2,1,0:T(8,128)(2,1)} %broadcast_in_dim.226), calls=%async_computation.24 | async-start | bytes 393216 | tf_op jit(solution)/shard_map/all_to_all | solution.py:149
  573.4 25.7 %collective-permute-start.19 = (bf16[4,2,96,128]{3,2,1,0:T(8,128)(2,1)S(1)}, bf16[4,2,96,128]{3,2,1,0:T(8,128)(2,1)}, u32[]{:S(2)}, u32[]{:S(2)}) collective-permute-start(bf16[4,2,96,128]{3,2,1,0:T(8,128)(2,1)S(1)} %get-tuple-element.111), channel_id=1, source_target_pairs={{0,4},{4,0},{1,5},{5,1},{2,6},{6,2},{3,7},{7,3},{8,12},{12,8},{9,1... | collective-permute-start | bytes 589832 | tf_op jit(solution)/shard_map/ppermute | solution.py:196
  599.1 7.0 %copy-start.33 = (f32[4,2,96,128]{3,2,0,1:T(8,128)S(1)}, f32[4,2,96,128]{3,2,0,1:T(8,128)}, u32[]{:S(2)}) copy-start(f32[4,2,96,128]{3,2,0,1:T(8,128)} %bitcast_dynamic-update-slice_fusion.18) | copy-start | bytes 1179652
  606.1 6.8 copy-start.34
  606.8 14.1 %all-to-all-start.26 = ((f32[2,2,96,128]{3,2,1,0:T(8,128)}), f32[2,2,96,128]{3,2,1,0:T(8,128)S(1)}, u32[]{:S(2)}, u32[]{:S(2)}) async-start(f32[2,2,96,128]{3,2,1,0:T(8,128)} %slice_bitcast_fusion.3), calls=%async_computation.26 | async-start | bytes 393216 | tf_op jit(solution)/shard_map/all_to_all | solution.py:200
  620.9 2.0 copy-start.35
  622.9 32.4 %all-to-all-start.25 = ((bf16[4,3,4,2,96,128]{5,4,3,2,1,0:T(8,128)(2,1)}), bf16[4,3,4,2,96,128]{5,4,3,2,1,0:T(8,128)(2,1)S(1)}, u32[]{:S(2)}, u32[]{:S(2)}) async-start(bf16[4,3,4,2,96,128]{5,4,3,2,1,0:T(8,128)(2,1)} %broadcast_in_dim.228), calls=%async_computation.25 | async-start | bytes 4718592 | tf_op jit(solution)/shard_map/all_to_all | solution.py:149
  626.5 18.0 %collective-permute-start.20 = (bf16[4,2,96,128]{3,2,1,0:T(8,128)(2,1)S(1)}, bf16[4,2,96,128]{3,2,1,0:T(8,128)(2,1)S(1)}, u32[]{:S(2)}, u32[]{:S(2)}) collective-permute-start(bf16[4,2,96,128]{3,2,1,0:T(8,128)(2,1)S(1)} %get-tuple-element.113), channel_id=1, source_target_pairs={{0,4},{4,0},{1,5},{5,1},{2,6},{6,2},{3,7},{7,3},{8,12},{12,8},{9,1... | collective-permute-start | bytes 589832 | tf_op jit(solution)/shard_map/ppermute | solution.py:198
  667.8 13.3 %all-to-all-start.27 = ((bf16[4,4,2,96,128]{4,3,2,1,0:T(8,128)(2,1)}), bf16[4,4,2,96,128]{4,3,2,1,0:T(8,128)(2,1)S(1)}, u32[]{:S(2)}, u32[]{:S(2)}) async-start(bf16[4,4,2,96,128]{4,3,2,1,0:T(8,128)(2,1)} %broadcast_in_dim.247), calls=%async_computation.27 | async-start | bytes 1572864 | tf_op jit(solution)/shard_map/all_to_all | solution.py:149
  681.1 1.5 copy-start
  (19 other events, 14.9 us)

commit v4 on v1

v4 whole, which is shorter than its diff:
```python
import jax
import jax.numpy as jnp
from jax import lax
from jax.experimental import pallas as pl
from jax.experimental.pallas import tpu as pltpu
from jax.sharding import Mesh, PartitionSpec as P

NB = 4
NY = 4
NZ = 8
NS = 16
BF = jnp.bfloat16
F32 = jnp.float32


def block_of(shape):
    lane = lax.broadcasted_iota(jnp.int32, shape, len(shape) - 1)
    return (lane // 16) % 4


def roll_blocks(x, k):
    k = (16 * k) % 128
    return pltpu.roll(x, k, x.ndim - 1) if k else x


def turn(x):
    lane = lax.broadcasted_iota(jnp.int32, x.shape, x.ndim - 1)
    swapped = pltpu.roll(x, 64, x.ndim - 1)
    return jnp.where(lane < 64, -swapped, swapped)


def pack_kernel(src_ref, out_ref):
    blk = block_of(src_ref.shape[1:])
    for b in range(NB):
        total = jnp.zeros(src_ref.shape[1:], F32)
        for y in range(NY):
            total = jnp.where(blk == y, roll_blocks(src_ref[y].astype(F32), y - b), total)
        out_ref[b] = total.astype(out_ref.dtype)


def swap_blocks(x, dtype):
    n, rows, lanes = x.shape
    step = 96
    return pl.pallas_call(
        pack_kernel,
        grid=(rows // step,),
        in_specs=[pl.BlockSpec((n, step, lanes), lambda i: (0, i, 0))],
        out_specs=pl.BlockSpec((n, step, lanes), lambda i: (0, i, 0)),
        out_shape=jax.ShapeDtypeStruct(x.shape, dtype),
        name="swap_blocks",
    )(x)


def step_kernel(idx_ref, g_ref, *refs):
    sources, (src_ref, out_ref, send_ref, op_ref, sems) = refs[:5], refs[5:]
    batch, y0 = idx_ref[0], idx_ref[1]
    n, depth = op_ref.shape[2], g_ref.shape[0]
    rows = NY * n
    own, up, down = sources[:3]
    copies = [
        [
            pltpu.make_async_copy(there, op_ref.at[p, (y0 + step) % NY], sems.at[p, j])
            for j, (there, step) in enumerate(((own.at[p], 0), (up.at[p], 3), (down.at[p], 1), (sources[3 + p], 2)))
        ]
        for p in range(2)
    ]
    for group in copies:
        for copy in group:
            copy.start()
    g = g_ref[...]
    blk = block_of((rows, 128))
    small = block_of((n, 128))
    parts = []
    for p in range(2):
        for copy in copies[p]:
            copy.wait()
        acc = jnp.zeros((rows, 128), F32)
        for q in range(NY):
            op = op_ref[p, :, :, depth * q : depth * (q + 1)].reshape(rows, depth)
            acc = jnp.where(blk == q, jnp.dot(op, g, preferred_element_type=F32), acc)
        parts.append(acc)
    d = parts[0] + turn(parts[1])
    d = d + roll_blocks(d, 1)
    d = d + roll_blocks(d, 2)
    total = jnp.zeros((n, 128), F32)
    for y in range(NY):
        total = jnp.where(small == y, roll_blocks(d[y * n : (y + 1) * n], y - 3), total)
    total = total + src_ref[batch]
    out_ref[...] = total
    send_ref[...] = total.astype(BF)


def apply_next(index, g, ops, src):
    n, depth = ops[3].shape
    there = pl.BlockSpec(memory_space=pl.ANY)
    whole = pl.BlockSpec(memory_space=pltpu.VMEM)
    return pl.pallas_call(
        step_kernel,
        in_specs=[pl.BlockSpec(memory_space=pltpu.SMEM), whole] + [there] * 5 + [whole],
        out_specs=[whole, whole],
        scratch_shapes=[pltpu.VMEM((2, NY, n, depth), BF), pltpu.SemaphoreType.DMA((2, NY))],
        out_shape=[jax.ShapeDtypeStruct((n, 128), F32), jax.ShapeDtypeStruct((n, 128), BF)],
        compiler_params=pltpu.CompilerParams(vmem_limit_bytes=24 * 2**20),
        cost_estimate=pl.CostEstimate(
            flops=4 * NY * n * depth * 128, bytes_accessed=4 * NY * n * depth, transcendentals=0
        ),
        name="apply_next",
    )(index, g, *ops, src)


def interior_kernel(idx_ref, op_ref, own_ref, up_ref, down_ref, top_ref, bottom_ref, last_ref, out_ref, v_ref):
    y0 = idx_ref[0]
    n = 96
    pieces = own_ref.shape[1] // n
    blk = block_of((n, 128))
    fronts = ((own_ref, 0), (up_ref, 3), (down_ref, 1), (None, 2))
    for ref, step in fronts:
        front = (y0 + step) % NY
        for z in range(pieces):
            at = slice(z * n, (z + 1) * n)
            if ref is not None:
                sets = [ref[b, at] for b in range(NB - 1)]
            elif z < pieces // 2:
                sets = [top_ref[b, at] for b in range(NB - 1)]
            else:
                sets = [bottom_ref[b, z * n - bottom_ref.shape[1] : (z + 1) * n - bottom_ref.shape[1]] for b in range(NB - 1)]
            sets = [x.astype(F32) for x in sets + [last_ref[front, at]]]
            for y in range(NY):
                total = jnp.zeros((n, 128), F32)
                for b, x in enumerate(sets):
                    total = jnp.where(blk == b, roll_blocks(x, b - y), total)
                v_ref[(y * pieces + z) * n : (y * pieces + z + 1) * n] = total.astype(BF)
        v = v_ref[...]
        d0 = jnp.dot(op_ref[0], v, preferred_element_type=F32)
        d1 = jnp.dot(op_ref[1], v, preferred_element_type=F32)
        out_ref[front] = d0 + turn(d1)


def apply_interior(index, op, sets):
    _, n, depth = op.shape
    whole = pl.BlockSpec(memory_space=pltpu.VMEM)
    return pl.pallas_call(
        interior_kernel,
        in_specs=[pl.BlockSpec(memory_space=pltpu.SMEM)] + [whole] * 7,
        out_specs=whole,
        out_shape=jax.ShapeDtypeStruct((NY, n, 128), F32),
        scratch_shapes=[pltpu.VMEM((depth, 128), BF)],
        compiler_params=pltpu.CompilerParams(vmem_limit_bytes=24 * 2**20),
        name="apply_interior",
    )(index, op, *sets)


def spread(x, axis):
    copies = jnp.broadcast_to(x, (lax.axis_size(axis), *x.shape))
    return lax.all_to_all(copies, axis, split_axis=0, concat_axis=0, tiled=True)


def ring(x, step):
    return lax.ppermute(x, "y", [(i, (i + step) % NY) for i in range(NY)])


def local(incident, green_interior, green_next, sources):
    s = lax.axis_index("slab")
    y = lax.axis_index("y")
    rows = incident.shape[1]
    together = lax.optimization_barrier
    op = green_next[0]
    up, down = ring(op, 1), ring(op, -1)
    ops = [op, up, down, ring(up[0], 1), ring(down[1], -1)]
    inc = lax.all_to_all(incident.astype(BF), "y", 0, 0, tiled=True)
    src = lax.all_to_all(sources[0], "y", 0, 0, tiled=True)
    inc = swap_blocks(inc, BF)
    src = swap_blocks(src, F32)
    stored = jnp.zeros((NB + 2, NZ * rows, 128), BF)
    kept = jnp.zeros((NB + 2, rows, 128), F32)
    received = jnp.zeros((rows, 128), BF)
    last_step = NS + NB - 2
    for c in range(last_step + 1):
        entering = jnp.where(s == 0, inc[min(c, NB - 1)], received)
        g = spread(entering, "zl").reshape(NZ * rows, 128)
        if c == last_step:
            g, up, down = together((g, up, down))
        batch = c - s
        index = jnp.stack([jnp.clip(batch, 0, NB - 1), y]).astype(jnp.int32)
        leaving, send = apply_next(index, g, ops, src)
        if c < last_step:
            pairs = [(a, a + 1) for a in range(NS - 1) if 0 <= c - a < NB]
            received = lax.ppermute(send, "slab", pairs)
        slot = jnp.clip(batch + 1, 0, NB + 1)
        stored = lax.dynamic_update_index_in_dim(stored, g, slot, 0)
        kept = lax.dynamic_update_index_in_dim(kept, leaving, slot, 0)
        if c == last_step - 1:
            early = stored[1:NB]
            up, down = ring(early, 1), ring(early, -1)
    half = NZ * rows // 2
    top, bottom = ring(up[:, :half], 1), ring(down[:, half:], -1)
    last = spread(stored[NB], "y")
    traces = swap_blocks(kept[1 : NB + 1], F32)
    traces = lax.all_to_all(traces, "y", 0, 0, tiled=True)
    sets = (early, up, down, top, bottom, last)
    interior = apply_interior(y.astype(jnp.int32).reshape(1), green_interior[0], sets)
    return interior[None], traces[None]


def solution(mesh):
    fine = Mesh(mesh.devices.reshape(NS, NY, NZ), ("slab", "y", "zl"))
    trace = ("y", "zl")
    return jax.shard_map(
        local,
        mesh=fine,
        in_specs=(
            P(None, trace, None),
            P("slab", None, trace, None),
            P("slab", None, trace, None),
            P("slab", None, trace, None),
        ),
        out_specs=(P("slab", None, trace, None), P("slab", None, trace, None)),
        check_vma=False,
    )
```

time: 684 us -> 678 us (level)
  the two profiles are of different devices: /device:TPU:484 before, /device:TPU:482 now
where the time goes in v4:
time: 678 us; the launch traced here: 665 us
  starting transfers between devices  248 us (37%)
  waiting for transfers between devices  235 us (35%)
  other arithmetic  111 us (16%)
  local copies, waits for them, and re-layouts  58.7 us (9%)
  Pallas kernels  10.2 us (2%)
    all_to_all x20, starting transfers between devices, spread(): return lax.all_to_all(copies, axis, split_axis=0, concat_axis=0, tiled=True)  193 us
    all_to_all x20, waiting for transfers between devices, spread(): return lax.all_to_all(copies, axis, split_axis=0, concat_axis=0, tiled=True)  98.9 us
    pallas_call x19, other arithmetic, apply_next(): pl.pallas_call(step_kernel, in_specs=[pl.BlockSpec(memory_space=pltpu.SME...  94 us
    ppermute x18, waiting for transfers between devices, local(): received = lax.ppermute(send, 'slab', pairs)  77 us
    ppermute x8, waiting for transfers between devices, ring(): return lax.ppermute(x, 'y', [(i, (i + step) % NY) for i in range(NY)])  30.2 us
    dynamic_update_slice x19, local copies, waits for them, and re-layouts, local(): stored = lax.dynamic_update_index_in_dim(stored, g, slot, 0)  29.8 us
    ppermute x8, starting transfers between devices, ring(): return lax.ppermute(x, 'y', [(i, (i + step) % NY) for i in range(NY)])  26.9 us
    all_to_all x1, waiting for transfers between devices, local(): inc = lax.all_to_all(incident.astype(BF), 'y', 0, 0, tiled=True)  23.8 us
  transfers between devices with their start and end apart: 49, of which 28 were waited for; matrix products, arithmetic and copies ran while one was open for 6% of the time, Pallas kernels for 1%

profile of v4, /device:TPU:482, one launch (start us, length us, event | category | flops | bytes accessed | tf_op | source)
XLA Modules:
  0.0 664.7 jit_solution(3376077344407280488)
XLA Ops:
  0.6 4.9 collective-permute-start.1
  13.6 23.8 %all-to-all-done.src_ref = bf16[4,96,128]{2,1,0:T(8,128)(2,1)S(1)} async-done(((bf16[4,96,128]{2,1,0:T(8,128)(2,1)}), bf16[4,96,128]{2,1,0:T(8,128)(2,1)S(1)}, u32[]{:S(2)}, u32[]{:S(2)}) %all-to-all-start) | async-done | bytes 98336 | tf_op jit(solution)/shard_map/all_to_all | solution.py:170
  44.0 5.1 collective-permute-start.3
  50.5 10.0 %all-to-all-start.1 = ((bf16[8,96,128]{2,1,0:T(8,128)(2,1)}), bf16[8,96,128]{2,1,0:T(8,128)(2,1)}, u32[]{:S(2)}, u32[]{:S(2)}) async-start(bf16[8,96,128]{2,1,0:T(8,128)(2,1)} %broadcast_in_dim.193), calls=%async_computation.1 | async-start | bytes 393216 | tf_op jit(solution)/shard_map/all_to_all | solution.py:155
  67.7 9.7 %collective-permute-done.2 = bf16[96,3072]{1,0:T(8,128)(2,1)} collective-permute-done((bf16[96,3072]{1,0:T(8,128)(2,1)}, bf16[96,3072]{1,0:T(8,128)(2,1)}, u32[]{:S(2)}, u32[]{:S(2)}) %collective-permute-start.2) | collective-permute-done | bytes 589856 | tf_op jit(solution)/shard_map/ppermute | solution.py:159
  78.1 5.0 apply_next.37
  85.3 9.9 %all-to-all-start.3 = ((bf16[8,96,128]{2,1,0:T(8,128)(2,1)}), bf16[8,96,128]{2,1,0:T(8,128)(2,1)}, u32[]{:S(2)}, u32[]{:S(2)}) async-start(bf16[8,96,128]{2,1,0:T(8,128)(2,1)} %broadcast_in_dim.195), calls=%async_computation.3 | async-start | bytes 393216 | tf_op jit(solution)/shard_map/all_to_all | solution.py:155
  95.2 6.3 all-to-all-done.3
  101.5 5.0 apply_next.36
  108.6 9.9 %all-to-all-start.4 = ((bf16[8,96,128]{2,1,0:T(8,128)(2,1)}), bf16[8,96,128]{2,1,0:T(8,128)(2,1)}, u32[]{:S(2)}, u32[]{:S(2)}) async-start(bf16[8,96,128]{2,1,0:T(8,128)(2,1)} %broadcast_in_dim.197), calls=%async_computation.4 | async-start | bytes 393216 | tf_op jit(solution)/shard_map/all_to_all | solution.py:155
  118.6 6.3 all-to-all-done.4
  124.8 5.0 apply_next.35
  131.9 9.9 %all-to-all-start.5 = ((bf16[8,96,128]{2,1,0:T(8,128)(2,1)}), bf16[8,96,128]{2,1,0:T(8,128)(2,1)}, u32[]{:S(2)}, u32[]{:S(2)}) async-start(bf16[8,96,128]{2,1,0:T(8,128)(2,1)} %broadcast_in_dim.199), calls=%async_computation.5 | async-start | bytes 393216 | tf_op jit(solution)/shard_map/all_to_all | solution.py:155
  141.9 6.3 all-to-all-done.5
  148.2 5.0 apply_next.34
  155.3 9.9 %all-to-all-start.6 = ((bf16[8,96,128]{2,1,0:T(8,128)(2,1)}), bf16[8,96,128]{2,1,0:T(8,128)(2,1)}, u32[]{:S(2)}, u32[]{:S(2)}) async-start(bf16[8,96,128]{2,1,0:T(8,128)(2,1)} %broadcast_in_dim.201), calls=%async_computation.6 | async-start | bytes 393216 | tf_op jit(solution)/shard_map/all_to_all | solution.py:155
  165.3 6.3 all-to-all-done.6
  171.5 5.0 apply_next.33
  178.6 9.9 %all-to-all-start.7 = ((bf16[8,96,128]{2,1,0:T(8,128)(2,1)}), bf16[8,96,128]{2,1,0:T(8,128)(2,1)}, u32[]{:S(2)}, u32[]{:S(2)}) async-start(bf16[8,96,128]{2,1,0:T(8,128)(2,1)} %broadcast_in_dim.203), calls=%async_computation.7 | async-start | bytes 393216 | tf_op jit(solution)/shard_map/all_to_all | solution.py:155
  188.6 6.3 all-to-all-done.7
  194.9 5.0 apply_next.32
  202.0 10.4 %all-to-all-start.8 = ((bf16[8,96,128]{2,1,0:T(8,128)(2,1)}), bf16[8,96,128]{2,1,0:T(8,128)(2,1)}, u32[]{:S(2)}, u32[]{:S(2)}) async-start(bf16[8,96,128]{2,1,0:T(8,128)(2,1)} %broadcast_in_dim.205), calls=%async_computation.8 | async-start | bytes 393216 | tf_op jit(solution)/shard_map/all_to_all | solution.py:155
  212.5 6.2 all-to-all-done.8
  218.7 5.0 apply_next.31
  225.8 9.9 %all-to-all-start.9 = ((bf16[8,96,128]{2,1,0:T(8,128)(2,1)}), bf16[8,96,128]{2,1,0:T(8,128)(2,1)}, u32[]{:S(2)}, u32[]{:S(2)}) async-start(bf16[8,96,128]{2,1,0:T(8,128)(2,1)} %broadcast_in_dim.207), calls=%async_computation.9 | async-start | bytes 393216 | tf_op jit(solution)/shard_map/all_to_all | solution.py:155
  235.7 6.3 all-to-all-done.9
  242.0 5.0 apply_next.30
  249.1 9.9 %all-to-all-start.10 = ((bf16[8,96,128]{2,1,0:T(8,128)(2,1)}), bf16[8,96,128]{2,1,0:T(8,128)(2,1)}, u32[]{:S(2)}, u32[]{:S(2)}) async-start(bf16[8,96,128]{2,1,0:T(8,128)(2,1)} %broadcast_in_dim.209), calls=%async_computation.10 | async-start | bytes 393216 | tf_op jit(solution)/shard_map/all_to_all | solution.py:155
  259.1 6.3 all-to-all-done.10
  265.3 5.0 apply_next.29
  272.5 9.9 %all-to-all-start.11 = ((bf16[8,96,128]{2,1,0:T(8,128)(2,1)}), bf16[8,96,128]{2,1,0:T(8,128)(2,1)}, u32[]{:S(2)}, u32[]{:S(2)}) async-start(bf16[8,96,128]{2,1,0:T(8,128)(2,1)} %broadcast_in_dim.211), calls=%async_computation.11 | async-start | bytes 393216 | tf_op jit(solution)/shard_map/all_to_all | solution.py:155
  282.4 6.3 all-to-all-done.11
  288.7 5.0 apply_next.28
  295.0 31.1 %collective-permute-done.13 = bf16[96,128]{1,0:T(8,128)(2,1)S(1)} collective-permute-done((bf16[96,128]{1,0:T(8,128)(2,1)S(1)}, bf16[96,128]{1,0:T(8,128)(2,1)S(1)}, u32[]{:S(2)}, u32[]{:S(2)}) %collective-permute-start.13) | collective-permute-done | bytes 24608 | tf_op jit(solution)/shard_map/ppermute | solution.py:188
  327.5 9.9 %all-to-all-start.12 = ((bf16[8,96,128]{2,1,0:T(8,128)(2,1)}), bf16[8,96,128]{2,1,0:T(8,128)(2,1)}, u32[]{:S(2)}, u32[]{:S(2)}) async-start(bf16[8,96,128]{2,1,0:T(8,128)(2,1)} %broadcast_in_dim.213), calls=%async_computation.12 | async-start | bytes 393216 | tf_op jit(solution)/shard_map/all_to_all | solution.py:155
  337.5 6.3 all-to-all-done.12
  343.7 5.0 apply_next.27
  350.6 14.0 %collective-permute-done.14 = bf16[96,128]{1,0:T(8,128)(2,1)S(1)} collective-permute-done((bf16[96,128]{1,0:T(8,128)(2,1)S(1)}, bf16[96,128]{1,0:T(8,128)(2,1)S(1)}, u32[]{:S(2)}, u32[]{:S(2)}) %collective-permute-start.14) | collective-permute-done | bytes 24608 | tf_op jit(solution)/shard_map/ppermute | solution.py:188
  366.1 9.9 %all-to-all-start.13 = ((bf16[8,96,128]{2,1,0:T(8,128)(2,1)}), bf16[8,96,128]{2,1,0:T(8,128)(2,1)}, u32[]{:S(2)}, u32[]{:S(2)}) async-start(bf16[8,96,128]{2,1,0:T(8,128)(2,1)} %broadcast_in_dim.215), calls=%async_computation.13 | async-start | bytes 393216 | tf_op jit(solution)/shard_map/all_to_all | solution.py:155
  376.1 6.3 all-to-all-done.13
  382.3 5.0 apply_next.26
  389.2 14.3 %collective-permute-done.15 = bf16[96,128]{1,0:T(8,128)(2,1)S(1)} collective-permute-done((bf16[96,128]{1,0:T(8,128)(2,1)S(1)}, bf16[96,128]{1,0:T(8,128)(2,1)S(1)}, u32[]{:S(2)}, u32[]{:S(2)}) %collective-permute-start.15) | collective-permute-done | bytes 24608 | tf_op jit(solution)/shard_map/ppermute | solution.py:188
  405.0 9.9 %all-to-all-start.14 = ((bf16[8,96,128]{2,1,0:T(8,128)(2,1)}), bf16[8,96,128]{2,1,0:T(8,128)(2,1)}, u32[]{:S(2)}, u32[]{:S(2)}) async-start(bf16[8,96,128]{2,1,0:T(8,128)(2,1)} %broadcast_in_dim.217), calls=%async_computation.14 | async-start | bytes 393216 | tf_op jit(solution)/shard_map/all_to_all | solution.py:155
  415.0 6.3 all-to-all-done.14
  421.2 5.0 apply_next.25
  428.1 16.7 %collective-permute-done.16 = bf16[96,128]{1,0:T(8,128)(2,1)S(1)} collective-permute-done((bf16[96,128]{1,0:T(8,128)(2,1)S(1)}, bf16[96,128]{1,0:T(8,128)(2,1)S(1)}, u32[]{:S(2)}, u32[]{:S(2)}) %collective-permute-start.16) | collective-permute-done | bytes 24608 | tf_op jit(solution)/shard_map/ppermute | solution.py:188
  446.3 10.1 %all-to-all-start.15 = ((bf16[8,96,128]{2,1,0:T(8,128)(2,1)}), bf16[8,96,128]{2,1,0:T(8,128)(2,1)}, u32[]{:S(2)}, u32[]{:S(2)}) async-start(bf16[8,96,128]{2,1,0:T(8,128)(2,1)} %broadcast_in_dim.219), calls=%async_computation.15 | async-start | bytes 393216 | tf_op jit(solution)/shard_map/all_to_all | solution.py:155
  456.5 6.2 all-to-all-done.15
  462.7 5.0 apply_next.24
  471.2 9.9 %all-to-all-start.16 = ((bf16[8,96,128]{2,1,0:T(8,128)(2,1)}), bf16[8,96,128]{2,1,0:T(8,128)(2,1)}, u32[]{:S(2)}, u32[]{:S(2)}) async-start(bf16[8,96,128]{2,1,0:T(8,128)(2,1)} %broadcast_in_dim.221), calls=%async_computation.16 | async-start | bytes 393216 | tf_op jit(solution)/shard_map/all_to_all | solution.py:155
  481.2 9.8 %all-to-all-done.16 = bf16[8,96,128]{2,1,0:T(8,128)(2,1)} async-done(((bf16[8,96,128]{2,1,0:T(8,128)(2,1)}), bf16[8,96,128]{2,1,0:T(8,128)(2,1)}, u32[]{:S(2)}, u32[]{:S(2)}) %all-to-all-start.16) | async-done | bytes 196640 | tf_op jit(solution)/shard_map/all_to_all | solution.py:155
  491.0 5.0 apply_next.23
  498.1 9.9 %all-to-all-start.17 = ((bf16[8,96,128]{2,1,0:T(8,128)(2,1)}), bf16[8,96,128]{2,1,0:T(8,128)(2,1)}, u32[]{:S(2)}, u32[]{:S(2)}) async-start(bf16[8,96,128]{2,1,0:T(8,128)(2,1)} %broadcast_in_dim.223), calls=%async_computation.17 | async-start | bytes 393216 | tf_op jit(solution)/shard_map/all_to_all | solution.py:155
  512.7 5.6 all-to-all-done.17
  518.3 5.0 apply_next.22
  527.0 9.9 %all-to-all-start.18 = ((bf16[8,96,128]{2,1,0:T(8,128)(2,1)}), bf16[8,96,128]{2,1,0:T(8,128)(2,1)}, u32[]{:S(2)}, u32[]{:S(2)}) async-start(bf16[8,96,128]{2,1,0:T(8,128)(2,1)} %broadcast_in_dim.225), calls=%async_computation.18 | async-start | bytes 393216 | tf_op jit(solution)/shard_map/all_to_all | solution.py:155
  546.6 5.0 apply_next.21
  555.4 9.9 %all-to-all-start.19 = ((bf16[8,96,128]{2,1,0:T(8,128)(2,1)}), bf16[8,96,128]{2,1,0:T(8,128)(2,1)}, u32[]{:S(2)}, u32[]{:S(2)}) async-start(bf16[8,96,128]{2,1,0:T(8,128)(2,1)} %broadcast_in_dim.227), calls=%async_computation.19 | async-start | bytes 393216 | tf_op jit(solution)/shard_map/all_to_all | solution.py:155
  575.0 5.0 apply_next.20
  583.7 10.0 %all-to-all-start.20 = ((bf16[8,96,128]{2,1,0:T(8,128)(2,1)}), bf16[8,96,128]{2,1,0:T(8,128)(2,1)S(1)}, u32[]{:S(2)}, u32[]{:S(2)}) async-start(bf16[8,96,128]{2,1,0:T(8,128)(2,1)} %broadcast_in_dim.229), calls=%async_computation.20 | async-start | bytes 393216 | tf_op jit(solution)/shard_map/all_to_all | solution.py:155
  602.4 9.6 %collective-permute-done.23.down_ref = bf16[3,768,128]{2,1,0:T(8,128)(2,1)S(1)} collective-permute-done((bf16[3,768,128]{2,1,0:T(8,128)(2,1)S(1)}, bf16[3,768,128]{2,1,0:T(8,128)(2,1)S(1)}, u32[]{:S(2)}, u32[]{:S(2)}) %collective-permute-start.23) | collective-permute-done | bytes 589856 | tf_op jit(solution)/shard_map/ppermute | solution.py:159
  628.2 5.3 all-to-all-done.22
  640.1 5.1 collective-permute-start.25
  658.9 4.9 apply_interior.1
  (173 shorter events, 143.4 us)
Async XLA Ops:
  0.6 42.5 %collective-permute-start.1 = (bf16[2,96,3072]{2,1,0:T(8,128)(2,1)}, bf16[2,96,3072]{2,1,0:T(8,128)(2,1)S(1)}, u32[]{:S(2)}, u32[]{:S(2)}) collective-permute-start(bf16[2,96,3072]{2,1,0:T(8,128)(2,1)} %bitcast.190), channel_id=1, source_target_pairs={{0,24},{8,0},{16,8},{24,16},{1,25},{9,1},{17,9},{25,17},{2,26},{10... | collective-permute-start | bytes 3538952 | tf_op jit(solution)/shard_map/ppermute | solution.py:159
  5.6 55.0 %collective-permute-start = (bf16[2,96,3072]{2,1,0:T(8,128)(2,1)}, bf16[2,96,3072]{2,1,0:T(8,128)(2,1)S(1)}, u32[]{:S(2)}, u32[]{:S(2)}) collective-permute-start(bf16[2,96,3072]{2,1,0:T(8,128)(2,1)} %bitcast.191), channel_id=1, source_target_pairs={{0,8},{8,16},{16,24},{24,0},{1,9},{9,17},{17,25},{25,1},{2,10},{10... | collective-permute-start | bytes 3538952 | tf_op jit(solution)/shard_map/ppermute | solution.py:159
  9.1 28.3 %all-to-all-start = ((bf16[4,96,128]{2,1,0:T(8,128)(2,1)}), bf16[4,96,128]{2,1,0:T(8,128)(2,1)S(1)}, u32[]{:S(2)}, u32[]{:S(2)}) async-start(bf16[4,96,128]{2,1,0:T(8,128)(2,1)} %convert_element_type.3), calls=%async_computation | async-start | bytes 196608 | tf_op jit(solution)/shard_map/all_to_all | solution.py:170
  37.4 3.4 copy-start.13
  37.4 11.8 %all-to-all-start.2 = ((f32[4,96,128]{2,1,0:T(8,128)}), f32[4,96,128]{2,1,0:T(8,128)S(1)}, u32[]{:S(2)}, u32[]{:S(2)}) async-start(f32[4,96,128]{2,1,0:T(8,128)} %bitcast.215), calls=%async_computation.2 | async-start | bytes 393216 | tf_op jit(solution)/shard_map/all_to_all | solution.py:171
  44.0 23.7 %collective-permute-start.3 = (bf16[96,3072]{1,0:T(8,128)(2,1)}, bf16[96,3072]{1,0:T(8,128)(2,1)}, u32[]{:S(2)}, u32[]{:S(2)}) collective-permute-start(bf16[96,3072]{1,0:T(8,128)(2,1)} %slice_bitcast_fusion), channel_id=1, source_target_pairs={{0,24},{8,0},{16,8},{24,16},{1,25},{9,1},{17,9},{25,17},{2,26},{10... | collective-permute-start | bytes 1769480 | tf_op jit(solution)/shard_map/ppermute | solution.py:159
  49.1 0.7 copy-start.10
  50.5 27.6 %copy-start.8 = (bf16[1,2,96,3072]{3,2,1,0:T(8,128)(2,1)S(1)}, bf16[1,2,96,3072]{3,2,1,0:T(8,128)(2,1)}, u32[]{:S(2)}) copy-start(bf16[1,2,96,3072]{3,2,1,0:T(8,128)(2,1)} %param.6) | copy-start | bytes 3538948
  50.5 17.2 %all-to-all-start.1 = ((bf16[8,96,128]{2,1,0:T(8,128)(2,1)}), bf16[8,96,128]{2,1,0:T(8,128)(2,1)}, u32[]{:S(2)}, u32[]{:S(2)}) async-start(bf16[8,96,128]{2,1,0:T(8,128)(2,1)} %broadcast_in_dim.193), calls=%async_computation.1 | async-start | bytes 393216 | tf_op jit(solution)/shard_map/all_to_all | solution.py:155
  60.6 514.4 %copy-start.7 = (bf16[2,96,3072]{2,1,0:T(8,128)(2,1)}, bf16[2,96,3072]{2,1,0:T(8,128)(2,1)S(1)}, u32[]{:S(2)}) copy-start(bf16[2,96,3072]{2,1,0:T(8,128)(2,1)S(1)} %collective-permute-done) | copy-start | bytes 3538948
  61.5 15.9 %collective-permute-start.2 = (bf16[96,3072]{1,0:T(8,128)(2,1)}, bf16[96,3072]{1,0:T(8,128)(2,1)}, u32[]{:S(2)}, u32[]{:S(2)}) collective-permute-start(bf16[96,3072]{1,0:T(8,128)(2,1)} %slice_bitcast_fusion.1), channel_id=1, source_target_pairs={{0,8},{8,16},{16,24},{24,0},{1,9},{9,17},{17,25},{25,1},{2,10},{10... | collective-permute-start | bytes 1769480 | tf_op jit(solution)/shard_map/ppermute | solution.py:159
  83.1 0.7 collective-permute-start.4
  85.3 16.2 %all-to-all-start.3 = ((bf16[8,96,128]{2,1,0:T(8,128)(2,1)}), bf16[8,96,128]{2,1,0:T(8,128)(2,1)}, u32[]{:S(2)}, u32[]{:S(2)}) async-start(bf16[8,96,128]{2,1,0:T(8,128)(2,1)} %broadcast_in_dim.195), calls=%async_computation.3 | async-start | bytes 393216 | tf_op jit(solution)/shard_map/all_to_all | solution.py:155
  106.5 0.7 collective-permute-start.5
  108.6 16.2 %all-to-all-start.4 = ((bf16[8,96,128]{2,1,0:T(8,128)(2,1)}), bf16[8,96,128]{2,1,0:T(8,128)(2,1)}, u32[]{:S(2)}, u32[]{:S(2)}) async-start(bf16[8,96,128]{2,1,0:T(8,128)(2,1)} %broadcast_in_dim.197), calls=%async_computation.4 | async-start | bytes 393216 | tf_op jit(solution)/shard_map/all_to_all | solution.py:155
  129.8 0.7 collective-permute-start.6
  131.9 16.2 %all-to-all-start.5 = ((bf16[8,96,128]{2,1,0:T(8,128)(2,1)}), bf16[8,96,128]{2,1,0:T(8,128)(2,1)}, u32[]{:S(2)}, u32[]{:S(2)}) async-start(bf16[8,96,128]{2,1,0:T(8,128)(2,1)} %broadcast_in_dim.199), calls=%async_computation.5 | async-start | bytes 393216 | tf_op jit(solution)/shard_map/all_to_all | solution.py:155
  153.2 0.7 collective-permute-start.7
  155.3 16.2 %all-to-all-start.6 = ((bf16[8,96,128]{2,1,0:T(8,128)(2,1)}), bf16[8,96,128]{2,1,0:T(8,128)(2,1)}, u32[]{:S(2)}, u32[]{:S(2)}) async-start(bf16[8,96,128]{2,1,0:T(8,128)(2,1)} %broadcast_in_dim.201), calls=%async_computation.6 | async-start | bytes 393216 | tf_op jit(solution)/shard_map/all_to_all | solution.py:155
  176.5 0.7 collective-permute-start.8
  178.6 16.2 %all-to-all-start.7 = ((bf16[8,96,128]{2,1,0:T(8,128)(2,1)}), bf16[8,96,128]{2,1,0:T(8,128)(2,1)}, u32[]{:S(2)}, u32[]{:S(2)}) async-start(bf16[8,96,128]{2,1,0:T(8,128)(2,1)} %broadcast_in_dim.203), calls=%async_computation.7 | async-start | bytes 393216 | tf_op jit(solution)/shard_map/all_to_all | solution.py:155
  199.8 0.7 collective-permute-start.9
  202.0 16.7 %all-to-all-start.8 = ((bf16[8,96,128]{2,1,0:T(8,128)(2,1)}), bf16[8,96,128]{2,1,0:T(8,128)(2,1)}, u32[]{:S(2)}, u32[]{:S(2)}) async-start(bf16[8,96,128]{2,1,0:T(8,128)(2,1)} %broadcast_in_dim.205), calls=%async_computation.8 | async-start | bytes 393216 | tf_op jit(solution)/shard_map/all_to_all | solution.py:155
  223.6 0.7 collective-permute-start.10
  225.8 16.2 %all-to-all-start.9 = ((bf16[8,96,128]{2,1,0:T(8,128)(2,1)}), bf16[8,96,128]{2,1,0:T(8,128)(2,1)}, u32[]{:S(2)}, u32[]{:S(2)}) async-start(bf16[8,96,128]{2,1,0:T(8,128)(2,1)} %broadcast_in_dim.207), calls=%async_computation.9 | async-start | bytes 393216 | tf_op jit(solution)/shard_map/all_to_all | solution.py:155
  247.0 0.7 collective-permute-start.11
  249.1 16.2 %all-to-all-start.10 = ((bf16[8,96,128]{2,1,0:T(8,128)(2,1)}), bf16[8,96,128]{2,1,0:T(8,128)(2,1)}, u32[]{:S(2)}, u32[]{:S(2)}) async-start(bf16[8,96,128]{2,1,0:T(8,128)(2,1)} %broadcast_in_dim.209), calls=%async_computation.10 | async-start | bytes 393216 | tf_op jit(solution)/shard_map/all_to_all | solution.py:155
  270.3 0.7 collective-permute-start.12
  272.5 16.2 %all-to-all-start.11 = ((bf16[8,96,128]{2,1,0:T(8,128)(2,1)}), bf16[8,96,128]{2,1,0:T(8,128)(2,1)}, u32[]{:S(2)}, u32[]{:S(2)}) async-start(bf16[8,96,128]{2,1,0:T(8,128)(2,1)} %broadcast_in_dim.211), calls=%async_computation.11 | async-start | bytes 393216 | tf_op jit(solution)/shard_map/all_to_all | solution.py:155
  293.7 32.4 %collective-permute-start.13 = (bf16[96,128]{1,0:T(8,128)(2,1)S(1)}, bf16[96,128]{1,0:T(8,128)(2,1)S(1)}, u32[]{:S(2)}, u32[]{:S(2)}) collective-permute-start(bf16[96,128]{1,0:T(8,128)(2,1)S(1)} %get-tuple-element.157), channel_id=1, source_target_pairs={{192,224},{224,256},{256,288},{288,320},{193,225},{225,257},{257,2... | collective-permute-start | bytes 73736 | tf_op jit(solution)/shard_map/ppermute | solution.py:188
  327.5 16.2 %all-to-all-start.12 = ((bf16[8,96,128]{2,1,0:T(8,128)(2,1)}), bf16[8,96,128]{2,1,0:T(8,128)(2,1)}, u32[]{:S(2)}, u32[]{:S(2)}) async-start(bf16[8,96,128]{2,1,0:T(8,128)(2,1)} %broadcast_in_dim.213), calls=%async_computation.12 | async-start | bytes 393216 | tf_op jit(solution)/shard_map/all_to_all | solution.py:155
  348.7 16.0 %collective-permute-start.14 = (bf16[96,128]{1,0:T(8,128)(2,1)S(1)}, bf16[96,128]{1,0:T(8,128)(2,1)S(1)}, u32[]{:S(2)}, u32[]{:S(2)}) collective-permute-start(bf16[96,128]{1,0:T(8,128)(2,1)S(1)} %get-tuple-element.117), channel_id=1, source_target_pairs={{224,256},{256,288},{288,320},{320,352},{225,257},{257,289},{289,3... | collective-permute-start | bytes 73736 | tf_op jit(solution)/shard_map/ppermute | solution.py:188
  366.1 16.2 %all-to-all-start.13 = ((bf16[8,96,128]{2,1,0:T(8,128)(2,1)}), bf16[8,96,128]{2,1,0:T(8,128)(2,1)}, u32[]{:S(2)}, u32[]{:S(2)}) async-start(bf16[8,96,128]{2,1,0:T(8,128)(2,1)} %broadcast_in_dim.215), calls=%async_computation.13 | async-start | bytes 393216 | tf_op jit(solution)/shard_map/all_to_all | solution.py:155
  387.3 16.2 %collective-permute-start.15 = (bf16[96,128]{1,0:T(8,128)(2,1)S(1)}, bf16[96,128]{1,0:T(8,128)(2,1)S(1)}, u32[]{:S(2)}, u32[]{:S(2)}) collective-permute-start(bf16[96,128]{1,0:T(8,128)(2,1)S(1)} %get-tuple-element.109), channel_id=1, source_target_pairs={{256,288},{288,320},{320,352},{352,384},{257,289},{289,321},{321,3... | collective-permute-start | bytes 73736 | tf_op jit(solution)/shard_map/ppermute | solution.py:188
  405.0 16.2 %all-to-all-start.14 = ((bf16[8,96,128]{2,1,0:T(8,128)(2,1)}), bf16[8,96,128]{2,1,0:T(8,128)(2,1)}, u32[]{:S(2)}, u32[]{:S(2)}) async-start(bf16[8,96,128]{2,1,0:T(8,128)(2,1)} %broadcast_in_dim.217), calls=%async_computation.14 | async-start | bytes 393216 | tf_op jit(solution)/shard_map/all_to_all | solution.py:155
  426.2 18.7 %collective-permute-start.16 = (bf16[96,128]{1,0:T(8,128)(2,1)S(1)}, bf16[96,128]{1,0:T(8,128)(2,1)S(1)}, u32[]{:S(2)}, u32[]{:S(2)}) collective-permute-start(bf16[96,128]{1,0:T(8,128)(2,1)S(1)} %get-tuple-element.84), channel_id=1, source_target_pairs={{288,320},{320,352},{352,384},{384,416},{289,321},{321,353},{353,3... | collective-permute-start | bytes 73736 | tf_op jit(solution)/shard_map/ppermute | solution.py:188
  446.3 16.4 %all-to-all-start.15 = ((bf16[8,96,128]{2,1,0:T(8,128)(2,1)}), bf16[8,96,128]{2,1,0:T(8,128)(2,1)}, u32[]{:S(2)}, u32[]{:S(2)}) async-start(bf16[8,96,128]{2,1,0:T(8,128)(2,1)} %broadcast_in_dim.219), calls=%async_computation.15 | async-start | bytes 393216 | tf_op jit(solution)/shard_map/all_to_all | solution.py:155
  467.7 2.1 collective-permute-start.17
  471.2 19.8 %all-to-all-start.16 = ((bf16[8,96,128]{2,1,0:T(8,128)(2,1)}), bf16[8,96,128]{2,1,0:T(8,128)(2,1)}, u32[]{:S(2)}, u32[]{:S(2)}) async-start(bf16[8,96,128]{2,1,0:T(8,128)(2,1)} %broadcast_in_dim.221), calls=%async_computation.16 | async-start | bytes 393216 | tf_op jit(solution)/shard_map/all_to_all | solution.py:155
  496.0 0.7 collective-permute-start.18
  498.1 20.2 %all-to-all-start.17 = ((bf16[8,96,128]{2,1,0:T(8,128)(2,1)}), bf16[8,96,128]{2,1,0:T(8,128)(2,1)}, u32[]{:S(2)}, u32[]{:S(2)}) async-start(bf16[8,96,128]{2,1,0:T(8,128)(2,1)} %broadcast_in_dim.223), calls=%async_computation.17 | async-start | bytes 393216 | tf_op jit(solution)/shard_map/all_to_all | solution.py:155
  523.3 2.3 collective-permute-start.19
  527.0 19.6 %all-to-all-start.18 = ((bf16[8,96,128]{2,1,0:T(8,128)(2,1)}), bf16[8,96,128]{2,1,0:T(8,128)(2,1)}, u32[]{:S(2)}, u32[]{:S(2)}) async-start(bf16[8,96,128]{2,1,0:T(8,128)(2,1)} %broadcast_in_dim.225), calls=%async_computation.18 | async-start | bytes 393216 | tf_op jit(solution)/shard_map/all_to_all | solution.py:155
  551.6 2.3 collective-permute-start.20
  555.4 19.6 %all-to-all-start.19 = ((bf16[8,96,128]{2,1,0:T(8,128)(2,1)}), bf16[8,96,128]{2,1,0:T(8,128)(2,1)}, u32[]{:S(2)}, u32[]{:S(2)}) async-start(bf16[8,96,128]{2,1,0:T(8,128)(2,1)} %broadcast_in_dim.227), calls=%async_computation.19 | async-start | bytes 393216 | tf_op jit(solution)/shard_map/all_to_all | solution.py:155
  579.9 2.3 collective-permute-start.21
  583.7 32.2 %copy-start.9 = (f32[4,96,128]{2,1,0:T(8,128)S(1)}, f32[4,96,128]{2,1,0:T(8,128)}, u32[]{:S(2)}) copy-start(f32[4,96,128]{2,1,0:T(8,128)} %swap_blocks.4) | copy-start | bytes 589828
  583.7 31.5 %all-to-all-start.20 = ((bf16[8,96,128]{2,1,0:T(8,128)(2,1)}), bf16[8,96,128]{2,1,0:T(8,128)(2,1)S(1)}, u32[]{:S(2)}, u32[]{:S(2)}) async-start(bf16[8,96,128]{2,1,0:T(8,128)(2,1)} %broadcast_in_dim.229), calls=%async_computation.20 | async-start | bytes 393216 | tf_op jit(solution)/shard_map/all_to_all | solution.py:155
  596.4 15.6 %collective-permute-start.23 = (bf16[3,768,128]{2,1,0:T(8,128)(2,1)S(1)}, bf16[3,768,128]{2,1,0:T(8,128)(2,1)S(1)}, u32[]{:S(2)}, u32[]{:S(2)}) collective-permute-start(bf16[3,768,128]{2,1,0:T(8,128)(2,1)S(1)} %slice.65.own_ref), channel_id=1, source_target_pairs={{0,24},{8,0},{16,8},{24,16},{1,25},{9,1},{17,9},{25,17},{2,26},{10... | collective-permute-start | bytes 1769480 | tf_op jit(solution)/shard_map/ppermute | solution.py:159
  598.4 16.8 %collective-permute-start.22 = (bf16[3,768,128]{2,1,0:T(8,128)(2,1)S(1)}, bf16[3,768,128]{2,1,0:T(8,128)(2,1)S(1)}, u32[]{:S(2)}, u32[]{:S(2)}) collective-permute-start(bf16[3,768,128]{2,1,0:T(8,128)(2,1)S(1)} %slice.65.own_ref), channel_id=1, source_target_pairs={{0,8},{8,16},{16,24},{24,0},{1,9},{9,17},{17,25},{25,1},{2,10},{10... | collective-permute-start | bytes 1769480 | tf_op jit(solution)/shard_map/ppermute | solution.py:159
  612.0 8.4 %copy-start.1 = (bf16[3,768,128]{2,1,0:T(8,128)(2,1)}, bf16[3,768,128]{2,1,0:T(8,128)(2,1)S(1)}, u32[]{:S(2)}) copy-start(bf16[3,768,128]{2,1,0:T(8,128)(2,1)S(1)} %collective-permute-done.23.down_ref) | copy-start | bytes 1769476
  615.1 5.3 copy-start.3
  623.9 9.7 %all-to-all-start.22 = ((f32[4,96,128]{2,1,0:T(8,128)}), f32[4,96,128]{2,1,0:T(8,128)S(1)}, u32[]{:S(2)}, u32[]{:S(2)}) async-start(f32[4,96,128]{2,1,0:T(8,128)} %swap_blocks.5), calls=%async_computation.22 | async-start | bytes 393216 | tf_op jit(solution)/shard_map/all_to_all | solution.py:199
  633.5 1.0 copy-start.11
  634.5 21.3 %copy-start = (bf16[1,2,144,3072]{3,2,1,0:T(8,128)(2,1)S(1)}, bf16[1,2,144,3072]{3,2,1,0:T(8,128)(2,1)}, u32[]{:S(2)}) copy-start(bf16[1,2,144,3072]{3,2,1,0:T(8,128)(2,1)} %param.5) | copy-start | bytes 5308420
  634.5 21.3 %all-to-all-start.21 = ((bf16[4,768,128]{2,1,0:T(8,128)(2,1)}), bf16[4,768,128]{2,1,0:T(8,128)(2,1)S(1)}, u32[]{:S(2)}, u32[]{:S(2)}) async-start(bf16[4,768,128]{2,1,0:T(8,128)(2,1)} %broadcast_in_dim.231), calls=%async_computation.21 | async-start | bytes 1572864 | tf_op jit(solution)/shard_map/all_to_all | solution.py:155
  640.1 11.9 %collective-permute-start.25 = (bf16[3,384,128]{2,1,0:T(8,128)(2,1)S(1)}, bf16[3,384,128]{2,1,0:T(8,128)(2,1)S(1)}, u32[]{:S(2)}, u32[]{:S(2)}) collective-permute-start(bf16[3,384,128]{2,1,0:T(8,128)(2,1)S(1)} %slice.56), channel_id=1, source_target_pairs={{0,24},{8,0},{16,8},{24,16},{1,25},{9,1},{17,9},{25,17},{2,26},{10... | collective-permute-start | bytes 884744 | tf_op jit(solution)/shard_map/ppermute | solution.py:159
  645.2 9.8 %collective-permute-start.24 = (bf16[3,384,128]{2,1,0:T(8,128)(2,1)S(1)}, bf16[3,384,128]{2,1,0:T(8,128)(2,1)S(1)}, u32[]{:S(2)}, u32[]{:S(2)}) collective-permute-start(bf16[3,384,128]{2,1,0:T(8,128)(2,1)S(1)} %slice.55), channel_id=1, source_target_pairs={{0,8},{8,16},{16,24},{24,0},{1,9},{9,17},{17,25},{25,1},{2,10},{10... | collective-permute-start | bytes 884744 | tf_op jit(solution)/shard_map/ppermute | solution.py:159
  655.1 0.7 copy-start.5
  655.8 1.1 copy-start.2
  656.9 1.1 copy-start.4
  657.9 1.0 copy-start.6
  658.9 4.9 copy-start.12

commit v5 on v4

--- a/solution.py
+++ b/solution.py
@@ -51,32 +51,45 @@
     )(x)
 
 
-def step_kernel(idx_ref, g_ref, *refs):
-    sources, (src_ref, out_ref, send_ref, op_ref, sems) = refs[:5], refs[5:]
-    batch, y0 = idx_ref[0], idx_ref[1]
-    n, depth = op_ref.shape[2], g_ref.shape[0]
+def hold_kernel(idx_ref, own, up, down, two_real, two_imag, real_ref, imag_ref, sems):
+    copies = []
+    for p, (out_ref, two) in enumerate(((real_ref, two_real), (imag_ref, two_imag))):
+        for j, (there, step) in enumerate(((own.at[p], 0), (up.at[p], 3), (down.at[p], 1), (two, 2))):
+            copies.append(pltpu.make_async_copy(there, out_ref.at[(idx_ref[0] + step) % NY], sems.at[p, j]))
+    for copy in copies:
+        copy.start()
+    for copy in copies:
+        copy.wait()
+
+
+def hold(index, *pieces):
+    there = pl.BlockSpec(memory_space=pl.ANY)
+    shape = (NY, *pieces[3].shape)
+    return pl.pallas_call(
+        hold_kernel,
+        in_specs=[pl.BlockSpec(memory_space=pltpu.SMEM)] + [there] * 5,
+        out_specs=[pl.BlockSpec(memory_space=pltpu.VMEM), there],
+        out_shape=[pltpu.VMEM(shape, BF), jax.ShapeDtypeStruct(shape, BF)],
+        scratch_shapes=[pltpu.SemaphoreType.DMA((2, NY))],
+        compiler_params=pltpu.CompilerParams(vmem_limit_bytes=16 * 2**20),
+        name="hold",
+    )(index, *pieces)
+
+
+def step_kernel(idx_ref, g_ref, held_ref, imag_ref, src_ref, _a, _b, send_ref, kept_ref, stored_ref, out_ref, sems):
+    batch, slot = idx_ref[0], idx_ref[1]
+    n, depth = held_ref.shape[1], g_ref.shape[0]
     rows = NY * n
-    own, up, down = sources[:3]
-    copies = [
-        [
-            pltpu.make_async_copy(there, op_ref.at[p, (y0 + step) % NY], sems.at[p, j])
-            for j, (there, step) in enumerate(((own.at[p], 0), (up.at[p], 3), (down.at[p], 1), (sources[3 + p], 2)))
-        ]
-        for p in range(2)
-    ]
-    for group in copies:
-        for copy in group:
-            copy.start()
+    keep = pltpu.make_async_copy(g_ref, stored_ref.at[slot], sems.at[0])
+    keep.start()
     g = g_ref[...]
     blk = block_of((rows, 128))
     small = block_of((n, 128))
     parts = []
-    for p in range(2):
-        for copy in copies[p]:
-            copy.wait()
+    for ref in (held_ref, imag_ref):
         acc = jnp.zeros((rows, 128), F32)
         for q in range(NY):
-            op = op_ref[p, :, :, depth * q : depth * (q + 1)].reshape(rows, depth)
+            op = ref[:, :, depth * q : depth * (q + 1)].reshape(rows, depth)
             acc = jnp.where(blk == q, jnp.dot(op, g, preferred_element_type=F32), acc)
         parts.append(acc)
     d = parts[0] + turn(parts[1])
@@ -88,24 +101,33 @@
     total = total + src_ref[batch]
     out_ref[...] = total
     send_ref[...] = total.astype(BF)
-
-
-def apply_next(index, g, ops, src):
-    n, depth = ops[3].shape
+    note = pltpu.make_async_copy(out_ref, kept_ref.at[slot], sems.at[1])
+    note.start()
+    keep.wait()
+    note.wait()
+
+
+def apply_next(index, g, held, imag, src, kept, stored):
+    _, n, depth = imag.shape
     there = pl.BlockSpec(memory_space=pl.ANY)
     whole = pl.BlockSpec(memory_space=pltpu.VMEM)
     return pl.pallas_call(
         step_kernel,
-        in_specs=[pl.BlockSpec(memory_space=pltpu.SMEM), whole] + [there] * 5 + [whole],
-        out_specs=[whole, whole],
-        scratch_shapes=[pltpu.VMEM((2, NY, n, depth), BF), pltpu.SemaphoreType.DMA((2, NY))],
-        out_shape=[jax.ShapeDtypeStruct((n, 128), F32), jax.ShapeDtypeStruct((n, 128), BF)],
-        compiler_params=pltpu.CompilerParams(vmem_limit_bytes=24 * 2**20),
+        in_specs=[pl.BlockSpec(memory_space=pltpu.SMEM)] + [whole] * 4 + [there] * 2,
+        out_specs=[whole, there, there],
+        scratch_shapes=[pltpu.VMEM((n, 128), F32), pltpu.SemaphoreType.DMA((2,))],
+        out_shape=[
+            jax.ShapeDtypeStruct((n, 128), BF),
+            pltpu.HBM(kept.shape, F32),
+            pltpu.HBM(stored.shape, BF),
+        ],
+        input_output_aliases={5: 1, 6: 2},
+        compiler_params=pltpu.CompilerParams(vmem_limit_bytes=16 * 2**20),
         cost_estimate=pl.CostEstimate(
             flops=4 * NY * n * depth * 128, bytes_accessed=4 * NY * n * depth, transcendentals=0
         ),
         name="apply_next",
-    )(index, g, *ops, src)
+    )(index, g, held, imag, src, kept, stored)
 
 
 def interior_kernel(idx_ref, op_ref, own_ref, up_ref, down_ref, top_ref, bottom_ref, last_ref, out_ref, v_ref):
@@ -166,7 +188,8 @@
     together = lax.optimization_barrier
     op = green_next[0]
     up, down = ring(op, 1), ring(op, -1)
-    ops = [op, up, down, ring(up[0], 1), ring(down[1], -1)]
+    two_real, two_imag = ring(up[0], 1), ring(down[1], -1)
+    held, imag = hold(y.astype(jnp.int32).reshape(1), op, up, down, two_real, two_imag)
     inc = lax.all_to_all(incident.astype(BF), "y", 0, 0, tiled=True)
     src = lax.all_to_all(sources[0], "y", 0, 0, tiled=True)
     inc = swap_blocks(inc, BF)
@@ -176,19 +199,17 @@
     received = jnp.zeros((rows, 128), BF)
     last_step = NS + NB - 2
     for c in range(last_step + 1):
-        entering = jnp.where(s == 0, inc[min(c, NB - 1)], received)
+        entering = jnp.where(s == 0, inc[c], received) if c < NB else received
         g = spread(entering, "zl").reshape(NZ * rows, 128)
         if c == last_step:
             g, up, down = together((g, up, down))
         batch = c - s
-        index = jnp.stack([jnp.clip(batch, 0, NB - 1), y]).astype(jnp.int32)
-        leaving, send = apply_next(index, g, ops, src)
+        slot = jnp.clip(batch + 1, 0, NB + 1)
+        index = jnp.stack([jnp.clip(batch, 0, NB - 1), slot]).astype(jnp.int32)
+        send, kept, stored = apply_next(index, g, held, imag, src, kept, stored)
         if c < last_step:
             pairs = [(a, a + 1) for a in range(NS - 1) if 0 <= c - a < NB]
             received = lax.ppermute(send, "slab", pairs)
-        slot = jnp.clip(batch + 1, 0, NB + 1)
-        stored = lax.dynamic_update_index_in_dim(stored, g, slot, 0)
-        kept = lax.dynamic_update_index_in_dim(kept, leaving, slot, 0)
         if c == last_step - 1:
             early = stored[1:NB]
             up, down = ring(early, 1), ring(early, -1)

time: 678 us -> 648 us (0.956)
  the two profiles are of different devices: /device:TPU:482 before, /device:TPU:486 now
where the time goes in v5:
time: 648 us; the launch traced here: 644 us
  waiting for transfers between devices  257 us (40%)
  starting transfers between devices  249 us (38%)
  Pallas kernels  67 us (10%)
  local copies, waits for them, and re-layouts  65.5 us (10%)
    all_to_all x20, starting transfers between devices, spread(): return lax.all_to_all(copies, axis, split_axis=0, concat_axis=0, tiled=True)  192 us
    all_to_all x20, waiting for transfers between devices, spread(): return lax.all_to_all(copies, axis, split_axis=0, concat_axis=0, tiled=True)  117 us
    ppermute x18, waiting for transfers between devices, local(): received = lax.ppermute(send, 'slab', pairs)  84 us
    pallas_call x19, Pallas kernels, apply_next(): pl.pallas_call(step_kernel, in_specs=[pl.BlockSpec(memory_space=pltpu.SME...  54.5 us
    unnamed x73, local copies, waits for them, and re-layouts  41.7 us
    ppermute x8, waiting for transfers between devices, ring(): return lax.ppermute(x, 'y', [(i, (i + step) % NY) for i in range(NY)])  28.6 us
    ppermute x8, starting transfers between devices, ring(): return lax.ppermute(x, 'y', [(i, (i + step) % NY) for i in range(NY)])  28.2 us
    all_to_all x1, waiting for transfers between devices, local(): inc = lax.all_to_all(incident.astype(BF), 'y', 0, 0, tiled=True)  21.8 us
  transfers between devices with their start and end apart: 49, of which 28 were waited for; matrix products, arithmetic and copies ran while one was open for 2% of the time, Pallas kernels for 1%

profile of v5, /device:TPU:486, one launch (start us, length us, event | category | flops | bytes accessed | tf_op | source)
XLA Modules:
  0.0 643.6 jit_solution(3825977602669803196)
XLA Ops:
  0.6 3.5 collective-permute-start
  4.1 3.6 collective-permute-start.1
  9.3 3.3 all-to-all-start
  12.6 21.8 %all-to-all-done.src_ref = bf16[4,96,128]{2,1,0:T(8,128)(2,1)S(1)} async-done(((bf16[4,96,128]{2,1,0:T(8,128)(2,1)}), bf16[4,96,128]{2,1,0:T(8,128)(2,1)S(1)}, u32[]{:S(2)}, u32[]{:S(2)}) %all-to-all-start) | async-done | bytes 98336 | tf_op jit(solution)/shard_map/all_to_all | solution.py:193
  34.5 4.5 all-to-all-start.2
  42.2 3.9 collective-permute-start.2
  46.9 9.9 %all-to-all-start.1 = ((bf16[8,96,128]{2,1,0:T(8,128)(2,1)}), bf16[8,96,128]{2,1,0:T(8,128)(2,1)}, u32[]{:S(2)}, u32[]{:S(2)}) async-start(bf16[8,96,128]{2,1,0:T(8,128)(2,1)} %broadcast_in_dim.76), calls=%async_computation.1 | async-start | bytes 393216 | tf_op jit(solution)/shard_map/all_to_all | solution.py:177
  57.8 3.1 collective-permute-start.3
  63.6 8.5 %collective-permute-done.3.two_imag = bf16[96,3072]{1,0:T(8,128)(2,1)S(1)} collective-permute-done((bf16[96,3072]{1,0:T(8,128)(2,1)}, bf16[96,3072]{1,0:T(8,128)(2,1)S(1)}, u32[]{:S(2)}, u32[]{:S(2)}) %collective-permute-start.3) | collective-permute-done | bytes 589856 | tf_op jit(solution)/shard_map/ppermute | solution.py:181
  83.7 3.2 apply_next.19
  88.3 9.9 %all-to-all-start.3 = ((bf16[8,96,128]{2,1,0:T(8,128)(2,1)}), bf16[8,96,128]{2,1,0:T(8,128)(2,1)S(1)}, u32[]{:S(2)}, u32[]{:S(2)}) async-start(bf16[8,96,128]{2,1,0:T(8,128)(2,1)} %broadcast_in_dim.79), calls=%async_computation.3 | async-start | bytes 393216 | tf_op jit(solution)/shard_map/all_to_all | solution.py:177
  98.3 6.1 all-to-all-done.3
  110.3 9.9 %all-to-all-start.4 = ((bf16[8,96,128]{2,1,0:T(8,128)(2,1)}), bf16[8,96,128]{2,1,0:T(8,128)(2,1)S(1)}, u32[]{:S(2)}, u32[]{:S(2)}) async-start(bf16[8,96,128]{2,1,0:T(8,128)(2,1)} %broadcast_in_dim.80), calls=%async_computation.4 | async-start | bytes 393216 | tf_op jit(solution)/shard_map/all_to_all | solution.py:177
  120.3 6.1 all-to-all-done.4
  132.4 9.9 %all-to-all-start.5 = ((bf16[8,96,128]{2,1,0:T(8,128)(2,1)}), bf16[8,96,128]{2,1,0:T(8,128)(2,1)S(1)}, u32[]{:S(2)}, u32[]{:S(2)}) async-start(bf16[8,96,128]{2,1,0:T(8,128)(2,1)} %broadcast_in_dim.81), calls=%async_computation.5 | async-start | bytes 393216 | tf_op jit(solution)/shard_map/all_to_all | solution.py:177
  142.3 6.1 all-to-all-done.5
  150.2 2.8 apply_next.22
  154.4 9.9 %all-to-all-start.6 = ((bf16[8,96,128]{2,1,0:T(8,128)(2,1)}), bf16[8,96,128]{2,1,0:T(8,128)(2,1)S(1)}, u32[]{:S(2)}, u32[]{:S(2)}) async-start(bf16[8,96,128]{2,1,0:T(8,128)(2,1)} %broadcast_in_dim.82), calls=%async_computation.6 | async-start | bytes 393216 | tf_op jit(solution)/shard_map/all_to_all | solution.py:177
  164.3 6.1 all-to-all-done.6
  176.4 9.9 %all-to-all-start.7 = ((bf16[8,96,128]{2,1,0:T(8,128)(2,1)}), bf16[8,96,128]{2,1,0:T(8,128)(2,1)S(1)}, u32[]{:S(2)}, u32[]{:S(2)}) async-start(bf16[8,96,128]{2,1,0:T(8,128)(2,1)} %broadcast_in_dim.83), calls=%async_computation.7 | async-start | bytes 393216 | tf_op jit(solution)/shard_map/all_to_all | solution.py:177
  186.3 6.1 all-to-all-done.7
  198.4 9.9 %all-to-all-start.8 = ((bf16[8,96,128]{2,1,0:T(8,128)(2,1)}), bf16[8,96,128]{2,1,0:T(8,128)(2,1)S(1)}, u32[]{:S(2)}, u32[]{:S(2)}) async-start(bf16[8,96,128]{2,1,0:T(8,128)(2,1)} %broadcast_in_dim.84), calls=%async_computation.8 | async-start | bytes 393216 | tf_op jit(solution)/shard_map/all_to_all | solution.py:177
  208.3 6.1 all-to-all-done.8
  220.4 9.9 %all-to-all-start.9 = ((bf16[8,96,128]{2,1,0:T(8,128)(2,1)}), bf16[8,96,128]{2,1,0:T(8,128)(2,1)S(1)}, u32[]{:S(2)}, u32[]{:S(2)}) async-start(bf16[8,96,128]{2,1,0:T(8,128)(2,1)} %broadcast_in_dim.85), calls=%async_computation.9 | async-start | bytes 393216 | tf_op jit(solution)/shard_map/all_to_all | solution.py:177
  230.3 6.1 all-to-all-done.9
  242.4 9.9 %all-to-all-start.10 = ((bf16[8,96,128]{2,1,0:T(8,128)(2,1)}), bf16[8,96,128]{2,1,0:T(8,128)(2,1)S(1)}, u32[]{:S(2)}, u32[]{:S(2)}) async-start(bf16[8,96,128]{2,1,0:T(8,128)(2,1)} %broadcast_in_dim.86), calls=%async_computation.10 | async-start | bytes 393216 | tf_op jit(solution)/shard_map/all_to_all | solution.py:177
  252.3 6.1 all-to-all-done.10
  264.4 9.9 %all-to-all-start.11 = ((bf16[8,96,128]{2,1,0:T(8,128)(2,1)}), bf16[8,96,128]{2,1,0:T(8,128)(2,1)S(1)}, u32[]{:S(2)}, u32[]{:S(2)}) async-start(bf16[8,96,128]{2,1,0:T(8,128)(2,1)} %broadcast_in_dim.87), calls=%async_computation.11 | async-start | bytes 393216 | tf_op jit(solution)/shard_map/all_to_all | solution.py:177
  274.3 6.1 all-to-all-done.11
  282.2 2.8 apply_next.28
  286.4 9.9 %all-to-all-start.12 = ((bf16[8,96,128]{2,1,0:T(8,128)(2,1)}), bf16[8,96,128]{2,1,0:T(8,128)(2,1)S(1)}, u32[]{:S(2)}, u32[]{:S(2)}) async-start(bf16[8,96,128]{2,1,0:T(8,128)(2,1)} %broadcast_in_dim.88), calls=%async_computation.12 | async-start | bytes 393216 | tf_op jit(solution)/shard_map/all_to_all | solution.py:177
  296.3 9.9 %all-to-all-done.12 = bf16[8,96,128]{2,1,0:T(8,128)(2,1)S(1)} async-done(((bf16[8,96,128]{2,1,0:T(8,128)(2,1)}), bf16[8,96,128]{2,1,0:T(8,128)(2,1)S(1)}, u32[]{:S(2)}, u32[]{:S(2)}) %all-to-all-start.12) | async-done | bytes 196640 | tf_op jit(solution)/shard_map/all_to_all | solution.py:177
  312.1 9.9 %all-to-all-start.13 = ((bf16[8,96,128]{2,1,0:T(8,128)(2,1)}), bf16[8,96,128]{2,1,0:T(8,128)(2,1)S(1)}, u32[]{:S(2)}, u32[]{:S(2)}) async-start(bf16[8,96,128]{2,1,0:T(8,128)(2,1)} %broadcast_in_dim.89), calls=%async_computation.13 | async-start | bytes 393216 | tf_op jit(solution)/shard_map/all_to_all | solution.py:177
  322.1 9.4 %all-to-all-done.13 = bf16[8,96,128]{2,1,0:T(8,128)(2,1)S(1)} async-done(((bf16[8,96,128]{2,1,0:T(8,128)(2,1)}), bf16[8,96,128]{2,1,0:T(8,128)(2,1)S(1)}, u32[]{:S(2)}, u32[]{:S(2)}) %all-to-all-start.13) | async-done | bytes 196640 | tf_op jit(solution)/shard_map/all_to_all | solution.py:177
  333.2 2.8 apply_next.30
  337.4 9.9 %all-to-all-start.14 = ((bf16[8,96,128]{2,1,0:T(8,128)(2,1)}), bf16[8,96,128]{2,1,0:T(8,128)(2,1)S(1)}, u32[]{:S(2)}, u32[]{:S(2)}) async-start(bf16[8,96,128]{2,1,0:T(8,128)(2,1)} %broadcast_in_dim.90), calls=%async_computation.14 | async-start | bytes 393216 | tf_op jit(solution)/shard_map/all_to_all | solution.py:177
  347.4 9.2 %all-to-all-done.14 = bf16[8,96,128]{2,1,0:T(8,128)(2,1)S(1)} async-done(((bf16[8,96,128]{2,1,0:T(8,128)(2,1)}), bf16[8,96,128]{2,1,0:T(8,128)(2,1)S(1)}, u32[]{:S(2)}, u32[]{:S(2)}) %all-to-all-start.14) | async-done | bytes 196640 | tf_op jit(solution)/shard_map/all_to_all | solution.py:177
  362.5 9.9 %all-to-all-start.15 = ((bf16[8,96,128]{2,1,0:T(8,128)(2,1)}), bf16[8,96,128]{2,1,0:T(8,128)(2,1)S(1)}, u32[]{:S(2)}, u32[]{:S(2)}) async-start(bf16[8,96,128]{2,1,0:T(8,128)(2,1)} %broadcast_in_dim.91), calls=%async_computation.15 | async-start | bytes 393216 | tf_op jit(solution)/shard_map/all_to_all | solution.py:177
  372.4 8.7 %all-to-all-done.15 = bf16[8,96,128]{2,1,0:T(8,128)(2,1)S(1)} async-done(((bf16[8,96,128]{2,1,0:T(8,128)(2,1)}), bf16[8,96,128]{2,1,0:T(8,128)(2,1)S(1)}, u32[]{:S(2)}, u32[]{:S(2)}) %all-to-all-start.15) | async-done | bytes 196640 | tf_op jit(solution)/shard_map/all_to_all | solution.py:177
  386.9 31.7 %collective-permute-done.17 = bf16[96,128]{1,0:T(8,128)(2,1)S(1)} collective-permute-done((bf16[96,128]{1,0:T(8,128)(2,1)S(1)}, bf16[96,128]{1,0:T(8,128)(2,1)S(1)}, u32[]{:S(2)}, u32[]{:S(2)}) %collective-permute-start.17) | collective-permute-done | bytes 24608 | tf_op jit(solution)/shard_map/ppermute | solution.py:212
  419.4 9.9 %all-to-all-start.16 = ((bf16[8,96,128]{2,1,0:T(8,128)(2,1)}), bf16[8,96,128]{2,1,0:T(8,128)(2,1)S(1)}, u32[]{:S(2)}, u32[]{:S(2)}) async-start(bf16[8,96,128]{2,1,0:T(8,128)(2,1)} %broadcast_in_dim.92), calls=%async_computation.16 | async-start | bytes 393216 | tf_op jit(solution)/shard_map/all_to_all | solution.py:177
  429.3 6.1 all-to-all-done.16
  441.9 14.0 %collective-permute-done.18 = bf16[96,128]{1,0:T(8,128)(2,1)S(1)} collective-permute-done((bf16[96,128]{1,0:T(8,128)(2,1)S(1)}, bf16[96,128]{1,0:T(8,128)(2,1)S(1)}, u32[]{:S(2)}, u32[]{:S(2)}) %collective-permute-start.18) | collective-permute-done | bytes 24608 | tf_op jit(solution)/shard_map/ppermute | solution.py:212
  456.7 9.9 %all-to-all-start.17 = ((bf16[8,96,128]{2,1,0:T(8,128)(2,1)}), bf16[8,96,128]{2,1,0:T(8,128)(2,1)S(1)}, u32[]{:S(2)}, u32[]{:S(2)}) async-start(bf16[8,96,128]{2,1,0:T(8,128)(2,1)} %broadcast_in_dim.93), calls=%async_computation.17 | async-start | bytes 393216 | tf_op jit(solution)/shard_map/all_to_all | solution.py:177
  466.6 6.1 all-to-all-done.17
  479.2 14.2 %collective-permute-done.19 = bf16[96,128]{1,0:T(8,128)(2,1)S(1)} collective-permute-done((bf16[96,128]{1,0:T(8,128)(2,1)S(1)}, bf16[96,128]{1,0:T(8,128)(2,1)S(1)}, u32[]{:S(2)}, u32[]{:S(2)}) %collective-permute-start.19) | collective-permute-done | bytes 24608 | tf_op jit(solution)/shard_map/ppermute | solution.py:212
  494.1 9.9 %all-to-all-start.18 = ((bf16[8,96,128]{2,1,0:T(8,128)(2,1)}), bf16[8,96,128]{2,1,0:T(8,128)(2,1)S(1)}, u32[]{:S(2)}, u32[]{:S(2)}) async-start(bf16[8,96,128]{2,1,0:T(8,128)(2,1)} %broadcast_in_dim.94), calls=%async_computation.18 | async-start | bytes 393216 | tf_op jit(solution)/shard_map/all_to_all | solution.py:177
  504.1 6.1 all-to-all-done.18
  511.9 2.8 apply_next.35
  516.7 23.1 %collective-permute-done.20 = bf16[96,128]{1,0:T(8,128)(2,1)S(1)} collective-permute-done((bf16[96,128]{1,0:T(8,128)(2,1)S(1)}, bf16[96,128]{1,0:T(8,128)(2,1)S(1)}, u32[]{:S(2)}, u32[]{:S(2)}) %collective-permute-start.20) | collective-permute-done | bytes 24608 | tf_op jit(solution)/shard_map/ppermute | solution.py:212
  540.5 9.9 %all-to-all-start.19 = ((bf16[8,96,128]{2,1,0:T(8,128)(2,1)}), bf16[8,96,128]{2,1,0:T(8,128)(2,1)S(1)}, u32[]{:S(2)}, u32[]{:S(2)}) async-start(bf16[8,96,128]{2,1,0:T(8,128)(2,1)} %broadcast_in_dim.95), calls=%async_computation.19 | async-start | bytes 393216 | tf_op jit(solution)/shard_map/all_to_all | solution.py:177
  550.4 6.1 all-to-all-done.19
  563.9 9.9 %all-to-all-start.20 = ((bf16[8,96,128]{2,1,0:T(8,128)(2,1)}), bf16[8,96,128]{2,1,0:T(8,128)(2,1)S(1)}, u32[]{:S(2)}, u32[]{:S(2)}) async-start(bf16[8,96,128]{2,1,0:T(8,128)(2,1)} %broadcast_in_dim.96), calls=%async_computation.20 | async-start | bytes 393216 | tf_op jit(solution)/shard_map/all_to_all | solution.py:177
  574.9 3.4 collective-permute-start.22
  578.3 3.7 collective-permute-start.23
  582.1 11.1 %collective-permute-done.22.up_ref = bf16[3,768,128]{2,1,0:T(8,128)(2,1)} collective-permute-done((bf16[3,768,128]{2,1,0:T(8,128)(2,1)S(1)}, bf16[3,768,128]{2,1,0:T(8,128)(2,1)}, u32[]{:S(2)}, u32[]{:S(2)}) %collective-permute-start.22) | collective-permute-done | bytes 589856 | tf_op jit(solution)/shard_map/ppermute | solution.py:181
  596.7 3.4 apply_next.37
  603.6 4.3 all-to-all-start.22
  608.8 5.4 all-to-all-done.22
  615.2 3.6 all-to-all-start.21
  619.8 3.9 collective-permute-start.24
  624.7 3.2 collective-permute-start.25
  627.9 7.1 %collective-permute-done.24.top_ref = bf16[3,384,128]{2,1,0:T(8,128)(2,1)S(1)} collective-permute-done((bf16[3,384,128]{2,1,0:T(8,128)(2,1)S(1)}, bf16[3,384,128]{2,1,0:T(8,128)(2,1)S(1)}, u32[]{:S(2)}, u32[]{:S(2)}) %collective-permute-start.24) | collective-permute-done | bytes 294944 | tf_op jit(solution)/shard_map/ppermute | solution.py:181
  636.7 6.2 apply_interior.1
  (184 shorter events, 131.9 us)
Async XLA Ops:
  0.6 40.7 %collective-permute-start = (bf16[2,96,3072]{2,1,0:T(8,128)(2,1)}, bf16[2,96,3072]{2,1,0:T(8,128)(2,1)S(1)}, u32[]{:S(2)}, u32[]{:S(2)}) collective-permute-start(bf16[2,96,3072]{2,1,0:T(8,128)(2,1)} %bitcast.84), channel_id=1, source_target_pairs={{0,8},{8,16},{16,24},{24,0},{1,9},{9,17},{17,25},{25,1},{2,10},{10... | collective-permute-start | bytes 3538952 | tf_op jit(solution)/shard_map/ppermute | solution.py:181
  4.1 52.7 %collective-permute-start.1 = (bf16[2,96,3072]{2,1,0:T(8,128)(2,1)}, bf16[2,96,3072]{2,1,0:T(8,128)(2,1)S(1)}, u32[]{:S(2)}, u32[]{:S(2)}) collective-permute-start(bf16[2,96,3072]{2,1,0:T(8,128)(2,1)} %bitcast.85), channel_id=1, source_target_pairs={{0,24},{8,0},{16,8},{24,16},{1,25},{9,1},{17,9},{25,17},{2,26},{10... | collective-permute-start | bytes 3538952 | tf_op jit(solution)/shard_map/ppermute | solution.py:181
  9.3 25.2 %all-to-all-start = ((bf16[4,96,128]{2,1,0:T(8,128)(2,1)}), bf16[4,96,128]{2,1,0:T(8,128)(2,1)S(1)}, u32[]{:S(2)}, u32[]{:S(2)}) async-start(bf16[4,96,128]{2,1,0:T(8,128)(2,1)} %convert_element_type.3), calls=%async_computation | async-start | bytes 196608 | tf_op jit(solution)/shard_map/all_to_all | solution.py:193
  34.4 4.5 copy-start.35
  34.5 11.7 %all-to-all-start.2 = ((f32[4,96,128]{2,1,0:T(8,128)}), f32[4,96,128]{2,1,0:T(8,128)S(1)}, u32[]{:S(2)}, u32[]{:S(2)}) async-start(f32[4,96,128]{2,1,0:T(8,128)} %bitcast.107), calls=%async_computation.2 | async-start | bytes 393216 | tf_op jit(solution)/shard_map/all_to_all | solution.py:194
  42.2 20.6 %collective-permute-start.2 = (bf16[96,3072]{1,0:T(8,128)(2,1)}, bf16[96,3072]{1,0:T(8,128)(2,1)S(1)}, u32[]{:S(2)}, u32[]{:S(2)}) collective-permute-start(bf16[96,3072]{1,0:T(8,128)(2,1)} %slice_bitcast_fusion.1), channel_id=1, source_target_pairs={{0,8},{8,16},{16,24},{24,0},{1,9},{9,17},{17,25},{25,1},{2,10},{10... | collective-permute-start | bytes 1769480 | tf_op jit(solution)/shard_map/ppermute | solution.py:181
  46.2 10.7 %copy-start.31 = (f32[4,96,128]{2,1,0:T(8,128)}, f32[4,96,128]{2,1,0:T(8,128)S(1)}, u32[]{:S(2)}) copy-start(f32[4,96,128]{2,1,0:T(8,128)S(1)} %all-to-all-done.2.src_ref) | copy-start | bytes 589828
  46.9 33.2 %all-to-all-start.1 = ((bf16[8,96,128]{2,1,0:T(8,128)(2,1)}), bf16[8,96,128]{2,1,0:T(8,128)(2,1)}, u32[]{:S(2)}, u32[]{:S(2)}) async-start(bf16[8,96,128]{2,1,0:T(8,128)(2,1)} %broadcast_in_dim.76), calls=%async_computation.1 | async-start | bytes 393216 | tf_op jit(solution)/shard_map/all_to_all | solution.py:177
  56.8 15.3 %copy-start.21 = (bf16[2,96,3072]{2,1,0:T(8,128)(2,1)}, bf16[2,96,3072]{2,1,0:T(8,128)(2,1)S(1)}, u32[]{:S(2)}) copy-start(bf16[2,96,3072]{2,1,0:T(8,128)(2,1)S(1)} %collective-permute-done.1.down) | copy-start | bytes 3538948
  57.8 14.4 %collective-permute-start.3 = (bf16[96,3072]{1,0:T(8,128)(2,1)}, bf16[96,3072]{1,0:T(8,128)(2,1)S(1)}, u32[]{:S(2)}, u32[]{:S(2)}) collective-permute-start(bf16[96,3072]{1,0:T(8,128)(2,1)} %slice_bitcast_fusion), channel_id=1, source_target_pairs={{0,24},{8,0},{16,8},{24,16},{1,25},{9,1},{17,9},{25,17},{2,26},{10... | collective-permute-start | bytes 1769480 | tf_op jit(solution)/shard_map/ppermute | solution.py:181
  80.1 1.9 copy-start.20
  83.7 3.9 copy-start.34
  86.9 0.7 collective-permute-start.4
  88.3 16.1 %all-to-all-start.3 = ((bf16[8,96,128]{2,1,0:T(8,128)(2,1)}), bf16[8,96,128]{2,1,0:T(8,128)(2,1)S(1)}, u32[]{:S(2)}, u32[]{:S(2)}) async-start(bf16[8,96,128]{2,1,0:T(8,128)(2,1)} %broadcast_in_dim.79), calls=%async_computation.3 | async-start | bytes 393216 | tf_op jit(solution)/shard_map/all_to_all | solution.py:177
  104.5 1.7 copy-start.2
  108.9 0.7 collective-permute-start.5
  110.3 16.1 %all-to-all-start.4 = ((bf16[8,96,128]{2,1,0:T(8,128)(2,1)}), bf16[8,96,128]{2,1,0:T(8,128)(2,1)S(1)}, u32[]{:S(2)}, u32[]{:S(2)}) async-start(bf16[8,96,128]{2,1,0:T(8,128)(2,1)} %broadcast_in_dim.80), calls=%async_computation.4 | async-start | bytes 393216 | tf_op jit(solution)/shard_map/all_to_all | solution.py:177
  126.5 1.7 copy-start.3
  131.0 0.7 collective-permute-start.6
  132.4 16.1 %all-to-all-start.5 = ((bf16[8,96,128]{2,1,0:T(8,128)(2,1)}), bf16[8,96,128]{2,1,0:T(8,128)(2,1)S(1)}, u32[]{:S(2)}, u32[]{:S(2)}) async-start(bf16[8,96,128]{2,1,0:T(8,128)(2,1)} %broadcast_in_dim.81), calls=%async_computation.5 | async-start | bytes 393216 | tf_op jit(solution)/shard_map/all_to_all | solution.py:177
  148.5 1.7 copy-start.4
  153.0 0.7 collective-permute-start.7
  154.4 16.1 %all-to-all-start.6 = ((bf16[8,96,128]{2,1,0:T(8,128)(2,1)}), bf16[8,96,128]{2,1,0:T(8,128)(2,1)S(1)}, u32[]{:S(2)}, u32[]{:S(2)}) async-start(bf16[8,96,128]{2,1,0:T(8,128)(2,1)} %broadcast_in_dim.82), calls=%async_computation.6 | async-start | bytes 393216 | tf_op jit(solution)/shard_map/all_to_all | solution.py:177
  170.5 1.7 copy-start.5
  175.0 0.7 collective-permute-start.8
  176.4 16.1 %all-to-all-start.7 = ((bf16[8,96,128]{2,1,0:T(8,128)(2,1)}), bf16[8,96,128]{2,1,0:T(8,128)(2,1)S(1)}, u32[]{:S(2)}, u32[]{:S(2)}) async-start(bf16[8,96,128]{2,1,0:T(8,128)(2,1)} %broadcast_in_dim.83), calls=%async_computation.7 | async-start | bytes 393216 | tf_op jit(solution)/shard_map/all_to_all | solution.py:177
  197.0 0.7 collective-permute-start.9
  198.4 16.1 %all-to-all-start.8 = ((bf16[8,96,128]{2,1,0:T(8,128)(2,1)}), bf16[8,96,128]{2,1,0:T(8,128)(2,1)S(1)}, u32[]{:S(2)}, u32[]{:S(2)}) async-start(bf16[8,96,128]{2,1,0:T(8,128)(2,1)} %broadcast_in_dim.84), calls=%async_computation.8 | async-start | bytes 393216 | tf_op jit(solution)/shard_map/all_to_all | solution.py:177
  219.0 0.7 collective-permute-start.10
  220.4 16.1 %all-to-all-start.9 = ((bf16[8,96,128]{2,1,0:T(8,128)(2,1)}), bf16[8,96,128]{2,1,0:T(8,128)(2,1)S(1)}, u32[]{:S(2)}, u32[]{:S(2)}) async-start(bf16[8,96,128]{2,1,0:T(8,128)(2,1)} %broadcast_in_dim.85), calls=%async_computation.9 | async-start | bytes 393216 | tf_op jit(solution)/shard_map/all_to_all | solution.py:177
  241.0 0.7 collective-permute-start.11
  242.4 16.1 %all-to-all-start.10 = ((bf16[8,96,128]{2,1,0:T(8,128)(2,1)}), bf16[8,96,128]{2,1,0:T(8,128)(2,1)S(1)}, u32[]{:S(2)}, u32[]{:S(2)}) async-start(bf16[8,96,128]{2,1,0:T(8,128)(2,1)} %broadcast_in_dim.86), calls=%async_computation.10 | async-start | bytes 393216 | tf_op jit(solution)/shard_map/all_to_all | solution.py:177
  263.0 0.7 collective-permute-start.12
  264.4 16.1 %all-to-all-start.11 = ((bf16[8,96,128]{2,1,0:T(8,128)(2,1)}), bf16[8,96,128]{2,1,0:T(8,128)(2,1)S(1)}, u32[]{:S(2)}, u32[]{:S(2)}) async-start(bf16[8,96,128]{2,1,0:T(8,128)(2,1)} %broadcast_in_dim.87), calls=%async_computation.11 | async-start | bytes 393216 | tf_op jit(solution)/shard_map/all_to_all | solution.py:177
  285.0 0.7 collective-permute-start.13
  286.4 19.9 %all-to-all-start.12 = ((bf16[8,96,128]{2,1,0:T(8,128)(2,1)}), bf16[8,96,128]{2,1,0:T(8,128)(2,1)S(1)}, u32[]{:S(2)}, u32[]{:S(2)}) async-start(bf16[8,96,128]{2,1,0:T(8,128)(2,1)} %broadcast_in_dim.88), calls=%async_computation.12 | async-start | bytes 393216 | tf_op jit(solution)/shard_map/all_to_all | solution.py:177
  310.8 0.7 collective-permute-start.14
  312.1 19.4 %all-to-all-start.13 = ((bf16[8,96,128]{2,1,0:T(8,128)(2,1)}), bf16[8,96,128]{2,1,0:T(8,128)(2,1)S(1)}, u32[]{:S(2)}, u32[]{:S(2)}) async-start(bf16[8,96,128]{2,1,0:T(8,128)(2,1)} %broadcast_in_dim.89), calls=%async_computation.13 | async-start | bytes 393216 | tf_op jit(solution)/shard_map/all_to_all | solution.py:177
  331.5 1.7 copy-start.12
  336.0 0.7 collective-permute-start.15
  337.4 19.2 %all-to-all-start.14 = ((bf16[8,96,128]{2,1,0:T(8,128)(2,1)}), bf16[8,96,128]{2,1,0:T(8,128)(2,1)S(1)}, u32[]{:S(2)}, u32[]{:S(2)}) async-start(bf16[8,96,128]{2,1,0:T(8,128)(2,1)} %broadcast_in_dim.90), calls=%async_computation.14 | async-start | bytes 393216 | tf_op jit(solution)/shard_map/all_to_all | solution.py:177
  361.1 0.7 collective-permute-start.16
  362.5 18.7 %all-to-all-start.15 = ((bf16[8,96,128]{2,1,0:T(8,128)(2,1)}), bf16[8,96,128]{2,1,0:T(8,128)(2,1)S(1)}, u32[]{:S(2)}, u32[]{:S(2)}) async-start(bf16[8,96,128]{2,1,0:T(8,128)(2,1)} %broadcast_in_dim.91), calls=%async_computation.15 | async-start | bytes 393216 | tf_op jit(solution)/shard_map/all_to_all | solution.py:177
  385.6 33.0 %collective-permute-start.17 = (bf16[96,128]{1,0:T(8,128)(2,1)S(1)}, bf16[96,128]{1,0:T(8,128)(2,1)S(1)}, u32[]{:S(2)}, u32[]{:S(2)}) collective-permute-start(bf16[96,128]{1,0:T(8,128)(2,1)S(1)} %get-tuple-element.104), channel_id=1, source_target_pairs={{320,352},{352,384},{384,416},{416,448},{321,353},{353,385},{385,4... | collective-permute-start | bytes 73736 | tf_op jit(solution)/shard_map/ppermute | solution.py:212
  419.4 16.1 %all-to-all-start.16 = ((bf16[8,96,128]{2,1,0:T(8,128)(2,1)}), bf16[8,96,128]{2,1,0:T(8,128)(2,1)S(1)}, u32[]{:S(2)}, u32[]{:S(2)}) async-start(bf16[8,96,128]{2,1,0:T(8,128)(2,1)} %broadcast_in_dim.92), calls=%async_computation.16 | async-start | bytes 393216 | tf_op jit(solution)/shard_map/all_to_all | solution.py:177
  440.0 16.0 %collective-permute-start.18 = (bf16[96,128]{1,0:T(8,128)(2,1)S(1)}, bf16[96,128]{1,0:T(8,128)(2,1)S(1)}, u32[]{:S(2)}, u32[]{:S(2)}) collective-permute-start(bf16[96,128]{1,0:T(8,128)(2,1)S(1)} %get-tuple-element.107), channel_id=1, source_target_pairs={{352,384},{384,416},{416,448},{448,480},{353,385},{385,417},{417,4... | collective-permute-start | bytes 73736 | tf_op jit(solution)/shard_map/ppermute | solution.py:212
  456.7 16.1 %all-to-all-start.17 = ((bf16[8,96,128]{2,1,0:T(8,128)(2,1)}), bf16[8,96,128]{2,1,0:T(8,128)(2,1)S(1)}, u32[]{:S(2)}, u32[]{:S(2)}) async-start(bf16[8,96,128]{2,1,0:T(8,128)(2,1)} %broadcast_in_dim.93), calls=%async_computation.17 | async-start | bytes 393216 | tf_op jit(solution)/shard_map/all_to_all | solution.py:177
  477.3 16.2 %collective-permute-start.19 = (bf16[96,128]{1,0:T(8,128)(2,1)S(1)}, bf16[96,128]{1,0:T(8,128)(2,1)S(1)}, u32[]{:S(2)}, u32[]{:S(2)}) collective-permute-start(bf16[96,128]{1,0:T(8,128)(2,1)S(1)} %get-tuple-element.110), channel_id=1, source_target_pairs={{384,416},{416,448},{448,480},{385,417},{417,449},{449,481},{386,4... | collective-permute-start | bytes 73736 | tf_op jit(solution)/shard_map/ppermute | solution.py:212
  494.1 16.1 %all-to-all-start.18 = ((bf16[8,96,128]{2,1,0:T(8,128)(2,1)}), bf16[8,96,128]{2,1,0:T(8,128)(2,1)S(1)}, u32[]{:S(2)}, u32[]{:S(2)}) async-start(bf16[8,96,128]{2,1,0:T(8,128)(2,1)} %broadcast_in_dim.94), calls=%async_computation.18 | async-start | bytes 393216 | tf_op jit(solution)/shard_map/all_to_all | solution.py:177
  510.3 1.7 copy-start.17
  514.8 25.0 %collective-permute-start.20 = (bf16[96,128]{1,0:T(8,128)(2,1)S(1)}, bf16[96,128]{1,0:T(8,128)(2,1)S(1)}, u32[]{:S(2)}, u32[]{:S(2)}) collective-permute-start(bf16[96,128]{1,0:T(8,128)(2,1)S(1)} %get-tuple-element.113), channel_id=1, source_target_pairs={{416,448},{448,480},{417,449},{449,481},{418,450},{450,482},{419,4... | collective-permute-start | bytes 73736 | tf_op jit(solution)/shard_map/ppermute | solution.py:212
  540.5 16.1 %all-to-all-start.19 = ((bf16[8,96,128]{2,1,0:T(8,128)(2,1)}), bf16[8,96,128]{2,1,0:T(8,128)(2,1)S(1)}, u32[]{:S(2)}, u32[]{:S(2)}) async-start(bf16[8,96,128]{2,1,0:T(8,128)(2,1)} %broadcast_in_dim.95), calls=%async_computation.19 | async-start | bytes 393216 | tf_op jit(solution)/shard_map/all_to_all | solution.py:177
  556.6 1.7 copy-start.18
  561.1 2.1 collective-permute-start.21
  563.9 31.1 %all-to-all-start.20 = ((bf16[8,96,128]{2,1,0:T(8,128)(2,1)}), bf16[8,96,128]{2,1,0:T(8,128)(2,1)S(1)}, u32[]{:S(2)}, u32[]{:S(2)}) async-start(bf16[8,96,128]{2,1,0:T(8,128)(2,1)} %broadcast_in_dim.96), calls=%async_computation.20 | async-start | bytes 393216 | tf_op jit(solution)/shard_map/all_to_all | solution.py:177
  574.9 18.2 %collective-permute-start.22 = (bf16[3,768,128]{2,1,0:T(8,128)(2,1)S(1)}, bf16[3,768,128]{2,1,0:T(8,128)(2,1)}, u32[]{:S(2)}, u32[]{:S(2)}) collective-permute-start(bf16[3,768,128]{2,1,0:T(8,128)(2,1)S(1)} %slice.39.own_ref), channel_id=1, source_target_pairs={{0,8},{8,16},{16,24},{24,0},{1,9},{9,17},{17,25},{25,1},{2,10},{10... | collective-permute-start | bytes 1769480 | tf_op jit(solution)/shard_map/ppermute | solution.py:181
  578.3 16.7 %collective-permute-start.23 = (bf16[3,768,128]{2,1,0:T(8,128)(2,1)S(1)}, bf16[3,768,128]{2,1,0:T(8,128)(2,1)}, u32[]{:S(2)}, u32[]{:S(2)}) collective-permute-start(bf16[3,768,128]{2,1,0:T(8,128)(2,1)S(1)} %slice.39.own_ref), channel_id=1, source_target_pairs={{0,24},{8,0},{16,8},{24,16},{1,25},{9,1},{17,9},{25,17},{2,26},{10... | collective-permute-start | bytes 1769480 | tf_op jit(solution)/shard_map/ppermute | solution.py:181
  595.0 1.7 copy-start.19
  603.6 10.6 %all-to-all-start.22 = ((f32[4,96,128]{2,1,0:T(8,128)}), f32[4,96,128]{2,1,0:T(8,128)S(1)}, u32[]{:S(2)}, u32[]{:S(2)}) async-start(f32[4,96,128]{2,1,0:T(8,128)} %swap_blocks.5), calls=%async_computation.22 | async-start | bytes 393216 | tf_op jit(solution)/shard_map/all_to_all | solution.py:220
  615.2 20.5 %copy-start.23 = (bf16[1,2,144,3072]{3,2,1,0:T(8,128)(2,1)S(1)}, bf16[1,2,144,3072]{3,2,1,0:T(8,128)(2,1)}, u32[]{:S(2)}) copy-start(bf16[1,2,144,3072]{3,2,1,0:T(8,128)(2,1)} %param.5) | copy-start | bytes 5308420
  615.2 20.5 %all-to-all-start.21 = ((bf16[4,768,128]{2,1,0:T(8,128)(2,1)}), bf16[4,768,128]{2,1,0:T(8,128)(2,1)S(1)}, u32[]{:S(2)}, u32[]{:S(2)}) async-start(bf16[4,768,128]{2,1,0:T(8,128)(2,1)} %broadcast_in_dim.97), calls=%async_computation.21 | async-start | bytes 1572864 | tf_op jit(solution)/shard_map/all_to_all | solution.py:177
  619.8 15.2 %collective-permute-start.24 = (bf16[3,384,128]{2,1,0:T(8,128)(2,1)S(1)}, bf16[3,384,128]{2,1,0:T(8,128)(2,1)S(1)}, u32[]{:S(2)}, u32[]{:S(2)}) collective-permute-start(bf16[3,384,128]{2,1,0:T(8,128)(2,1)S(1)} %slice.40), channel_id=1, source_target_pairs={{0,8},{8,16},{16,24},{24,0},{1,9},{9,17},{17,25},{25,1},{2,10},{10... | collective-permute-start | bytes 884744 | tf_op jit(solution)/shard_map/ppermute | solution.py:181
  624.7 10.3 %collective-permute-start.25 = (bf16[3,384,128]{2,1,0:T(8,128)(2,1)S(1)}, bf16[3,384,128]{2,1,0:T(8,128)(2,1)S(1)}, u32[]{:S(2)}, u32[]{:S(2)}) collective-permute-start(bf16[3,384,128]{2,1,0:T(8,128)(2,1)S(1)} %slice.41), channel_id=1, source_target_pairs={{0,24},{8,0},{16,8},{24,16},{1,25},{9,1},{17,9},{25,17},{2,26},{10... | collective-permute-start | bytes 884744 | tf_op jit(solution)/shard_map/ppermute | solution.py:181
  636.7 6.2 copy-start.33
  (21 other events, 28.7 us)

commit v6 on v5

--- a/solution.py
+++ b/solution.py
@@ -188,11 +188,12 @@
     together = lax.optimization_barrier
     op = green_next[0]
     up, down = ring(op, 1), ring(op, -1)
+    inc = lax.all_to_all(incident.astype(BF), "y", 0, 0, tiled=True)
+    inc = swap_blocks(inc, BF)
+    up, down, inc, sources = together((up, down, inc, sources))
     two_real, two_imag = ring(up[0], 1), ring(down[1], -1)
     held, imag = hold(y.astype(jnp.int32).reshape(1), op, up, down, two_real, two_imag)
-    inc = lax.all_to_all(incident.astype(BF), "y", 0, 0, tiled=True)
     src = lax.all_to_all(sources[0], "y", 0, 0, tiled=True)
-    inc = swap_blocks(inc, BF)
     src = swap_blocks(src, F32)
     stored = jnp.zeros((NB + 2, NZ * rows, 128), BF)
     kept = jnp.zeros((NB + 2, rows, 128), F32)
@@ -216,6 +217,7 @@
     half = NZ * rows // 2
     top, bottom = ring(up[:, :half], 1), ring(down[:, half:], -1)
     last = spread(stored[NB], "y")
+    kept, last = together((kept, last))
     traces = swap_blocks(kept[1 : NB + 1], F32)
     traces = lax.all_to_all(traces, "y", 0, 0, tiled=True)
     sets = (early, up, down, top, bottom, last)

time: 648 us -> 651 us (level)
  the two profiles are of different devices: /device:TPU:486 before, /device:TPU:494 now
where the time goes in v6:
time: 651 us; the launch traced here: 647 us
  starting transfers between devices  255 us (39%)
  waiting for transfers between devices  254 us (39%)
  Pallas kernels  67.1 us (10%)
  local copies, waits for them, and re-layouts  66.9 us (10%)
    all_to_all x20, starting transfers between devices, spread(): return lax.all_to_all(copies, axis, split_axis=0, concat_axis=0, tiled=True)  195 us
    all_to_all x20, waiting for transfers between devices, spread(): return lax.all_to_all(copies, axis, split_axis=0, concat_axis=0, tiled=True)  117 us
    ppermute x18, waiting for transfers between devices, local(): received = lax.ppermute(send, 'slab', pairs)  83.9 us
    pallas_call x19, Pallas kernels, apply_next(): pl.pallas_call(step_kernel, in_specs=[pl.BlockSpec(memory_space=pltpu.SME...  54.5 us
    unnamed x65, local copies, waits for them, and re-layouts  41.6 us
    ppermute x8, starting transfers between devices, ring(): return lax.ppermute(x, 'y', [(i, (i + step) % NY) for i in range(NY)])  24.7 us
    all_to_all x1, waiting for transfers between devices, local(): inc = lax.all_to_all(incident.astype(BF), 'y', 0, 0, tiled=True)  22.4 us
    ppermute x8, waiting for transfers between devices, ring(): return lax.ppermute(x, 'y', [(i, (i + step) % NY) for i in range(NY)])  20.9 us
  transfers between devices with their start and end apart: 49, of which 28 were waited for; matrix products, arithmetic and copies ran while one was open for 2% of the time, Pallas kernels for 2%

profile of v6, /device:TPU:494, one launch (start us, length us, event | category | flops | bytes accessed | tf_op | source)
XLA Modules:
  0.0 647.4 jit_solution(5714430922057872210)
XLA Ops:
  0.6 3.5 collective-permute-start
  8.1 4.9 all-to-all-start
  13.0 22.4 %all-to-all-done.src_ref = bf16[4,96,128]{2,1,0:T(8,128)(2,1)S(1)} async-done(((bf16[4,96,128]{2,1,0:T(8,128)(2,1)}), bf16[4,96,128]{2,1,0:T(8,128)(2,1)S(1)}, u32[]{:S(2)}, u32[]{:S(2)}) %all-to-all-start) | async-done | bytes 98336 | tf_op jit(solution)/shard_map/all_to_all | solution.py:191
  40.9 5.1 all-to-all-start.2
  46.7 9.2 %all-to-all-done.2.src_ref = f32[4,96,128]{2,1,0:T(8,128)S(1)} async-done(((f32[4,96,128]{2,1,0:T(8,128)}), f32[4,96,128]{2,1,0:T(8,128)S(1)}, u32[]{:S(2)}, u32[]{:S(2)}) %all-to-all-start.2) | async-done | bytes 196640 | tf_op jit(solution)/shard_map/all_to_all | solution.py:196
  56.7 9.9 %all-to-all-start.1 = ((bf16[8,96,128]{2,1,0:T(8,128)(2,1)}), bf16[8,96,128]{2,1,0:T(8,128)(2,1)}, u32[]{:S(2)}, u32[]{:S(2)}) async-start(bf16[8,96,128]{2,1,0:T(8,128)(2,1)} %broadcast_in_dim.76), calls=%async_computation.1 | async-start | bytes 393216 | tf_op jit(solution)/shard_map/all_to_all | solution.py:177
  67.4 4.6 collective-permute-start.3
  74.8 7.0 %collective-permute-done.3.two_imag = bf16[96,3072]{1,0:T(8,128)(2,1)S(1)} collective-permute-done((bf16[96,3072]{1,0:T(8,128)(2,1)}, bf16[96,3072]{1,0:T(8,128)(2,1)S(1)}, u32[]{:S(2)}, u32[]{:S(2)}) %collective-permute-start.3) | collective-permute-done | bytes 589856 | tf_op jit(solution)/shard_map/ppermute | solution.py:181
  93.3 3.2 apply_next.19
  98.0 9.9 %all-to-all-start.3 = ((bf16[8,96,128]{2,1,0:T(8,128)(2,1)}), bf16[8,96,128]{2,1,0:T(8,128)(2,1)S(1)}, u32[]{:S(2)}, u32[]{:S(2)}) async-start(bf16[8,96,128]{2,1,0:T(8,128)(2,1)} %broadcast_in_dim.79), calls=%async_computation.3 | async-start | bytes 393216 | tf_op jit(solution)/shard_map/all_to_all | solution.py:177
  108.0 6.1 all-to-all-done.3
  115.8 2.8 apply_next.20
  120.0 9.9 %all-to-all-start.4 = ((bf16[8,96,128]{2,1,0:T(8,128)(2,1)}), bf16[8,96,128]{2,1,0:T(8,128)(2,1)S(1)}, u32[]{:S(2)}, u32[]{:S(2)}) async-start(bf16[8,96,128]{2,1,0:T(8,128)(2,1)} %broadcast_in_dim.80), calls=%async_computation.4 | async-start | bytes 393216 | tf_op jit(solution)/shard_map/all_to_all | solution.py:177
  130.0 6.1 all-to-all-done.4
  137.8 2.8 apply_next.21
  142.0 9.9 %all-to-all-start.5 = ((bf16[8,96,128]{2,1,0:T(8,128)(2,1)}), bf16[8,96,128]{2,1,0:T(8,128)(2,1)S(1)}, u32[]{:S(2)}, u32[]{:S(2)}) async-start(bf16[8,96,128]{2,1,0:T(8,128)(2,1)} %broadcast_in_dim.81), calls=%async_computation.5 | async-start | bytes 393216 | tf_op jit(solution)/shard_map/all_to_all | solution.py:177
  152.0 6.1 all-to-all-done.5
  164.0 9.9 %all-to-all-start.6 = ((bf16[8,96,128]{2,1,0:T(8,128)(2,1)}), bf16[8,96,128]{2,1,0:T(8,128)(2,1)S(1)}, u32[]{:S(2)}, u32[]{:S(2)}) async-start(bf16[8,96,128]{2,1,0:T(8,128)(2,1)} %broadcast_in_dim.82), calls=%async_computation.6 | async-start | bytes 393216 | tf_op jit(solution)/shard_map/all_to_all | solution.py:177
  174.0 6.1 all-to-all-done.6
  181.8 2.8 apply_next.23
  186.0 9.9 %all-to-all-start.7 = ((bf16[8,96,128]{2,1,0:T(8,128)(2,1)}), bf16[8,96,128]{2,1,0:T(8,128)(2,1)S(1)}, u32[]{:S(2)}, u32[]{:S(2)}) async-start(bf16[8,96,128]{2,1,0:T(8,128)(2,1)} %broadcast_in_dim.83), calls=%async_computation.7 | async-start | bytes 393216 | tf_op jit(solution)/shard_map/all_to_all | solution.py:177
  196.0 6.1 all-to-all-done.7
  208.0 9.9 %all-to-all-start.8 = ((bf16[8,96,128]{2,1,0:T(8,128)(2,1)}), bf16[8,96,128]{2,1,0:T(8,128)(2,1)S(1)}, u32[]{:S(2)}, u32[]{:S(2)}) async-start(bf16[8,96,128]{2,1,0:T(8,128)(2,1)} %broadcast_in_dim.84), calls=%async_computation.8 | async-start | bytes 393216 | tf_op jit(solution)/shard_map/all_to_all | solution.py:177
  218.0 6.1 all-to-all-done.8
  225.8 2.8 apply_next.25
  230.0 9.9 %all-to-all-start.9 = ((bf16[8,96,128]{2,1,0:T(8,128)(2,1)}), bf16[8,96,128]{2,1,0:T(8,128)(2,1)S(1)}, u32[]{:S(2)}, u32[]{:S(2)}) async-start(bf16[8,96,128]{2,1,0:T(8,128)(2,1)} %broadcast_in_dim.85), calls=%async_computation.9 | async-start | bytes 393216 | tf_op jit(solution)/shard_map/all_to_all | solution.py:177
  240.0 6.1 all-to-all-done.9
  252.0 9.9 %all-to-all-start.10 = ((bf16[8,96,128]{2,1,0:T(8,128)(2,1)}), bf16[8,96,128]{2,1,0:T(8,128)(2,1)S(1)}, u32[]{:S(2)}, u32[]{:S(2)}) async-start(bf16[8,96,128]{2,1,0:T(8,128)(2,1)} %broadcast_in_dim.86), calls=%async_computation.10 | async-start | bytes 393216 | tf_op jit(solution)/shard_map/all_to_all | solution.py:177
  262.0 6.1 all-to-all-done.10
  269.8 2.8 apply_next.27
  274.0 9.9 %all-to-all-start.11 = ((bf16[8,96,128]{2,1,0:T(8,128)(2,1)}), bf16[8,96,128]{2,1,0:T(8,128)(2,1)S(1)}, u32[]{:S(2)}, u32[]{:S(2)}) async-start(bf16[8,96,128]{2,1,0:T(8,128)(2,1)} %broadcast_in_dim.87), calls=%async_computation.11 | async-start | bytes 393216 | tf_op jit(solution)/shard_map/all_to_all | solution.py:177
  284.0 6.1 all-to-all-done.11
  296.0 9.9 %all-to-all-start.12 = ((bf16[8,96,128]{2,1,0:T(8,128)(2,1)}), bf16[8,96,128]{2,1,0:T(8,128)(2,1)S(1)}, u32[]{:S(2)}, u32[]{:S(2)}) async-start(bf16[8,96,128]{2,1,0:T(8,128)(2,1)} %broadcast_in_dim.88), calls=%async_computation.12 | async-start | bytes 393216 | tf_op jit(solution)/shard_map/all_to_all | solution.py:177
  306.0 10.1 %all-to-all-done.12 = bf16[8,96,128]{2,1,0:T(8,128)(2,1)S(1)} async-done(((bf16[8,96,128]{2,1,0:T(8,128)(2,1)}), bf16[8,96,128]{2,1,0:T(8,128)(2,1)S(1)}, u32[]{:S(2)}, u32[]{:S(2)}) %all-to-all-start.12) | async-done | bytes 196640 | tf_op jit(solution)/shard_map/all_to_all | solution.py:177
  322.0 9.9 %all-to-all-start.13 = ((bf16[8,96,128]{2,1,0:T(8,128)(2,1)}), bf16[8,96,128]{2,1,0:T(8,128)(2,1)S(1)}, u32[]{:S(2)}, u32[]{:S(2)}) async-start(bf16[8,96,128]{2,1,0:T(8,128)(2,1)} %broadcast_in_dim.89), calls=%async_computation.13 | async-start | bytes 393216 | tf_op jit(solution)/shard_map/all_to_all | solution.py:177
  331.9 9.3 %all-to-all-done.13 = bf16[8,96,128]{2,1,0:T(8,128)(2,1)S(1)} async-done(((bf16[8,96,128]{2,1,0:T(8,128)(2,1)}), bf16[8,96,128]{2,1,0:T(8,128)(2,1)S(1)}, u32[]{:S(2)}, u32[]{:S(2)}) %all-to-all-start.13) | async-done | bytes 196640 | tf_op jit(solution)/shard_map/all_to_all | solution.py:177
  347.1 9.9 %all-to-all-start.14 = ((bf16[8,96,128]{2,1,0:T(8,128)(2,1)}), bf16[8,96,128]{2,1,0:T(8,128)(2,1)S(1)}, u32[]{:S(2)}, u32[]{:S(2)}) async-start(bf16[8,96,128]{2,1,0:T(8,128)(2,1)} %broadcast_in_dim.90), calls=%async_computation.14 | async-start | bytes 393216 | tf_op jit(solution)/shard_map/all_to_all | solution.py:177
  357.1 9.2 %all-to-all-done.14 = bf16[8,96,128]{2,1,0:T(8,128)(2,1)S(1)} async-done(((bf16[8,96,128]{2,1,0:T(8,128)(2,1)}), bf16[8,96,128]{2,1,0:T(8,128)(2,1)S(1)}, u32[]{:S(2)}, u32[]{:S(2)}) %all-to-all-start.14) | async-done | bytes 196640 | tf_op jit(solution)/shard_map/all_to_all | solution.py:177
  367.9 2.8 apply_next.31
  372.1 9.9 %all-to-all-start.15 = ((bf16[8,96,128]{2,1,0:T(8,128)(2,1)}), bf16[8,96,128]{2,1,0:T(8,128)(2,1)S(1)}, u32[]{:S(2)}, u32[]{:S(2)}) async-start(bf16[8,96,128]{2,1,0:T(8,128)(2,1)} %broadcast_in_dim.91), calls=%async_computation.15 | async-start | bytes 393216 | tf_op jit(solution)/shard_map/all_to_all | solution.py:177
  382.1 8.7 %all-to-all-done.15 = bf16[8,96,128]{2,1,0:T(8,128)(2,1)S(1)} async-done(((bf16[8,96,128]{2,1,0:T(8,128)(2,1)}), bf16[8,96,128]{2,1,0:T(8,128)(2,1)S(1)}, u32[]{:S(2)}, u32[]{:S(2)}) %all-to-all-start.15) | async-done | bytes 196640 | tf_op jit(solution)/shard_map/all_to_all | solution.py:177
  392.5 2.8 apply_next.32
  396.6 31.7 %collective-permute-done.17 = bf16[96,128]{1,0:T(8,128)(2,1)S(1)} collective-permute-done((bf16[96,128]{1,0:T(8,128)(2,1)S(1)}, bf16[96,128]{1,0:T(8,128)(2,1)S(1)}, u32[]{:S(2)}, u32[]{:S(2)}) %collective-permute-start.17) | collective-permute-done | bytes 24608 | tf_op jit(solution)/shard_map/ppermute | solution.py:213
  429.0 9.9 %all-to-all-start.16 = ((bf16[8,96,128]{2,1,0:T(8,128)(2,1)}), bf16[8,96,128]{2,1,0:T(8,128)(2,1)S(1)}, u32[]{:S(2)}, u32[]{:S(2)}) async-start(bf16[8,96,128]{2,1,0:T(8,128)(2,1)} %broadcast_in_dim.92), calls=%async_computation.16 | async-start | bytes 393216 | tf_op jit(solution)/shard_map/all_to_all | solution.py:177
  439.0 6.1 all-to-all-done.16
  446.8 2.8 apply_next.33
  451.6 14.0 %collective-permute-done.18 = bf16[96,128]{1,0:T(8,128)(2,1)S(1)} collective-permute-done((bf16[96,128]{1,0:T(8,128)(2,1)S(1)}, bf16[96,128]{1,0:T(8,128)(2,1)S(1)}, u32[]{:S(2)}, u32[]{:S(2)}) %collective-permute-start.18) | collective-permute-done | bytes 24608 | tf_op jit(solution)/shard_map/ppermute | solution.py:213
  466.3 9.9 %all-to-all-start.17 = ((bf16[8,96,128]{2,1,0:T(8,128)(2,1)}), bf16[8,96,128]{2,1,0:T(8,128)(2,1)S(1)}, u32[]{:S(2)}, u32[]{:S(2)}) async-start(bf16[8,96,128]{2,1,0:T(8,128)(2,1)} %broadcast_in_dim.93), calls=%async_computation.17 | async-start | bytes 393216 | tf_op jit(solution)/shard_map/all_to_all | solution.py:177
  476.3 6.1 all-to-all-done.17
  484.1 2.8 apply_next.34
  488.9 14.2 %collective-permute-done.19 = bf16[96,128]{1,0:T(8,128)(2,1)S(1)} collective-permute-done((bf16[96,128]{1,0:T(8,128)(2,1)S(1)}, bf16[96,128]{1,0:T(8,128)(2,1)S(1)}, u32[]{:S(2)}, u32[]{:S(2)}) %collective-permute-start.19) | collective-permute-done | bytes 24608 | tf_op jit(solution)/shard_map/ppermute | solution.py:213
  503.8 9.9 %all-to-all-start.18 = ((bf16[8,96,128]{2,1,0:T(8,128)(2,1)}), bf16[8,96,128]{2,1,0:T(8,128)(2,1)S(1)}, u32[]{:S(2)}, u32[]{:S(2)}) async-start(bf16[8,96,128]{2,1,0:T(8,128)(2,1)} %broadcast_in_dim.94), calls=%async_computation.18 | async-start | bytes 393216 | tf_op jit(solution)/shard_map/all_to_all | solution.py:177
  513.8 6.1 all-to-all-done.18
  526.4 23.1 %collective-permute-done.20 = bf16[96,128]{1,0:T(8,128)(2,1)S(1)} collective-permute-done((bf16[96,128]{1,0:T(8,128)(2,1)S(1)}, bf16[96,128]{1,0:T(8,128)(2,1)S(1)}, u32[]{:S(2)}, u32[]{:S(2)}) %collective-permute-start.20) | collective-permute-done | bytes 24608 | tf_op jit(solution)/shard_map/ppermute | solution.py:213
  550.1 9.9 %all-to-all-start.19 = ((bf16[8,96,128]{2,1,0:T(8,128)(2,1)}), bf16[8,96,128]{2,1,0:T(8,128)(2,1)S(1)}, u32[]{:S(2)}, u32[]{:S(2)}) async-start(bf16[8,96,128]{2,1,0:T(8,128)(2,1)} %broadcast_in_dim.95), calls=%async_computation.19 | async-start | bytes 393216 | tf_op jit(solution)/shard_map/all_to_all | solution.py:177
  560.1 6.1 all-to-all-done.19
  573.6 9.9 %all-to-all-start.20 = ((bf16[8,96,128]{2,1,0:T(8,128)(2,1)}), bf16[8,96,128]{2,1,0:T(8,128)(2,1)S(1)}, u32[]{:S(2)}, u32[]{:S(2)}) async-start(bf16[8,96,128]{2,1,0:T(8,128)(2,1)} %broadcast_in_dim.96), calls=%async_computation.20 | async-start | bytes 393216 | tf_op jit(solution)/shard_map/all_to_all | solution.py:177
  584.6 3.4 collective-permute-start.22
  590.9 11.4 %collective-permute-done.22.up_ref = bf16[3,768,128]{2,1,0:T(8,128)(2,1)} collective-permute-done((bf16[3,768,128]{2,1,0:T(8,128)(2,1)S(1)}, bf16[3,768,128]{2,1,0:T(8,128)(2,1)}, u32[]{:S(2)}, u32[]{:S(2)}) %collective-permute-start.22) | collective-permute-done | bytes 589856 | tf_op jit(solution)/shard_map/ppermute | solution.py:181
  606.5 3.4 apply_next.37
  611.8 6.5 %all-to-all-start.21 = ((bf16[4,768,128]{2,1,0:T(8,128)(2,1)}), bf16[4,768,128]{2,1,0:T(8,128)(2,1)S(1)}, u32[]{:S(2)}, u32[]{:S(2)}) async-start(bf16[4,768,128]{2,1,0:T(8,128)(2,1)} %broadcast_in_dim.97), calls=%async_computation.21 | async-start | bytes 1572864 | tf_op jit(solution)/shard_map/all_to_all | solution.py:177
  620.2 3.4 collective-permute-start.24
  631.4 8.1 %all-to-all-start.22 = ((f32[4,96,128]{2,1,0:T(8,128)}), f32[4,96,128]{2,1,0:T(8,128)}, u32[]{:S(2)}, u32[]{:S(2)}) async-start(f32[4,96,128]{2,1,0:T(8,128)} %swap_blocks.5), calls=%async_computation.22 | async-start | bytes 393216 | tf_op jit(solution)/shard_map/all_to_all | solution.py:222
  639.5 6.2 apply_interior.1
  (176 shorter events, 129.9 us)
Async XLA Ops:
  0.6 37.1 %collective-permute-start = (bf16[2,96,3072]{2,1,0:T(8,128)(2,1)}, bf16[2,96,3072]{2,1,0:T(8,128)(2,1)S(1)}, u32[]{:S(2)}, u32[]{:S(2)}) collective-permute-start(bf16[2,96,3072]{2,1,0:T(8,128)(2,1)} %bitcast.78), channel_id=1, source_target_pairs={{0,8},{8,16},{16,24},{24,0},{1,9},{9,17},{17,25},{25,1},{2,10},{10... | collective-permute-start | bytes 3538952 | tf_op jit(solution)/shard_map/ppermute | solution.py:181
  4.1 33.6 %collective-permute-start.1 = (bf16[2,96,3072]{2,1,0:T(8,128)(2,1)}, bf16[2,96,3072]{2,1,0:T(8,128)(2,1)S(1)}, u32[]{:S(2)}, u32[]{:S(2)}) collective-permute-start(bf16[2,96,3072]{2,1,0:T(8,128)(2,1)} %bitcast.79), channel_id=1, source_target_pairs={{0,24},{8,0},{16,8},{24,16},{1,25},{9,1},{17,9},{25,17},{2,26},{10... | collective-permute-start | bytes 3538952 | tf_op jit(solution)/shard_map/ppermute | solution.py:181
  8.1 27.4 %all-to-all-start = ((bf16[4,96,128]{2,1,0:T(8,128)(2,1)}), bf16[4,96,128]{2,1,0:T(8,128)(2,1)S(1)}, u32[]{:S(2)}, u32[]{:S(2)}) async-start(bf16[4,96,128]{2,1,0:T(8,128)(2,1)} %convert_element_type.3), calls=%async_computation | async-start | bytes 196608 | tf_op jit(solution)/shard_map/all_to_all | solution.py:191
  37.8 29.7 %copy-start.21 = (bf16[2,96,3072]{2,1,0:T(8,128)(2,1)}, bf16[2,96,3072]{2,1,0:T(8,128)(2,1)S(1)}, u32[]{:S(2)}) copy-start(bf16[2,96,3072]{2,1,0:T(8,128)(2,1)S(1)} %collective-permute-done.1.down) | copy-start | bytes 3538948
  38.7 35.3 %collective-permute-start.2 = (bf16[96,3072]{1,0:T(8,128)(2,1)}, bf16[96,3072]{1,0:T(8,128)(2,1)S(1)}, u32[]{:S(2)}, u32[]{:S(2)}) collective-permute-start(bf16[96,3072]{1,0:T(8,128)(2,1)} %slice_bitcast_fusion.1), channel_id=1, source_target_pairs={{0,8},{8,16},{16,24},{24,0},{1,9},{9,17},{17,25},{25,1},{2,10},{10... | collective-permute-start | bytes 1769480 | tf_op jit(solution)/shard_map/ppermute | solution.py:181
  40.9 15.1 %all-to-all-start.2 = ((f32[4,96,128]{2,1,0:T(8,128)}), f32[4,96,128]{2,1,0:T(8,128)S(1)}, u32[]{:S(2)}, u32[]{:S(2)}) async-start(f32[4,96,128]{2,1,0:T(8,128)} %bitcast.46), calls=%async_computation.2 | async-start | bytes 393216 | tf_op jit(solution)/shard_map/all_to_all | solution.py:196
  55.9 10.6 %copy-start.29 = (f32[4,96,128]{2,1,0:T(8,128)}, f32[4,96,128]{2,1,0:T(8,128)S(1)}, u32[]{:S(2)}) copy-start(f32[4,96,128]{2,1,0:T(8,128)S(1)} %all-to-all-done.2.src_ref) | copy-start | bytes 589828
  56.7 33.1 %all-to-all-start.1 = ((bf16[8,96,128]{2,1,0:T(8,128)(2,1)}), bf16[8,96,128]{2,1,0:T(8,128)(2,1)}, u32[]{:S(2)}, u32[]{:S(2)}) async-start(bf16[8,96,128]{2,1,0:T(8,128)(2,1)} %broadcast_in_dim.76), calls=%async_computation.1 | async-start | bytes 393216 | tf_op jit(solution)/shard_map/all_to_all | solution.py:177
  67.4 14.4 %collective-permute-start.3 = (bf16[96,3072]{1,0:T(8,128)(2,1)}, bf16[96,3072]{1,0:T(8,128)(2,1)S(1)}, u32[]{:S(2)}, u32[]{:S(2)}) collective-permute-start(bf16[96,3072]{1,0:T(8,128)(2,1)} %slice_bitcast_fusion), channel_id=1, source_target_pairs={{0,24},{8,0},{16,8},{24,16},{1,25},{9,1},{17,9},{25,17},{2,26},{10... | collective-permute-start | bytes 1769480 | tf_op jit(solution)/shard_map/ppermute | solution.py:181
  89.8 1.9 copy-start.20
  91.7 1.7 copy-start.1
  93.3 3.9 copy-start.30
  96.6 0.7 collective-permute-start.4
  98.0 16.1 %all-to-all-start.3 = ((bf16[8,96,128]{2,1,0:T(8,128)(2,1)}), bf16[8,96,128]{2,1,0:T(8,128)(2,1)S(1)}, u32[]{:S(2)}, u32[]{:S(2)}) async-start(bf16[8,96,128]{2,1,0:T(8,128)(2,1)} %broadcast_in_dim.79), calls=%async_computation.3 | async-start | bytes 393216 | tf_op jit(solution)/shard_map/all_to_all | solution.py:177
  114.1 1.7 copy-start.2
  118.6 0.7 collective-permute-start.5
  120.0 16.1 %all-to-all-start.4 = ((bf16[8,96,128]{2,1,0:T(8,128)(2,1)}), bf16[8,96,128]{2,1,0:T(8,128)(2,1)S(1)}, u32[]{:S(2)}, u32[]{:S(2)}) async-start(bf16[8,96,128]{2,1,0:T(8,128)(2,1)} %broadcast_in_dim.80), calls=%async_computation.4 | async-start | bytes 393216 | tf_op jit(solution)/shard_map/all_to_all | solution.py:177
  140.6 0.7 collective-permute-start.6
  142.0 16.1 %all-to-all-start.5 = ((bf16[8,96,128]{2,1,0:T(8,128)(2,1)}), bf16[8,96,128]{2,1,0:T(8,128)(2,1)S(1)}, u32[]{:S(2)}, u32[]{:S(2)}) async-start(bf16[8,96,128]{2,1,0:T(8,128)(2,1)} %broadcast_in_dim.81), calls=%async_computation.5 | async-start | bytes 393216 | tf_op jit(solution)/shard_map/all_to_all | solution.py:177
  162.6 0.7 collective-permute-start.7
  164.0 16.1 %all-to-all-start.6 = ((bf16[8,96,128]{2,1,0:T(8,128)(2,1)}), bf16[8,96,128]{2,1,0:T(8,128)(2,1)S(1)}, u32[]{:S(2)}, u32[]{:S(2)}) async-start(bf16[8,96,128]{2,1,0:T(8,128)(2,1)} %broadcast_in_dim.82), calls=%async_computation.6 | async-start | bytes 393216 | tf_op jit(solution)/shard_map/all_to_all | solution.py:177
  180.2 1.7 copy-start.5
  184.6 0.7 collective-permute-start.8
  186.0 16.1 %all-to-all-start.7 = ((bf16[8,96,128]{2,1,0:T(8,128)(2,1)}), bf16[8,96,128]{2,1,0:T(8,128)(2,1)S(1)}, u32[]{:S(2)}, u32[]{:S(2)}) async-start(bf16[8,96,128]{2,1,0:T(8,128)(2,1)} %broadcast_in_dim.83), calls=%async_computation.7 | async-start | bytes 393216 | tf_op jit(solution)/shard_map/all_to_all | solution.py:177
  202.2 1.7 copy-start.6
  206.6 0.7 collective-permute-start.9
  208.0 16.1 %all-to-all-start.8 = ((bf16[8,96,128]{2,1,0:T(8,128)(2,1)}), bf16[8,96,128]{2,1,0:T(8,128)(2,1)S(1)}, u32[]{:S(2)}, u32[]{:S(2)}) async-start(bf16[8,96,128]{2,1,0:T(8,128)(2,1)} %broadcast_in_dim.84), calls=%async_computation.8 | async-start | bytes 393216 | tf_op jit(solution)/shard_map/all_to_all | solution.py:177
  224.2 1.7 copy-start.7
  228.6 0.7 collective-permute-start.10
  230.0 16.1 %all-to-all-start.9 = ((bf16[8,96,128]{2,1,0:T(8,128)(2,1)}), bf16[8,96,128]{2,1,0:T(8,128)(2,1)S(1)}, u32[]{:S(2)}, u32[]{:S(2)}) async-start(bf16[8,96,128]{2,1,0:T(8,128)(2,1)} %broadcast_in_dim.85), calls=%async_computation.9 | async-start | bytes 393216 | tf_op jit(solution)/shard_map/all_to_all | solution.py:177
  246.2 1.7 copy-start.8
  250.6 0.7 collective-permute-start.11
  252.0 16.1 %all-to-all-start.10 = ((bf16[8,96,128]{2,1,0:T(8,128)(2,1)}), bf16[8,96,128]{2,1,0:T(8,128)(2,1)S(1)}, u32[]{:S(2)}, u32[]{:S(2)}) async-start(bf16[8,96,128]{2,1,0:T(8,128)(2,1)} %broadcast_in_dim.86), calls=%async_computation.10 | async-start | bytes 393216 | tf_op jit(solution)/shard_map/all_to_all | solution.py:177
  268.2 1.7 copy-start.9
  272.6 0.7 collective-permute-start.12
  274.0 16.1 %all-to-all-start.11 = ((bf16[8,96,128]{2,1,0:T(8,128)(2,1)}), bf16[8,96,128]{2,1,0:T(8,128)(2,1)S(1)}, u32[]{:S(2)}, u32[]{:S(2)}) async-start(bf16[8,96,128]{2,1,0:T(8,128)(2,1)} %broadcast_in_dim.87), calls=%async_computation.11 | async-start | bytes 393216 | tf_op jit(solution)/shard_map/all_to_all | solution.py:177
  290.2 1.7 copy-start.10
  294.6 0.7 collective-permute-start.13
  296.0 20.1 %all-to-all-start.12 = ((bf16[8,96,128]{2,1,0:T(8,128)(2,1)}), bf16[8,96,128]{2,1,0:T(8,128)(2,1)S(1)}, u32[]{:S(2)}, u32[]{:S(2)}) async-start(bf16[8,96,128]{2,1,0:T(8,128)(2,1)} %broadcast_in_dim.88), calls=%async_computation.12 | async-start | bytes 393216 | tf_op jit(solution)/shard_map/all_to_all | solution.py:177
  320.6 0.7 collective-permute-start.14
  322.0 19.2 %all-to-all-start.13 = ((bf16[8,96,128]{2,1,0:T(8,128)(2,1)}), bf16[8,96,128]{2,1,0:T(8,128)(2,1)S(1)}, u32[]{:S(2)}, u32[]{:S(2)}) async-start(bf16[8,96,128]{2,1,0:T(8,128)(2,1)} %broadcast_in_dim.89), calls=%async_computation.13 | async-start | bytes 393216 | tf_op jit(solution)/shard_map/all_to_all | solution.py:177
  345.7 0.7 collective-permute-start.15
  347.1 19.2 %all-to-all-start.14 = ((bf16[8,96,128]{2,1,0:T(8,128)(2,1)}), bf16[8,96,128]{2,1,0:T(8,128)(2,1)S(1)}, u32[]{:S(2)}, u32[]{:S(2)}) async-start(bf16[8,96,128]{2,1,0:T(8,128)(2,1)} %broadcast_in_dim.90), calls=%async_computation.14 | async-start | bytes 393216 | tf_op jit(solution)/shard_map/all_to_all | solution.py:177
  366.3 1.7 copy-start.13
  370.8 0.7 collective-permute-start.16
  372.1 18.7 %all-to-all-start.15 = ((bf16[8,96,128]{2,1,0:T(8,128)(2,1)}), bf16[8,96,128]{2,1,0:T(8,128)(2,1)S(1)}, u32[]{:S(2)}, u32[]{:S(2)}) async-start(bf16[8,96,128]{2,1,0:T(8,128)(2,1)} %broadcast_in_dim.91), calls=%async_computation.15 | async-start | bytes 393216 | tf_op jit(solution)/shard_map/all_to_all | solution.py:177
  395.3 33.0 %collective-permute-start.17 = (bf16[96,128]{1,0:T(8,128)(2,1)S(1)}, bf16[96,128]{1,0:T(8,128)(2,1)S(1)}, u32[]{:S(2)}, u32[]{:S(2)}) collective-permute-start(bf16[96,128]{1,0:T(8,128)(2,1)S(1)} %get-tuple-element.114), channel_id=1, source_target_pairs={{320,352},{352,384},{384,416},{416,448},{321,353},{353,385},{385,4... | collective-permute-start | bytes 73736 | tf_op jit(solution)/shard_map/ppermute | solution.py:213
  429.0 16.1 %all-to-all-start.16 = ((bf16[8,96,128]{2,1,0:T(8,128)(2,1)}), bf16[8,96,128]{2,1,0:T(8,128)(2,1)S(1)}, u32[]{:S(2)}, u32[]{:S(2)}) async-start(bf16[8,96,128]{2,1,0:T(8,128)(2,1)} %broadcast_in_dim.92), calls=%async_computation.16 | async-start | bytes 393216 | tf_op jit(solution)/shard_map/all_to_all | solution.py:177
  449.6 16.0 %collective-permute-start.18 = (bf16[96,128]{1,0:T(8,128)(2,1)S(1)}, bf16[96,128]{1,0:T(8,128)(2,1)S(1)}, u32[]{:S(2)}, u32[]{:S(2)}) collective-permute-start(bf16[96,128]{1,0:T(8,128)(2,1)S(1)} %get-tuple-element.117), channel_id=1, source_target_pairs={{352,384},{384,416},{416,448},{448,480},{353,385},{385,417},{417,4... | collective-permute-start | bytes 73736 | tf_op jit(solution)/shard_map/ppermute | solution.py:213
  466.3 16.1 %all-to-all-start.17 = ((bf16[8,96,128]{2,1,0:T(8,128)(2,1)}), bf16[8,96,128]{2,1,0:T(8,128)(2,1)S(1)}, u32[]{:S(2)}, u32[]{:S(2)}) async-start(bf16[8,96,128]{2,1,0:T(8,128)(2,1)} %broadcast_in_dim.93), calls=%async_computation.17 | async-start | bytes 393216 | tf_op jit(solution)/shard_map/all_to_all | solution.py:177
  486.9 16.2 %collective-permute-start.19 = (bf16[96,128]{1,0:T(8,128)(2,1)S(1)}, bf16[96,128]{1,0:T(8,128)(2,1)S(1)}, u32[]{:S(2)}, u32[]{:S(2)}) collective-permute-start(bf16[96,128]{1,0:T(8,128)(2,1)S(1)} %get-tuple-element.120), channel_id=1, source_target_pairs={{384,416},{416,448},{448,480},{385,417},{417,449},{449,481},{386,4... | collective-permute-start | bytes 73736 | tf_op jit(solution)/shard_map/ppermute | solution.py:213
  503.8 16.1 %all-to-all-start.18 = ((bf16[8,96,128]{2,1,0:T(8,128)(2,1)}), bf16[8,96,128]{2,1,0:T(8,128)(2,1)S(1)}, u32[]{:S(2)}, u32[]{:S(2)}) async-start(bf16[8,96,128]{2,1,0:T(8,128)(2,1)} %broadcast_in_dim.94), calls=%async_computation.18 | async-start | bytes 393216 | tf_op jit(solution)/shard_map/all_to_all | solution.py:177
  524.4 25.0 %collective-permute-start.20 = (bf16[96,128]{1,0:T(8,128)(2,1)S(1)}, bf16[96,128]{1,0:T(8,128)(2,1)S(1)}, u32[]{:S(2)}, u32[]{:S(2)}) collective-permute-start(bf16[96,128]{1,0:T(8,128)(2,1)S(1)} %get-tuple-element.123), channel_id=1, source_target_pairs={{416,448},{448,480},{417,449},{449,481},{418,450},{450,482},{419,4... | collective-permute-start | bytes 73736 | tf_op jit(solution)/shard_map/ppermute | solution.py:213
  550.1 16.1 %all-to-all-start.19 = ((bf16[8,96,128]{2,1,0:T(8,128)(2,1)}), bf16[8,96,128]{2,1,0:T(8,128)(2,1)S(1)}, u32[]{:S(2)}, u32[]{:S(2)}) async-start(bf16[8,96,128]{2,1,0:T(8,128)(2,1)} %broadcast_in_dim.95), calls=%async_computation.19 | async-start | bytes 393216 | tf_op jit(solution)/shard_map/all_to_all | solution.py:177
  570.7 2.1 collective-permute-start.21
  573.6 31.2 %all-to-all-start.20 = ((bf16[8,96,128]{2,1,0:T(8,128)(2,1)}), bf16[8,96,128]{2,1,0:T(8,128)(2,1)S(1)}, u32[]{:S(2)}, u32[]{:S(2)}) async-start(bf16[8,96,128]{2,1,0:T(8,128)(2,1)} %broadcast_in_dim.96), calls=%async_computation.20 | async-start | bytes 393216 | tf_op jit(solution)/shard_map/all_to_all | solution.py:177
  584.6 17.7 %collective-permute-start.22 = (bf16[3,768,128]{2,1,0:T(8,128)(2,1)S(1)}, bf16[3,768,128]{2,1,0:T(8,128)(2,1)}, u32[]{:S(2)}, u32[]{:S(2)}) collective-permute-start(bf16[3,768,128]{2,1,0:T(8,128)(2,1)S(1)} %slice.39.own_ref), channel_id=1, source_target_pairs={{0,8},{8,16},{16,24},{24,0},{1,9},{9,17},{17,25},{25,1},{2,10},{10... | collective-permute-start | bytes 1769480 | tf_op jit(solution)/shard_map/ppermute | solution.py:181
  588.0 16.8 %collective-permute-start.23 = (bf16[3,768,128]{2,1,0:T(8,128)(2,1)S(1)}, bf16[3,768,128]{2,1,0:T(8,128)(2,1)}, u32[]{:S(2)}, u32[]{:S(2)}) collective-permute-start(bf16[3,768,128]{2,1,0:T(8,128)(2,1)S(1)} %slice.39.own_ref), channel_id=1, source_target_pairs={{0,24},{8,0},{16,8},{24,16},{1,25},{9,1},{17,9},{25,17},{2,26},{10... | collective-permute-start | bytes 1769480 | tf_op jit(solution)/shard_map/ppermute | solution.py:181
  604.8 1.7 copy-start.19
  611.8 16.2 %all-to-all-start.21 = ((bf16[4,768,128]{2,1,0:T(8,128)(2,1)}), bf16[4,768,128]{2,1,0:T(8,128)(2,1)S(1)}, u32[]{:S(2)}, u32[]{:S(2)}) async-start(bf16[4,768,128]{2,1,0:T(8,128)(2,1)} %broadcast_in_dim.97), calls=%async_computation.21 | async-start | bytes 1572864 | tf_op jit(solution)/shard_map/all_to_all | solution.py:177
  618.4 21.2 %copy-start.23 = (bf16[1,2,144,3072]{3,2,1,0:T(8,128)(2,1)S(1)}, bf16[1,2,144,3072]{3,2,1,0:T(8,128)(2,1)}, u32[]{:S(2)}) copy-start(bf16[1,2,144,3072]{3,2,1,0:T(8,128)(2,1)} %param.5) | copy-start | bytes 5308420
  620.2 19.3 %collective-permute-start.24 = (bf16[3,384,128]{2,1,0:T(8,128)(2,1)}, bf16[3,384,128]{2,1,0:T(8,128)(2,1)S(1)}, u32[]{:S(2)}, u32[]{:S(2)}) collective-permute-start(bf16[3,384,128]{2,1,0:T(8,128)(2,1)} %slice.40), channel_id=1, source_target_pairs={{0,8},{8,16},{16,24},{24,0},{1,9},{9,17},{17,25},{25,1},{2,10},{10... | collective-permute-start | bytes 884744 | tf_op jit(solution)/shard_map/ppermute | solution.py:181
  625.3 14.3 %collective-permute-start.25 = (bf16[3,384,128]{2,1,0:T(8,128)(2,1)}, bf16[3,384,128]{2,1,0:T(8,128)(2,1)}, u32[]{:S(2)}, u32[]{:S(2)}) collective-permute-start(bf16[3,384,128]{2,1,0:T(8,128)(2,1)} %slice.41), channel_id=1, source_target_pairs={{0,24},{8,0},{16,8},{24,16},{1,25},{9,1},{17,9},{25,17},{2,26},{10... | collective-permute-start | bytes 884744 | tf_op jit(solution)/shard_map/ppermute | solution.py:181
  631.4 14.3 %all-to-all-start.22 = ((f32[4,96,128]{2,1,0:T(8,128)}), f32[4,96,128]{2,1,0:T(8,128)}, u32[]{:S(2)}, u32[]{:S(2)}) async-start(f32[4,96,128]{2,1,0:T(8,128)} %swap_blocks.5), calls=%async_computation.22 | async-start | bytes 393216 | tf_op jit(solution)/shard_map/all_to_all | solution.py:222
  (17 other events, 23.3 us)
